TPU v7x, 128 devices: a whole 4x4x4 slice. The times are simulated.
128 devices in a mesh: row: 8 (over z_lo, y), col: 16 (over x, z_hi, core).
Axes of the slice: x: 4, y: 4, z: 4 (z_hi: 2, z_lo: 2; z = z_hi * 2 + z_lo), core: 2. Of those that a mesh axis runs over, the one named last changes fastest.
Arguments:
- moisture: float32 [4, 524288], P(None, ('row', 'col')), may hold values from 0.05 to 0.4
- conduct: float32 [4, 524288], P(None, ('row', 'col')), may hold values from 0.01 to 0.1
- rainfall: float32 [524288], P(('row', 'col')), may hold values from 0.2 to 1.5
- weights: float32 [100, 524288], P(None, ('row', 'col')), may hold values from 0.2 to 5
- land_tile: int32 [524288], P(('row', 'col')), may hold values from 0 to 127, as said below
- head: float32 [5120, 10240], P('row', 'col'), may hold values from 0 to 0.5
- rate: float32 [5120, 10240], P('row', 'col'), may hold values from 0.2 to 5
- flow_code: int32 [5120, 10240], P('row', 'col'), may hold values from 0 to 7
- lake_slot: int32 [5120, 10240], P('row', 'col'), may hold values from 0 to 64, as said below
- lake_table: int32 [8192], P(('row', 'col')), may hold values from 0 to 8191, as said below
- lake_phase: float32 [8192], P(('row', 'col')), may hold values from 0.5 to 2
- lake_area: float32 [8192], P(('row', 'col')), may hold values from 100 to 1000
- lake_crest: float32 [8192], P(('row', 'col')), may hold values from 0.5 to 3
Outputs:
- new_moisture: float32 [4, 524288], P(None, ('row', 'col'))
- surface: float32 [5120, 10240], P('row', 'col')
- level: float32 [8192], P(('row', 'col'))
- outflow: float32 [8192], P(('row', 'col'))
Inputs may be any that keep to these rules, and one draw needn't show every extreme that they name: `land_tile`: the 4096 blocks of one device form aligned runs of 32 blocks; each run goes whole to one tile, different runs of a device to different tiles, and every tile receives each block position exactly once. `lake_slot`: the value 64 marks cells outside lakes; the cells of one slot lie within one rectangle of the tile. `lake_table`: lake k is owned by device k // 64 of the joined axis; a slot may name a lake of any owner.
All inputs are finite; a program needn't handle non-finite values.
Results may differ from a plain program's by a relative error of at most 0.00019.
Values sent between devices are 32-bit elements; how exact they have to be, the bound alone decides.
No kernel may reach another device: no remote copies, remote signals or barrier semaphores. Data moves between devices by JAX's collectives and lax.ppermute only.
A program may use at most 192 MiB of HBM per device.

v0:
```python
import jax
import jax.numpy as jnp
import numpy as np
from jax import lax
from jax.experimental import pallas as pl
from jax.experimental.pallas import tpu as pltpu
from jax.sharding import PartitionSpec as P

AGG = 10
LLOC = 64
LANES = 128
RUNS = 128
RUN_ROWS = 26
SLABS = 6
ROWS = 672
FIRST = 16

LAYER_DEPTHS = (0.1, 0.3, 0.6, 1.0)
POROSITY = 0.45
TIME_STEP = 0.05
F32 = jnp.float32
BF16 = jnp.bfloat16
VMEM = pl.BlockSpec(memory_space=pltpu.VMEM)
SMEM = pl.BlockSpec(memory_space=pltpu.SMEM)


def params(mebibytes):
    return pltpu.CompilerParams(vmem_limit_bytes=mebibytes * 1024 * 1024)


def lanes_of(shape):
    return lax.broadcasted_iota(jnp.int32, shape, len(shape) - 1)


def rows_of(shape):
    return lax.broadcasted_iota(jnp.int32, shape, 0)


def split3(value):
    high = value.astype(BF16)
    rest = value - high.astype(F32)
    middle = rest.astype(BF16)
    low = (rest - middle.astype(F32)).astype(BF16)
    return high, middle, low


def select_dot(picks, value):
    return sum(jnp.dot(picks, part, preferred_element_type=F32) for part in split3(value))


def dot_select(value, picks):
    return sum(jnp.dot(part, picks, preferred_element_type=F32) for part in split3(value))


def quarter_transpose(arrays, quarter):
    rolled = []
    for d in range(4):
        skew = arrays[(3 + d) % 4]
        for m in range(3):
            skew = jnp.where(quarter == m, arrays[(m + d) % 4], skew)
        rolled.append(pltpu.roll(skew, 32 * d, 1) if d else skew)
    outs = []
    for r in range(4):
        out = rolled[(3 - r) % 4]
        for m in range(3):
            out = jnp.where(quarter == m, rolled[(m - r) % 4], out)
        outs.append(out)
    return outs


def send_kernel(tile_ref, moisture_ref, conduct_ref, rain_ref, weights_ref, out_ref, slab_ref, edge_ref, sems):
    count = slab_ref.shape[0]

    def fetch(i):
        start = pl.multiple_of(i * LANES, LANES)
        return pltpu.make_async_copy(weights_ref.at[:, pl.ds(start, LANES)], slab_ref.at[i], sems.at[i])

    def begin(i, carry):
        fetch(i).start()
        return carry

    lax.fori_loop(0, count, begin, 0)
    lane = lanes_of((1, LANES))
    quarter = lane >> 5

    def step(i, carry):
        edges, tiles = carry
        start = pl.multiple_of(i * LANES, LANES)
        conduct = conduct_ref[0:1, pl.ds(start, LANES)]
        moisture = moisture_ref[0:1, pl.ds(start, LANES)]
        rain = rain_ref[0:1, pl.ds(start, LANES)]
        capacity = 10.0 * conduct * (1.5 - moisture / POROSITY)
        runoff = rain - rain * capacity / (rain + capacity)
        fetch(i).wait()
        parts = [slab_ref[i, pl.ds(b, AGG, stride=AGG), :] for b in range(AGG)]
        total = sum(parts[1:], parts[0])
        mean = jnp.sum(total, axis=0, keepdims=True) * 0.01
        scale = runoff / mean
        parts = [part * scale for part in parts]
        tail = [slab_ref[i, pl.ds(first, 5, stride=AGG), :] * scale for first in (8, 9, 58, 59)]
        groups = (
            (0, AGG, quarter_transpose(parts[0:4], quarter)),
            (AGG, AGG, quarter_transpose(parts[4:8], quarter)),
            (2 * AGG, 5, quarter_transpose(tail, quarter)),
        )
        for r in range(4):
            tile = tile_ref[(4 * i + r) * 32]
            tiles = jnp.where(lane == 32 * r + i, tile, tiles)
            for offset, length, outs in groups:
                out_ref[pl.ds(tile * RUN_ROWS + offset, length), :] = outs[r]
        place = lane & 63
        new_edges = []
        for b in range(2):
            left = pltpu.roll(parts[b], i, 1)
            right = pltpu.roll(parts[8 + b], i + 97, 1)
            edge = jnp.where(place == i, left, edges[b])
            new_edges.append(jnp.where(place == i + 32, right, edge))
        return tuple(new_edges), tiles

    zeros = jnp.zeros((AGG, LANES), F32)
    edges, tiles = lax.fori_loop(0, count, step, ((zeros, zeros), jnp.zeros((1, LANES), jnp.int32)))
    edge_ref[...] = jnp.zeros((LANES, LANES), F32)
    edge_ref[0:AGG, :] = edges[0]
    edge_ref[16 : 16 + AGG, :] = edges[1]
    edge_ref[15:16, :] = (4 * (lane & 31) + (lane >> 5)).astype(F32)
    by_run = edge_ref[...].T
    square = (LANES, LANES)
    here = (rows_of(square) == tiles).astype(F32).astype(BF16)
    by_tile = select_dot(here, by_run)
    run = by_tile[:, 15:16].astype(jnp.int32)
    wide = lanes_of(square)
    cell = wide & 15
    odd = (run & 1) == 1
    no_edge = jnp.where(wide == 15, -1.0, 0.0)
    low = cell < 2
    high = (cell == 8) | (cell == 9)

    def moved(picked, down, across):
        value = pltpu.roll(picked, down % LANES, 0)
        return pltpu.roll(value, across, 1) if across else value

    def corner(number, cells):
        return jnp.where((run == number) & cells, by_tile, 0.0)

    row = moved(jnp.where(odd, by_tile, no_edge), 1, 0)
    row = row + moved(jnp.where(odd, no_edge, by_tile), -1, 32)
    row = row + moved(corner(127, high), 17, 64) + moved(corner(1, low), -15, 64)
    row = row + moved(corner(126, high), 15, 96) + moved(corner(0, low), -17, 96)
    row = row + jnp.where(wide == 127, run.astype(F32), 0.0)
    out_ref[pl.ds(25, RUNS, stride=RUN_ROWS), :] = row


def land_payload(land_tile, moisture, conduct, rainfall, weights):
    blocks = weights.shape[1]
    count = blocks // LANES
    return pl.pallas_call(
        send_kernel,
        out_shape=jax.ShapeDtypeStruct((RUNS * RUN_ROWS, LANES), F32),
        in_specs=[SMEM, VMEM, VMEM, VMEM, pl.BlockSpec(memory_space=pl.ANY)],
        out_specs=VMEM,
        scratch_shapes=[
            pltpu.VMEM((count, AGG * AGG, LANES), F32),
            pltpu.VMEM((LANES, LANES), F32),
            pltpu.SemaphoreType.DMA((count,)),
        ],
        compiler_params=params(12),
        name="land",
    )(land_tile, moisture, conduct, rainfall.reshape(1, blocks), weights)


def spread_columns():
    picks = np.zeros((SLABS * LANES, 640), np.float32)
    for half in range(2):
        for j in range(3):
            for k in range(4 if j < 2 else 2):
                for i in range(32):
                    picks[(half * 3 + j) * LANES + 32 * k + i, (half * 32 + i) * AGG + 4 * j + k] = 1.0
    return picks


def place_kernel(pay_ref, head_ref, side_ref, picks_ref, depth_ref, top_ref, bottom_ref, cells_ref, tag_ref, tags, sem):
    arrived = pay_ref[pl.ds(25, RUNS, stride=RUN_ROWS), :]
    by_lane = arrived.T
    tag_ref[...] = jnp.broadcast_to(by_lane[127:128, :].astype(jnp.int32), (8, LANES))
    copy = pltpu.make_async_copy(tag_ref, tags, sem)
    copy.start()
    copy.wait()

    def settle(s, carry):
        run = tags[0, s]
        slab = (run & 1) * 3
        row = (run >> 1) * AGG
        start = s * RUN_ROWS
        cells_ref[slab, pl.ds(row, AGG), :] = pay_ref[pl.ds(start, AGG), :]
        cells_ref[slab + 1, pl.ds(row, AGG), :] = pay_ref[pl.ds(start + AGG, AGG), :]
        last = pay_ref[pl.ds(start + 2 * AGG, 5), :]
        cells_ref[slab + 2, pl.ds(row, 5), :] = last
        cells_ref[slab + 2, pl.ds(row + 5, 5), :] = pltpu.roll(last, 64, 1)
        return carry

    lax.fori_loop(0, RUNS, settle, 0, unroll=4)
    picks = picks_ref[...]
    chunk = 160
    for m in range(0, 640, chunk):
        cells = jnp.concatenate([cells_ref[c, m : m + chunk, :] for c in range(SLABS)], axis=1)
        laid = dot_select(cells, picks)
        for c in range(SLABS - 1):
            columns = slice(c * LANES, (c + 1) * LANES)
            depth = laid[:, columns] + head_ref[m : m + chunk, columns]
            depth_ref[c, FIRST + m : FIRST + m + chunk, :] = depth
            if m == 0:
                top_ref[:, columns] = depth[0:8]
            if m == 640 - chunk:
                bottom_ref[:, columns] = depth[chunk - 8 :]

    tall = (640, LANES)
    row = rows_of(tall)
    block = (row * 6554) >> 16
    lane = lanes_of(tall)
    left = (by_lane[15:16, :].astype(jnp.int32) == 2 * block + 1).astype(F32).astype(BF16)
    right = (by_lane[47:48, :].astype(jnp.int32) == 2 * block).astype(F32).astype(BF16)
    square = (LANES, LANES)
    wide = lanes_of(square)
    strips = select_dot(left, jnp.where(wide < 32, arrived, 0.0))
    strips = strips + select_dot(right, jnp.where((wide >= 32) & (wide < 64), arrived, 0.0))
    strips = jnp.where((lane & 15) == row - AGG * block, strips, 0.0)
    corners = jnp.sum(arrived, axis=0, keepdims=True)
    flat = (8, LANES)
    cell = lanes_of(flat) & 15
    late = lanes_of(flat) >= 64
    above = jnp.where(late & (cell == rows_of(flat) + 2), corners, 0.0)
    below = jnp.where(late & (cell == rows_of(flat)), corners, 0.0)
    source = rows_of(square)
    group = source >> 4
    target = jnp.where((group & 2) == 0, 126, 0) + (group & 1)
    fold = (((source & 15) < AGG) & (target == wide)).astype(F32).astype(BF16)
    depth_ref[SLABS - 1, 8:FIRST, :] = dot_select(above, fold) + side_ref[0:8, :]
    depth_ref[SLABS - 1, FIRST : FIRST + 640, :] = dot_select(strips, fold) + side_ref[8:648, :]
    depth_ref[SLABS - 1, FIRST + 640 : FIRST + 648, :] = dot_select(below, fold) + side_ref[648:656, :]


def place(payload, head, side):
    picks = jnp.asarray(spread_columns(), BF16)
    strip = jax.ShapeDtypeStruct((8, 640), F32)
    return pl.pallas_call(
        place_kernel,
        out_shape=(jax.ShapeDtypeStruct((SLABS, ROWS, LANES), F32), strip, strip),
        in_specs=[VMEM] * 4,
        out_specs=(VMEM,) * 3,
        scratch_shapes=[
            pltpu.VMEM((SLABS, 640, LANES), F32),
            pltpu.VMEM((8, LANES), jnp.int32),
            pltpu.SMEM((8, LANES), jnp.int32),
            pltpu.SemaphoreType.DMA(()),
        ],
        compiler_params=params(24),
        name="place",
    )(payload, head, side, picks)


def rim_kernel(rate_ref, code_ref, slot_ref, head_ref, top_ref, bottom_ref, cols_ref):
    def four(rows, columns):
        code = code_ref[rows, columns].astype(F32)
        lake = (slot_ref[rows, columns] < LLOC).astype(F32)
        return rate_ref[rows, columns], code, lake, head_ref[rows, columns]

    for n, (first, last) in enumerate(zip(four(slice(0, 8), slice(None)), four(slice(632, 640), slice(None)))):
        top_ref[2 * n : 2 * n + 2, :] = first[0:2]
        bottom_ref[2 * n : 2 * n + 2, :] = last[6:8]
    lane = lanes_of((640, LANES))
    gathered = jnp.zeros((640, LANES), F32)
    for n, first in enumerate(four(slice(None), slice(0, LANES))):
        value = pltpu.roll(first, 2 * n, 1) if n else first
        gathered = jnp.where((lane >> 1) == n, value, gathered)
    for n, last in enumerate(four(slice(None), slice(640 - LANES, 640))):
        value = pltpu.roll(last, 2 * n + 10, 1)
        gathered = jnp.where((lane >> 1) == n + 4, value, gathered)
    cols_ref[...] = gathered.T[0:16, :]


def static_kernel(edge_ref, rate_ref, code_ref, slot_ref, up_ref, down_ref, left_ref, right_ref, rates_ref, codes_ref, side_ref, ranges_ref, turn_ref, bits_ref):
    def signed(rate, lake):
        return jnp.where(lake, -rate, rate)

    def center(g, carry):
        rows = pl.ds(pl.multiple_of(g * 8, 8), 8)
        into = pl.ds(pl.multiple_of(g * 8 + FIRST, 8), 8)
        low = jnp.zeros((8, LANES), jnp.int32)
        high = jnp.zeros((8, LANES), jnp.int32)
        for c in range(SLABS - 1):
            columns = slice(c * LANES, (c + 1) * LANES)
            slot = slot_ref[rows, columns]
            rates_ref[c, into, :] = signed(rate_ref[rows, columns], slot < LLOC)
            codes_ref[c, into, :] = code_ref[rows, columns]
            bit = jnp.left_shift(1, slot & 31)
            low = low | jnp.where(slot < 32, bit, 0)
            high = high | jnp.where((slot >= 32) & (slot < LLOC), bit, 0)
        for shift in (4, 2, 1):
            low = low | pltpu.roll(low, shift, 0)
            high = high | pltpu.roll(high, shift, 0)
        bits_ref[0, pl.ds(g, 1), :] = low[0:1]
        bits_ref[1, pl.ds(g, 1), :] = high[0:1]
        return carry

    lax.fori_loop(0, 80, center, 0)
    low, high = bits_ref[0], bits_ref[1]
    for shift in (64, 32, 16, 8, 4, 2, 1):
        low = low | pltpu.roll(low, shift, 1)
        high = high | pltpu.roll(high, shift, 1)
    shape = (80, LANES)
    lane = lanes_of(shape)
    found = (jnp.right_shift(jnp.where(lane < 32, low, high), lane & 31) & 1) == 1
    group = rows_of(shape)
    ranges_ref[...] = jnp.zeros((8, LANES), jnp.int32)
    ranges_ref[0:1, :] = jnp.min(jnp.where(found, group, 80), axis=0, keepdims=True)
    ranges_ref[1:2, :] = jnp.max(jnp.where(found, group + 1, 0), axis=0, keepdims=True)

    first_row, last_row, first_col, last_col = (edge_ref[n] == 1 for n in range(4))
    eight = (8, LANES)
    for c in range(SLABS - 1):
        columns = slice(c * LANES, (c + 1) * LANES)
        for ref, base, offset, outside in ((up_ref, 8, 6, first_row), (down_ref, FIRST + 640, 0, last_row)):
            four = ref[:, columns]
            rates_ref[c, base : base + 8, :] = jnp.zeros(eight, F32)
            codes_ref[c, base : base + 8, :] = jnp.full(eight, -1, jnp.int32)
            at = slice(base + offset, base + offset + 2)
            rates_ref[c, at, :] = signed(four[0:2], four[4:6] > 0.5)
            codes_ref[c, at, :] = jnp.where(outside, -1, four[2:4].astype(jnp.int32))

    turn_ref[...] = jnp.zeros(turn_ref.shape, F32)
    turn_ref[0:8, :] = right_ref[...]
    turn_ref[8:16, :] = left_ref[...]
    turned = turn_ref[...].T[0:656, :]
    lane = lanes_of((656, LANES))
    row = rows_of((656, LANES))
    rightmost = lane < 2
    leftmost = lane >= 126

    def slab(n):
        right = pltpu.roll(turned, LANES - 2 * n, 1) if n else turned
        left = pltpu.roll(turned, 118 - 2 * n, 1)
        return jnp.where(rightmost, right, jnp.where(leftmost, left, 0.0))

    beyond = ((row < 8) & first_row) | ((row >= 648) & last_row) | (leftmost & first_col) | (rightmost & last_col)
    inside = (rightmost | leftmost) & (row >= 6) & (row < 650) & jnp.logical_not(beyond)
    rates_ref[SLABS - 1, 8:664, :] = signed(slab(0), slab(2) > 0.5)
    codes_ref[SLABS - 1, 8:664, :] = jnp.where(inside, slab(1).astype(jnp.int32), -1)
    side_ref[...] = slab(3)


def ring(axis, step):
    count = lax.axis_size(axis)
    return [(i, (i + step) % count) for i in range(count)]


def statics(rate, flow_code, lake_slot, head):
    strip = jax.ShapeDtypeStruct((8, 640), F32)
    top, bottom, cols = pl.pallas_call(
        rim_kernel,
        out_shape=(strip, strip, jax.ShapeDtypeStruct((16, 640), F32)),
        in_specs=[VMEM] * 4,
        out_specs=(VMEM,) * 3,
        compiler_params=params(16),
        name="rim",
    )(rate, flow_code, lake_slot, head)
    up = lax.ppermute(bottom, "row", ring("row", 1))
    down = lax.ppermute(top, "row", ring("row", -1))

    def corner(strips, columns):
        return strips[:, columns].reshape(4, 2, 2).transpose(0, 2, 1).reshape(8, 2)

    def tall(own, columns):
        pad = jnp.zeros((8, 6), F32)
        rest = jnp.zeros((8, 768 - 650), F32)
        return jnp.concatenate([pad, corner(up, columns), own, corner(down, columns), rest], axis=1)

    left = lax.ppermute(tall(cols[8:16], slice(638, 640)), "col", ring("col", 1))
    right = lax.ppermute(tall(cols[0:8], slice(0, 2)), "col", ring("col", -1))
    at_row, at_col = lax.axis_index("row"), lax.axis_index("col")
    edges = jnp.stack(
        [at_row == 0, at_row == lax.axis_size("row") - 1, at_col == 0, at_col == lax.axis_size("col") - 1]
    ).astype(jnp.int32)
    slabs = (SLABS, ROWS, LANES)
    return pl.pallas_call(
        static_kernel,
        out_shape=(
            jax.ShapeDtypeStruct(slabs, F32),
            jax.ShapeDtypeStruct(slabs, jnp.int32),
            jax.ShapeDtypeStruct((656, LANES), F32),
            jax.ShapeDtypeStruct((8, LANES), jnp.int32),
        ),
        in_specs=[SMEM] + [VMEM] * 7,
        out_specs=(VMEM,) * 4,
        scratch_shapes=[pltpu.VMEM((LANES, 768), F32), pltpu.VMEM((2, 80, LANES), jnp.int32)],
        compiler_params=params(20),
        name="static",
    )(edges, rate, flow_code, lake_slot, up, down, left, right)


def leave(depth, rate):
    conveyance = rate * jnp.exp(jnp.log(depth) * (2.0 / 3.0))
    return depth * conveyance / (1.0 + conveyance)


def route_kernel(
    ranges, depth_ref, up_ref, down_ref, rates_ref, codes_ref, slot_ref, wide_table_ref, tall_table_ref,
    surface_ref, spread_ref, leave_ref, next_ref, stay_ref, lake_ref, sums_ref,
):
    lane = lanes_of((8, LANES))

    def at(g):
        return pl.ds(pl.multiple_of(g * 8, 8), 8)

    def start(c, rows, depth):
        leaving = leave(depth, jnp.abs(rates_ref[c, rows, :]))
        leave_ref[c, rows, :] = leaving
        stay_ref[c, rows, :] = depth - leaving

    for g, ref in ((1, up_ref), (82, down_ref)):
        rows = slice(g * 8, g * 8 + 8)
        for c in range(SLABS - 1):
            start(c, rows, ref[:, c * LANES : (c + 1) * LANES])
        start(SLABS - 1, rows, depth_ref[SLABS - 1, rows, :])

    def first(g, carry):
        rows = at(g)
        for c in range(SLABS):
            start(c, rows, depth_ref[c, rows, :])
        return carry

    lax.fori_loop(2, 82, first, 0)

    def gained(ref, g, slabs):
        east, middle, west = [], [], []
        base = g * 8
        for c in range(SLABS):
            here, above, below = (ref[c, pl.ds(base + d, 8), :] for d in (0, -1, 1))
            code, code_above, code_below = (codes_ref[c, pl.ds(base + d, 8), :] for d in (0, -1, 1))

            def pick(which, number, value):
                return jnp.where(which == number, value, 0.0)

            east.append(pick(code, 0, here) + pick(code_above, 1, above) + pick(code_below, 7, below))
            middle.append(pick(code_above, 2, above) + pick(code_below, 6, below))
            west.append(pick(code, 4, here) + pick(code_above, 3, above) + pick(code_below, 5, below))
        east = [pltpu.roll(value, 1, 1) for value in east]
        west = [pltpu.roll(value, LANES - 1, 1) for value in west]
        return [
            middle[c]
            + jnp.where(lane == 0, east[c - 1], east[c])
            + jnp.where(lane == LANES - 1, west[(c + 1) % SLABS], west[c])
            for c in range(slabs)
        ]

    def second(g, carry):
        rows = at(g)
        for c, gain in enumerate(gained(leave_ref, g, SLABS)):
            rate = rates_ref[c, rows, :]
            lake = rate < 0.0
            depth = stay_ref[c, rows, :] + gain
            kept = jnp.where(lake, 0.0, depth)
            leaving = leave(kept, jnp.abs(rate))
            next_ref[c, rows, :] = leaving
            stay_ref[c, rows, :] = kept - leaving
            if c < SLABS - 1:
                lake_ref[c, rows, :] = depth - kept
        return carry

    lax.fori_loop(1, 83, second, 0)

    def third(g, carry):
        rows = at(g)
        out = at(g - 2)
        for c, gain in enumerate(gained(next_ref, g, SLABS - 1)):
            depth = stay_ref[c, rows, :] + gain
            kept = jnp.where(rates_ref[c, rows, :] < 0.0, 0.0, depth)
            lake_ref[c, rows, :] += depth - kept
            surface_ref[out, c * LANES : (c + 1) * LANES] = kept
        return carry

    lax.fori_loop(2, 82, third, 0)

    def lake(slot, carry):
        def add(g, total):
            rows = at(g)
            from_rows = at(g + 2)
            for c in range(SLABS - 1):
                mine = slot_ref[rows, c * LANES : (c + 1) * LANES] == slot
                total = total + jnp.where(mine, lake_ref[c, from_rows, :], 0.0)
            return total

        total = lax.fori_loop(ranges[0, slot], ranges[1, slot], add, jnp.zeros((8, LANES), F32))
        sums_ref[pl.ds(slot, 1), :] = jnp.sum(total, axis=0, keepdims=True)
        return carry

    lax.fori_loop(0, LLOC, lake, 0)
    totals = jnp.sum(sums_ref[...], axis=1, keepdims=True)
    owner = (wide_table_ref[...] >> 6 == rows_of((LANES, LLOC))).astype(F32).astype(BF16)
    number = (tall_table_ref[...] & 63) == lanes_of((LLOC, LANES))
    spread_ref[...] = select_dot(owner, jnp.where(number, totals, 0.0))


def route(depth, up, down, rates, codes, ranges, lake_slot, lake_table):
    slabs = pltpu.VMEM((SLABS, ROWS, LANES), F32)
    return pl.pallas_call(
        route_kernel,
        out_shape=(jax.ShapeDtypeStruct(lake_slot.shape, F32), jax.ShapeDtypeStruct((LANES, LANES), F32)),
        in_specs=[SMEM] + [VMEM] * 8,
        out_specs=(VMEM,) * 2,
        scratch_shapes=[slabs, slabs, slabs, slabs, pltpu.VMEM((LLOC, LANES), F32)],
        compiler_params=params(28),
        name="route",
    )(ranges, depth, up, down, rates, codes, lake_slot, lake_table.reshape(1, LLOC), lake_table.reshape(LLOC, 1))


def pool_kernel(spread_ref, phase_ref, area_ref, crest_ref, level_ref, outflow_ref):
    inflow = jnp.sum(spread_ref[...], axis=0, keepdims=True)[:, :LLOC]
    area = area_ref[...]
    phase = phase_ref[...] + inflow / area
    excess = jnp.maximum(phase - crest_ref[...], 0.0)
    outflow = excess * jnp.sqrt(excess)
    level_ref[...] = phase - outflow / area
    outflow_ref[...] = outflow


def level_pool(spread, lake_phase, lake_area, lake_crest):
    row = jax.ShapeDtypeStruct((1, LLOC), F32)
    level, outflow = pl.pallas_call(
        pool_kernel,
        out_shape=(row, row),
        in_specs=[VMEM] * 4,
        out_specs=(VMEM,) * 2,
        name="pool",
    )(spread, *(value.reshape(1, LLOC) for value in (lake_phase, lake_area, lake_crest)))
    return level.reshape(LLOC), outflow.reshape(LLOC)


def new_moisture_of(moisture, conduct, rainfall):
    saturation = moisture / POROSITY
    capacity = 10.0 * conduct[0] * (1.5 - saturation[0])
    infiltration = rainfall * capacity / (rainfall + capacity)
    drainage = conduct * saturation**4
    incoming = jnp.concatenate([infiltration[None, :], drainage[:-1]], axis=0)
    thickness = jnp.array(LAYER_DEPTHS, F32)[:, None]
    return moisture + TIME_STEP * (incoming - drainage) / thickness


def body(
    moisture, conduct, rainfall, weights, land_tile, head, rate, flow_code, lake_slot, lake_table,
    lake_phase, lake_area, lake_crest,
):
    both = ("row", "col")
    payload = land_payload(land_tile, moisture, conduct, rainfall, weights)
    payload, rate, flow_code, lake_slot, head, moisture = lax.optimization_barrier(
        (payload, rate, flow_code, lake_slot, head, moisture)
    )
    arrived = lax.all_to_all(
        payload.reshape(RUNS, 1, RUN_ROWS * LANES), both, split_axis=0, concat_axis=0, tiled=True
    ).reshape(RUNS * RUN_ROWS, LANES)
    new_moisture = new_moisture_of(moisture, conduct, rainfall)
    rates, codes, side, ranges = statics(rate, flow_code, lake_slot, head)
    depth, top, bottom = place(arrived, head, side)
    up = lax.ppermute(bottom, "row", ring("row", 1))
    down = lax.ppermute(top, "row", ring("row", -1))
    surface, spread = route(depth, up, down, rates, codes, ranges, lake_slot, lake_table)
    spread = lax.all_to_all(
        spread.reshape(RUNS, 1, LANES), both, split_axis=0, concat_axis=0, tiled=True
    ).reshape(RUNS, LANES)
    level, outflow = level_pool(spread, lake_phase, lake_area, lake_crest)
    return (new_moisture, surface, level, outflow)


def solution(mesh):
    blocks = P(("row", "col"))
    layers = P(None, ("row", "col"))
    cells = P("row", "col")
    in_specs = (layers, layers, blocks, layers, blocks) + (cells,) * 4 + (blocks,) * 4
    out_specs = (layers, cells, blocks, blocks)
    return jax.shard_map(body, mesh=mesh, in_specs=in_specs, out_specs=out_specs, check_vma=False)
```

profile of v0, /device:TPU:1, one launch (start us, length us, event | category | flops | bytes accessed | tf_op | source)
XLA Modules:
  0.0 129.2 jit_solution(6535856133731146230)
XLA Ops:
  0.6 1.4 %copy-done.13 = f32[100,4096]{1,0:T(8,128)S(1)} copy-done((f32[100,4096]{1,0:T(8,128)S(1)}, f32[100,4096]{1,0:T(8,128)}, u32[]{:S(2)}) %copy-start.13) | copy-done | bytes 1638424
  5.2 7.7 %land.1 = f32[3328,128]{1,0:T(8,128)} custom-call(s32[4096]{0:T(1024)S(1)} %copy-done.23, f32[4,4096]{1,0:T(4,128)S(1)} %copy-done.17, f32[4,4096]{1,0:T(4,128)S(1)} %copy-done.15, f32[1,4096]{1,0:T(1,128)S(1)} %bitcast.46, f32[100,4096]{1,0:T(8,128)S(1)} %copy-done.13), custom_call_target="tpu_custom_call" | custom-call | tf_op jit(solution)/shard_map/land/pallas_call | solution.py:156
  13.0 1.4 %copy-done.3 = s32[640,640]{1,0:T(8,128)S(1)} copy-done((s32[640,640]{1,0:T(8,128)S(1)}, s32[640,640]{1,0:T(8,128)}, u32[]{:S(2)}) %copy-start.3) | copy-done | bytes 1638424
  14.4 1.4 %copy-done.5 = f32[640,640]{1,0:T(8,128)S(1)} copy-done((f32[640,640]{1,0:T(8,128)S(1)}, f32[640,640]{1,0:T(8,128)}, u32[]{:S(2)}) %copy-start.5) | copy-done | bytes 1638424
  15.8 1.2 rim.1
  17.0 2.1 %collective-permute-start = (f32[8,640]{1,0:T(8,128)}, f32[8,640]{1,0:T(8,128)S(1)}, u32[]{:S(2)}, u32[]{:S(2)}) collective-permute-start(f32[8,640]{1,0:T(8,128)} %get-tuple-element.29), channel_id=1, source_target_pairs={{0,16},{16,32},{32,48},{48,64},{64,80},{80,96},{96,112},{112,0},{1... | collective-permute-start | bytes 61448 | tf_op jit(solution)/shard_map/ppermute | solution.py:366
  19.1 2.8 %collective-permute-start.1 = (f32[8,640]{1,0:T(8,128)}, f32[8,640]{1,0:T(8,128)S(1)}, u32[]{:S(2)}, u32[]{:S(2)}) collective-permute-start(f32[8,640]{1,0:T(8,128)} %get-tuple-element.30), channel_id=1, source_target_pairs={{0,112},{16,0},{32,16},{48,32},{64,48},{80,64},{96,80},{112,96},{1... | collective-permute-start | bytes 61448 | tf_op jit(solution)/shard_map/ppermute | solution.py:367
  21.9 8.6 %all-to-all-start = ((f32[128,1,3328]{2,1,0:T(1,128)}), f32[128,1,3328]{2,1,0:T(1,128)S(1)}, u32[]{:S(2)}, u32[]{:S(2)}) async-start(f32[128,1,3328]{2,1,0:T(1,128)} %bitcast.23), calls=%async_computation | async-start | bytes 3407872 | tf_op jit(solution)/shard_map/all_to_all | solution.py:557
  33.5 1.4 %concatenate.11 = f32[8,768]{1,0:T(8,128)} concatenate(f32[8,6]{1,0:T(8,128)S(1)} %broadcast.12, f32[8,2]{1,0:T(8,128)S(1)} %bitcast.61, f32[8,640]{1,0:T(8,128)} %get-tuple-element.46, f32[8,2]{1,0:T(8,128)S(1)} %bitcast.63, f32[8,118]{1,0:T(8,128)S(1)} %broadcast.13), dimensions={1} | concatenate | bytes 49152 | tf_op jit(solution)/shard_map/concatenate | solution.py:375
  34.9 1.1 collective-permute-start.3
  37.4 1.4 %concatenate.10 = f32[8,768]{1,0:T(8,128)} concatenate(f32[8,6]{1,0:T(8,128)S(1)} %broadcast.12, f32[8,2]{1,0:T(8,128)S(1)} %bitcast.62, f32[8,640]{1,0:T(8,128)} %get-tuple-element.47, f32[8,2]{1,0:T(8,128)} %bitcast.64, f32[8,118]{1,0:T(8,128)S(1)} %broadcast.13), dimensions={1} | concatenate | bytes 49152 | tf_op jit(solution)/shard_map/concatenate | solution.py:375
  38.8 2.5 %collective-permute-start.2 = (f32[8,768]{1,0:T(8,128)}, f32[8,768]{1,0:T(8,128)S(1)}, u32[]{:S(2)}, u32[]{:S(2)}) collective-permute-start(f32[8,768]{1,0:T(8,128)} %concatenate.10), channel_id=1, source_target_pairs={{0,1},{1,2},{2,3},{3,4},{4,5},{5,6},{6,7},{7,8},{8,9},{9,10},{10,1... | collective-permute-start | bytes 73736 | tf_op jit(solution)/shard_map/ppermute | solution.py:377
  41.4 5.0 %collective-permute-done.3.right_ref = f32[8,768]{1,0:T(8,128)S(1)} collective-permute-done((f32[8,768]{1,0:T(8,128)}, f32[8,768]{1,0:T(8,128)S(1)}, u32[]{:S(2)}, u32[]{:S(2)}) %collective-permute-start.3) | collective-permute-done | bytes 24608 | tf_op jit(solution)/shard_map/ppermute | solution.py:378
  46.4 1.4 %copy-done.2 = f32[640,640]{1,0:T(8,128)S(1)} copy-done((f32[640,640]{1,0:T(8,128)S(1)}, f32[640,640]{1,0:T(8,128)}, u32[]{:S(2)}) %copy-start.2) | copy-done | bytes 1638424
  47.8 1.4 %copy-done.4 = s32[640,640]{1,0:T(8,128)S(1)} copy-done((s32[640,640]{1,0:T(8,128)S(1)}, s32[640,640]{1,0:T(8,128)}, u32[]{:S(2)}) %copy-start.4) | copy-done | bytes 1638424
  49.2 3.2 %static.1 = (f32[6,672,128]{2,1,0:T(8,128)S(1)}, s32[6,672,128]{2,1,0:T(8,128)S(1)}, f32[656,128]{1,0:T(8,128)S(1)}, s32[8,128]{1,0:T(8,128)S(1)}) custom-call(s32[4]{0:T(128)S(1)} %add_convert_fusion.edge_ref, f32[640,640]{1,0:T(8,128)S(1)} %copy-done.2, s32[640,640]{1,0:T(8,128)S(1)} %copy-done.4, s32[640,640]{1,0:T(8,128)S(1)} %copy-done, ...), custom_call_target="tpu_custom_call" | custom-call | tf_op jit(solution)/shard_map/static/pallas_call | solution.py:384
  52.5 1.3 %copy-done.7 = f32[6,672,128]{2,1,0:T(8,128)} copy-done((f32[6,672,128]{2,1,0:T(8,128)}, f32[6,672,128]{2,1,0:T(8,128)S(1)}, u32[]{:S(2)}) %copy-start.7) | copy-done | bytes 2064408
  53.8 1.3 %copy-done.9 = s32[6,672,128]{2,1,0:T(8,128)} copy-done((s32[6,672,128]{2,1,0:T(8,128)}, s32[6,672,128]{2,1,0:T(8,128)S(1)}, u32[]{:S(2)}) %copy-start.9) | copy-done | bytes 2064408
  56.8 1.4 %copy-done.6 = f32[640,640]{1,0:T(8,128)S(1)} copy-done((f32[640,640]{1,0:T(8,128)S(1)}, f32[640,640]{1,0:T(8,128)}, u32[]{:S(2)}) %copy-start.6) | copy-done | bytes 1638424
  58.2 1.2 copy-done.14
  60.4 6.4 %place.1 = (f32[6,672,128]{2,1,0:T(8,128)S(1)}, f32[8,640]{1,0:T(8,128)S(1)}, f32[8,640]{1,0:T(8,128)S(1)}) custom-call(f32[3328,128]{1,0:T(8,128)S(1)} %bitcast.45, f32[640,640]{1,0:T(8,128)S(1)} %copy-done.6, f32[656,128]{1,0:T(8,128)S(1)} %copy-done.20, bf16[768,640]{1,0:T(8,128)(2,1)S(1)} %copy-done.14), custom_call_target="tpu_custom_call" | custom-call | tf_op jit(solution)/shard_map/place/pallas_call | solution.py:245
  66.8 1.4 %copy-done.11 = f32[6,672,128]{2,1,0:T(8,128)} copy-done((f32[6,672,128]{2,1,0:T(8,128)}, f32[6,672,128]{2,1,0:T(8,128)S(1)}, u32[]{:S(2)}) %copy-start.11) | copy-done | bytes 2064408
  68.2 1.7 %collective-permute-start.4 = (f32[8,640]{1,0:T(8,128)S(1)}, f32[8,640]{1,0:T(8,128)S(1)}, u32[]{:S(2)}, u32[]{:S(2)}) collective-permute-start(f32[8,640]{1,0:T(8,128)S(1)} %get-tuple-element.36), channel_id=1, source_target_pairs={{0,16},{16,32},{32,48},{48,64},{64,80},{80,96},{96,112},{112,0},{1... | collective-permute-start | bytes 61448 | tf_op jit(solution)/shard_map/ppermute | solution.py:563
  69.9 1.9 %collective-permute-start.5 = (f32[8,640]{1,0:T(8,128)S(1)}, f32[8,640]{1,0:T(8,128)S(1)}, u32[]{:S(2)}, u32[]{:S(2)}) collective-permute-start(f32[8,640]{1,0:T(8,128)S(1)} %get-tuple-element.37), channel_id=1, source_target_pairs={{0,112},{16,0},{32,16},{48,32},{64,48},{80,64},{96,80},{112,96},{1... | collective-permute-start | bytes 61448 | tf_op jit(solution)/shard_map/ppermute | solution.py:564
  72.9 2.2 %collective-permute-done.5.down_ref = f32[8,640]{1,0:T(8,128)S(1)} collective-permute-done((f32[8,640]{1,0:T(8,128)S(1)}, f32[8,640]{1,0:T(8,128)S(1)}, u32[]{:S(2)}, u32[]{:S(2)}) %collective-permute-start.5) | collective-permute-done | bytes 20512 | tf_op jit(solution)/shard_map/ppermute | solution.py:564
  75.1 1.6 %copy-done.8 = f32[6,672,128]{2,1,0:T(8,128)S(1)} copy-done((f32[6,672,128]{2,1,0:T(8,128)S(1)}, f32[6,672,128]{2,1,0:T(8,128)}, u32[]{:S(2)}) %copy-start.8) | copy-done | bytes 2064408
  76.7 1.6 %copy-done.10 = s32[6,672,128]{2,1,0:T(8,128)S(1)} copy-done((s32[6,672,128]{2,1,0:T(8,128)S(1)}, s32[6,672,128]{2,1,0:T(8,128)}, u32[]{:S(2)}) %copy-start.10) | copy-done | bytes 2064408
  78.2 1.6 %copy-done.12 = f32[6,672,128]{2,1,0:T(8,128)S(1)} copy-done((f32[6,672,128]{2,1,0:T(8,128)S(1)}, f32[6,672,128]{2,1,0:T(8,128)}, u32[]{:S(2)}) %copy-start.12) | copy-done | bytes 2064408
  79.8 24.7 %route.1 = (f32[640,640]{1,0:T(8,128)}, f32[128,128]{1,0:T(8,128)}) custom-call(s32[8,128]{1,0:T(8,128)S(1)} %get-tuple-element.32.ranges, f32[6,672,128]{2,1,0:T(8,128)S(1)} %copy-done.12, f32[8,640]{1,0:T(8,128)S(1)} %collective-permute-done.4.up_ref, f32[8,640]{1,0:T(8,128)S(1)} %collective-permute-done.5.down_ref, f32[6,672,128]{2,1,0:T(8,128)S(1)} %copy-done.8, ...), custom_call_target="tpu_custom_call" | custom-call | tf_op jit(solution)/shard_map/route/pallas_call | solution.py:505
  104.6 13.1 %all-to-all-start.1 = ((f32[128,1,128]{2,1,0:T(1,128)}), f32[128,1,128]{2,1,0:T(1,128)S(1)}, u32[]{:S(2)}, u32[]{:S(2)}) async-start(f32[128,1,128]{2,1,0:T(1,128)} %bitcast.28), calls=%async_computation.1 | async-start | bytes 131072 | tf_op jit(solution)/shard_map/all_to_all | solution.py:566
  118.4 8.7 %all-to-all-done.1 = f32[128,1,128]{2,1,0:T(1,128)S(1)} async-done(((f32[128,1,128]{2,1,0:T(1,128)}), f32[128,1,128]{2,1,0:T(1,128)S(1)}, u32[]{:S(2)}, u32[]{:S(2)}) %all-to-all-start.1) | async-done | bytes 65568 | tf_op jit(solution)/shard_map/all_to_all | solution.py:566
  127.8 1.4 %pool.1 = (f32[1,64]{1,0:T(1,128)}, f32[1,64]{1,0:T(1,128)}) custom-call(f32[128,128]{1,0:T(8,128)} %bitcast.50, f32[1,64]{1,0:T(1,128)} %bitcast.65, f32[1,64]{1,0:T(1,128)} %bitcast.66, f32[1,64]{1,0:T(1,128)} %bitcast.67), custom_call_target="tpu_custom_call" | custom-call | tf_op jit(solution)/shard_map/pool/pallas_call | solution.py:528
  (69 shorter events, 12.7 us)
Async XLA Ops:
  0.6 1.5 %copy-start.13 = (f32[100,4096]{1,0:T(8,128)S(1)}, f32[100,4096]{1,0:T(8,128)}, u32[]{:S(2)}) copy-start(f32[100,4096]{1,0:T(8,128)} %weights_ref.1) | copy-start | bytes 4915204
  2.1 0.8 copy-start.15
  5.2 7.7 %copy-start = (s32[640,640]{1,0:T(8,128)S(1)}, s32[640,640]{1,0:T(8,128)}, u32[]{:S(2)}) copy-start(s32[640,640]{1,0:T(8,128)} %slot_ref.2) | copy-start | bytes 4915204
  5.2 7.7 %copy-start.1 = (f32[640,640]{1,0:T(8,128)S(1)}, f32[640,640]{1,0:T(8,128)}, u32[]{:S(2)}) copy-start(f32[640,640]{1,0:T(8,128)} %rate_ref.1) | copy-start | bytes 4915204
  12.9 1.4 %copy-start.3 = (s32[640,640]{1,0:T(8,128)S(1)}, s32[640,640]{1,0:T(8,128)}, u32[]{:S(2)}) copy-start(s32[640,640]{1,0:T(8,128)} %code_ref.1) | copy-start | bytes 4915204
  14.4 1.4 %copy-start.5 = (f32[640,640]{1,0:T(8,128)S(1)}, f32[640,640]{1,0:T(8,128)}, u32[]{:S(2)}) copy-start(f32[640,640]{1,0:T(8,128)} %head_ref.1) | copy-start | bytes 4915204
  17.0 15.5 %collective-permute-start = (f32[8,640]{1,0:T(8,128)}, f32[8,640]{1,0:T(8,128)S(1)}, u32[]{:S(2)}, u32[]{:S(2)}) collective-permute-start(f32[8,640]{1,0:T(8,128)} %get-tuple-element.29), channel_id=1, source_target_pairs={{0,16},{16,32},{32,48},{48,64},{64,80},{80,96},{96,112},{112,0},{1... | collective-permute-start | bytes 61448 | tf_op jit(solution)/shard_map/ppermute | solution.py:366
  19.1 13.5 %collective-permute-start.1 = (f32[8,640]{1,0:T(8,128)}, f32[8,640]{1,0:T(8,128)S(1)}, u32[]{:S(2)}, u32[]{:S(2)}) collective-permute-start(f32[8,640]{1,0:T(8,128)} %get-tuple-element.30), channel_id=1, source_target_pairs={{0,112},{16,0},{32,16},{48,32},{64,48},{80,64},{96,80},{112,96},{1... | collective-permute-start | bytes 61448 | tf_op jit(solution)/shard_map/ppermute | solution.py:367
  21.9 8.6 %copy-start.16 = (f32[4,4096]{1,0:T(4,128)S(1)}, f32[4,4096]{1,0:T(4,128)}, u32[]{:S(2)}) copy-start(f32[4,4096]{1,0:T(4,128)} %conduct_ref.1) | copy-start | bytes 196612
  21.9 8.6 %copy-start.18 = (f32[4,4096]{1,0:T(4,128)S(1)}, f32[4,4096]{1,0:T(4,128)}, u32[]{:S(2)}) copy-start(f32[4,4096]{1,0:T(4,128)} %moisture_ref.1) | copy-start | bytes 196612
  21.9 34.8 %all-to-all-start = ((f32[128,1,3328]{2,1,0:T(1,128)}), f32[128,1,3328]{2,1,0:T(1,128)S(1)}, u32[]{:S(2)}, u32[]{:S(2)}) async-start(f32[128,1,3328]{2,1,0:T(1,128)} %bitcast.23), calls=%async_computation | async-start | bytes 3407872 | tf_op jit(solution)/shard_map/all_to_all | solution.py:557
  34.9 11.5 %collective-permute-start.3 = (f32[8,768]{1,0:T(8,128)}, f32[8,768]{1,0:T(8,128)S(1)}, u32[]{:S(2)}, u32[]{:S(2)}) collective-permute-start(f32[8,768]{1,0:T(8,128)} %concatenate.11), channel_id=1, source_target_pairs={{0,15},{1,0},{2,1},{3,2},{4,3},{5,4},{6,5},{7,6},{8,7},{9,8},{10,9... | collective-permute-start | bytes 73736 | tf_op jit(solution)/shard_map/ppermute | solution.py:378
  38.8 7.5 %collective-permute-start.2 = (f32[8,768]{1,0:T(8,128)}, f32[8,768]{1,0:T(8,128)S(1)}, u32[]{:S(2)}, u32[]{:S(2)}) collective-permute-start(f32[8,768]{1,0:T(8,128)} %concatenate.10), channel_id=1, source_target_pairs={{0,1},{1,2},{2,3},{3,4},{4,5},{5,6},{6,7},{7,8},{8,9},{9,10},{10,1... | collective-permute-start | bytes 73736 | tf_op jit(solution)/shard_map/ppermute | solution.py:377
  46.4 1.4 %copy-start.2 = (f32[640,640]{1,0:T(8,128)S(1)}, f32[640,640]{1,0:T(8,128)}, u32[]{:S(2)}) copy-start(f32[640,640]{1,0:T(8,128)} %rate_ref.1) | copy-start | bytes 4915204
  47.8 1.4 %copy-start.4 = (s32[640,640]{1,0:T(8,128)S(1)}, s32[640,640]{1,0:T(8,128)}, u32[]{:S(2)}) copy-start(s32[640,640]{1,0:T(8,128)} %code_ref.1) | copy-start | bytes 4915204
  52.5 1.3 %copy-start.7 = (f32[6,672,128]{2,1,0:T(8,128)}, f32[6,672,128]{2,1,0:T(8,128)S(1)}, u32[]{:S(2)}) copy-start(f32[6,672,128]{2,1,0:T(8,128)S(1)} %get-tuple-element.38.rates_ref) | copy-start | bytes 6193156
  53.8 1.3 %copy-start.9 = (s32[6,672,128]{2,1,0:T(8,128)}, s32[6,672,128]{2,1,0:T(8,128)S(1)}, u32[]{:S(2)}) copy-start(s32[6,672,128]{2,1,0:T(8,128)S(1)} %get-tuple-element.39.codes_ref) | copy-start | bytes 6193156
  56.8 1.4 %copy-start.6 = (f32[640,640]{1,0:T(8,128)S(1)}, f32[640,640]{1,0:T(8,128)}, u32[]{:S(2)}) copy-start(f32[640,640]{1,0:T(8,128)} %head_ref.1) | copy-start | bytes 4915204
  58.2 1.2 copy-start.14
  59.4 1.0 copy-start.20
  60.4 11.4 %copy-start.22 = (f32[4096]{0:T(1024)S(1)}, f32[4096]{0:T(1024)}, u32[]{:S(2)}) copy-start(f32[4096]{0:T(1024)} %param.17) | copy-start | bytes 49156
  60.4 11.4 %copy-start.27 = (f32[1,4096]{1,0:T(1,128)S(1)}, f32[1,4096]{1,0:T(1,128)}, u32[]{:S(2)}) copy-start(f32[1,4096]{1,0:T(1,128)} %fusion.3) | copy-start | bytes 49156
  60.4 11.4 %copy-start.24 = (s32[64]{0:T(128)S(1)}, s32[64]{0:T(128)}, u32[]{:S(2)}) copy-start(s32[64]{0:T(128)} %param.24) | copy-start | bytes 772
  66.8 1.4 %copy-start.11 = (f32[6,672,128]{2,1,0:T(8,128)}, f32[6,672,128]{2,1,0:T(8,128)S(1)}, u32[]{:S(2)}) copy-start(f32[6,672,128]{2,1,0:T(8,128)S(1)} %get-tuple-element.35.depth_ref) | copy-start | bytes 6193156
  68.2 4.7 %collective-permute-start.4 = (f32[8,640]{1,0:T(8,128)S(1)}, f32[8,640]{1,0:T(8,128)S(1)}, u32[]{:S(2)}, u32[]{:S(2)}) collective-permute-start(f32[8,640]{1,0:T(8,128)S(1)} %get-tuple-element.36), channel_id=1, source_target_pairs={{0,16},{16,32},{32,48},{48,64},{64,80},{80,96},{96,112},{112,0},{1... | collective-permute-start | bytes 61448 | tf_op jit(solution)/shard_map/ppermute | solution.py:563
  69.9 5.2 %collective-permute-start.5 = (f32[8,640]{1,0:T(8,128)S(1)}, f32[8,640]{1,0:T(8,128)S(1)}, u32[]{:S(2)}, u32[]{:S(2)}) collective-permute-start(f32[8,640]{1,0:T(8,128)S(1)} %get-tuple-element.37), channel_id=1, source_target_pairs={{0,112},{16,0},{32,16},{48,32},{64,48},{80,64},{96,80},{112,96},{1... | collective-permute-start | bytes 61448 | tf_op jit(solution)/shard_map/ppermute | solution.py:564
  75.1 1.6 %copy-start.8 = (f32[6,672,128]{2,1,0:T(8,128)S(1)}, f32[6,672,128]{2,1,0:T(8,128)}, u32[]{:S(2)}) copy-start(f32[6,672,128]{2,1,0:T(8,128)} %copy-done.7) | copy-start | bytes 6193156
  76.7 1.6 %copy-start.10 = (s32[6,672,128]{2,1,0:T(8,128)S(1)}, s32[6,672,128]{2,1,0:T(8,128)}, u32[]{:S(2)}) copy-start(s32[6,672,128]{2,1,0:T(8,128)} %copy-done.9) | copy-start | bytes 6193156
  78.2 1.6 %copy-start.12 = (f32[6,672,128]{2,1,0:T(8,128)S(1)}, f32[6,672,128]{2,1,0:T(8,128)}, u32[]{:S(2)}) copy-start(f32[6,672,128]{2,1,0:T(8,128)} %copy-done.11) | copy-start | bytes 6193156
  79.8 37.9 %copy-start.25 = (f32[4,4096]{1,0:T(4,128)S(1)}, f32[4,4096]{1,0:T(4,128)}, u32[]{:S(2)}) copy-start(f32[4,4096]{1,0:T(4,128)} %get-tuple-element.45) | copy-start | bytes 196612
  79.8 37.9 %copy-start.28 = (f32[4]{0:T(128)S(1)}, f32[4]{0:T(128)}, u32[]{:S(2)}) copy-start(f32[4]{0:T(128)} %constant.37) | copy-start | bytes 52
  104.6 22.6 %all-to-all-start.1 = ((f32[128,1,128]{2,1,0:T(1,128)}), f32[128,1,128]{2,1,0:T(1,128)S(1)}, u32[]{:S(2)}, u32[]{:S(2)}) async-start(f32[128,1,128]{2,1,0:T(1,128)} %bitcast.28), calls=%async_computation.1 | async-start | bytes 131072 | tf_op jit(solution)/shard_map/all_to_all | solution.py:566
  (5 other events, 3.6 us)
where the time goes:
time: 130 us; the launch traced here: 129 us
  Pallas kernels  44.8 us (34%)
  starting transfers between devices  33.7 us (26%)
  local copies, waits for them, and re-layouts  30 us (23%)
  waiting for transfers between devices  17.8 us (14%)
  other arithmetic  2.08 us (2%)
    pallas_call x1, Pallas kernels, route(): pl.pallas_call(route_kernel, out_shape=(jax.ShapeDtypeStruct(lake_slot.sh...  24.7 us
    unnamed x58, local copies, waits for them, and re-layouts  24 us
    all_to_all x1, starting transfers between devices, body(): lax.all_to_all(spread.reshape(RUNS, 1, LANES), both, split_axis=0, concat...  13.1 us
    all_to_all x1, waiting for transfers between devices, body(): lax.all_to_all(spread.reshape(RUNS, 1, LANES), both, split_axis=0, concat...  8.73 us
    all_to_all x1, starting transfers between devices, body(): lax.all_to_all(payload.reshape(RUNS, 1, RUN_ROWS * LANES), both, split_ax...  8.6 us
    pallas_call x1, Pallas kernels, land_payload(): pl.pallas_call(send_kernel, out_shape=jax.ShapeDtypeStruct((RUNS * RUN_RO...  7.71 us
    pallas_call x1, Pallas kernels, place(): pl.pallas_call(place_kernel, out_shape=(jax.ShapeDtypeStruct((SLABS, ROWS...  6.43 us
    ppermute x1, waiting for transfers between devices, statics(): right = lax.ppermute(tall(cols[0:8], slice(0, 2)), 'col', ring('col', -1))  4.99 us
  transfers between devices with their start and end apart: 8, of which 5 were waited for; matrix products, arithmetic and copies ran while one was open for 6% of the time, Pallas kernels for 3%

commit v1 on v0

v1 whole, which is shorter than its diff:
```python
import jax
import jax.numpy as jnp
import numpy as np
from jax import lax
from jax.experimental import pallas as pl
from jax.experimental.pallas import tpu as pltpu
from jax.sharding import PartitionSpec as P

AGG = 10
LLOC = 64
LANES = 128
RUNS = 128
RUN_ROWS = 26
SLABS = 6
ROWS = 672
FIRST = 16

LAYER_DEPTHS = (0.1, 0.3, 0.6, 1.0)
POROSITY = 0.45
TIME_STEP = 0.05
F32 = jnp.float32
BF16 = jnp.bfloat16
VMEM = pl.BlockSpec(memory_space=pltpu.VMEM)
HBM = pl.BlockSpec(memory_space=pltpu.HBM)
SMEM = pl.BlockSpec(memory_space=pltpu.SMEM)


def params(mebibytes=60):
    return pltpu.CompilerParams(vmem_limit_bytes=mebibytes * 1024 * 1024)


def lanes_of(shape):
    return lax.broadcasted_iota(jnp.int32, shape, len(shape) - 1)


def rows_of(shape):
    return lax.broadcasted_iota(jnp.int32, shape, 0)


def split3(value):
    high = value.astype(BF16)
    rest = value - high.astype(F32)
    middle = rest.astype(BF16)
    low = (rest - middle.astype(F32)).astype(BF16)
    return high, middle, low


def select_dot(picks, value):
    return sum(jnp.dot(picks, part, preferred_element_type=F32) for part in split3(value))


def signed(rate, lake):
    return jnp.where(lake, -rate, rate)


def ring(axis, step):
    count = lax.axis_size(axis)
    return [(i, (i + step) % count) for i in range(count)]


def dot_select(value, picks):
    return sum(jnp.dot(part, picks, preferred_element_type=F32) for part in split3(value))


def quarter_transpose(arrays, quarter):
    rolled = []
    for d in range(4):
        skew = arrays[(3 + d) % 4]
        for m in range(3):
            skew = jnp.where(quarter == m, arrays[(m + d) % 4], skew)
        rolled.append(pltpu.roll(skew, 32 * d, 1) if d else skew)
    outs = []
    for r in range(4):
        out = rolled[(3 - r) % 4]
        for m in range(3):
            out = jnp.where(quarter == m, rolled[(m - r) % 4], out)
        outs.append(out)
    return outs


def send_kernel(
    tile_hbm, moisture_hbm, conduct_hbm, rain_hbm, weights_hbm, out_ref,
    tile_ref, moisture_ref, conduct_ref, rain_ref, slab_ref, edge_ref, sems,
):
    count = slab_ref.shape[0]

    def fetch(i):
        start = pl.multiple_of(i * LANES, LANES)
        return pltpu.make_async_copy(weights_hbm.at[:, pl.ds(start, LANES)], slab_ref.at[i], sems.at[i])

    small = [
        pltpu.make_async_copy(source, into, sems.at[count + n])
        for n, (source, into) in enumerate(
            ((tile_hbm, tile_ref), (moisture_hbm, moisture_ref), (conduct_hbm, conduct_ref), (rain_hbm, rain_ref))
        )
    ]
    for copy in small:
        copy.start()

    def begin(i, carry):
        fetch(i).start()
        return carry

    lax.fori_loop(0, count, begin, 0, unroll=4)
    for copy in small:
        copy.wait()
    lane = lanes_of((1, LANES))
    quarter = lane >> 5

    def step(i, carry):
        edges, tiles = carry
        start = pl.multiple_of(i * LANES, LANES)
        conduct = conduct_ref[0:1, pl.ds(start, LANES)]
        moisture = moisture_ref[0:1, pl.ds(start, LANES)]
        rain = rain_ref[0:1, pl.ds(start, LANES)]
        capacity = 10.0 * conduct * (1.5 - moisture / POROSITY)
        runoff = rain - rain * capacity / (rain + capacity)
        fetch(i).wait()
        parts = [slab_ref[i, pl.ds(b, AGG, stride=AGG), :] for b in range(AGG)]
        total = sum(parts[1:], parts[0])
        mean = jnp.sum(total, axis=0, keepdims=True) * 0.01
        scale = runoff / mean
        parts = [part * scale for part in parts]
        tail = [slab_ref[i, pl.ds(first, 5, stride=AGG), :] * scale for first in (8, 9, 58, 59)]
        groups = (
            (0, AGG, quarter_transpose(parts[0:4], quarter)),
            (AGG, AGG, quarter_transpose(parts[4:8], quarter)),
            (2 * AGG, 5, quarter_transpose(tail, quarter)),
        )
        for r in range(4):
            tile = tile_ref[(4 * i + r) * 32]
            tiles = jnp.where(lane == 32 * r + i, tile, tiles)
            for offset, length, outs in groups:
                out_ref[pl.ds(tile * RUN_ROWS + offset, length), :] = outs[r]
        place = lane & 63
        new_edges = []
        for b in range(2):
            left = pltpu.roll(parts[b], i, 1)
            right = pltpu.roll(parts[8 + b], i + 97, 1)
            edge = jnp.where(place == i, left, edges[b])
            new_edges.append(jnp.where(place == i + 32, right, edge))
        return tuple(new_edges), tiles

    zeros = jnp.zeros((AGG, LANES), F32)
    edges, tiles = lax.fori_loop(0, count, step, ((zeros, zeros), jnp.zeros((1, LANES), jnp.int32)))
    edge_ref[...] = jnp.zeros((LANES, LANES), F32)
    edge_ref[0:AGG, :] = edges[0]
    edge_ref[16 : 16 + AGG, :] = edges[1]
    edge_ref[15:16, :] = (4 * (lane & 31) + (lane >> 5)).astype(F32)
    by_run = edge_ref[...].T
    square = (LANES, LANES)
    here = (rows_of(square) == tiles).astype(F32).astype(BF16)
    by_tile = select_dot(here, by_run)
    run = by_tile[:, 15:16].astype(jnp.int32)
    wide = lanes_of(square)
    odd = (run & 1) == 1
    no_edge = jnp.where(wide == 15, -1.0, 0.0)
    row = pltpu.roll(jnp.where(odd, by_tile, no_edge), 1, 0)
    row = row + pltpu.roll(pltpu.roll(jnp.where(odd, no_edge, by_tile), LANES - 1, 0), 32, 1)
    row = row + jnp.where(wide == 127, run.astype(F32), 0.0)
    out_ref[pl.ds(25, RUNS, stride=RUN_ROWS), :] = row


def land_payload(land_tile, moisture, conduct, rainfall, weights):
    blocks = weights.shape[1]
    count = blocks // LANES
    return pl.pallas_call(
        send_kernel,
        out_shape=jax.ShapeDtypeStruct((RUNS * RUN_ROWS, LANES), F32),
        in_specs=[HBM] * 5,
        out_specs=VMEM,
        scratch_shapes=[
            pltpu.SMEM((blocks,), jnp.int32),
            pltpu.VMEM(moisture.shape, F32),
            pltpu.VMEM(conduct.shape, F32),
            pltpu.VMEM((1, blocks), F32),
            pltpu.VMEM((count, AGG * AGG, LANES), F32),
            pltpu.VMEM((LANES, LANES), F32),
            pltpu.SemaphoreType.DMA((count + 4,)),
        ],
        compiler_params=params(),
        name="land",
    )(land_tile, moisture, conduct, rainfall.reshape(1, blocks), weights)


def spread_columns():
    picks = np.zeros((SLABS * LANES, 640), np.float32)
    for half in range(2):
        for j in range(3):
            for k in range(4 if j < 2 else 2):
                for i in range(32):
                    picks[(half * 3 + j) * LANES + 32 * k + i, (half * 32 + i) * AGG + 4 * j + k] = 1.0
    return picks


def place_kernel(
    edge_ref, left_ref, right_ref, top_in, bottom_in, pay_hbm, head_hbm, picks_hbm,
    depth_hbm, rate_hbm, code_hbm, top_ref, bottom_ref,
    pay_ref, head_ref, picks_ref, depth_ref, rate_ref, code_ref, turn_ref, cells_ref, tag_ref, tags, sems,
):
    fetches = [
        pltpu.make_async_copy(source, into, sems.at[n])
        for n, (source, into) in enumerate(((pay_hbm, pay_ref), (picks_hbm, picks_ref), (head_hbm, head_ref)))
    ]
    for copy in fetches:
        copy.start()
    top_ref[...] = top_in[...]
    bottom_ref[...] = bottom_in[...]
    turn_ref[...] = jnp.zeros(turn_ref.shape, F32)
    turn_ref[0:8, :] = right_ref[...]
    turn_ref[8:16, :] = left_ref[...]
    turned = turn_ref[...].T
    tall = (640, LANES)
    lane = lanes_of(tall)
    rightmost = lane < 2
    leftmost = lane >= 126

    def slab(n):
        right = pltpu.roll(turned, LANES - 2 * n, 1) if n else turned
        left = pltpu.roll(turned, 118 - 2 * n, 1)
        return jnp.where(rightmost, right, jnp.where(leftmost, left, 0.0))

    first_col, last_col = edge_ref[2] == 1, edge_ref[3] == 1
    inside = (rightmost & jnp.logical_not(last_col)) | (leftmost & jnp.logical_not(first_col))
    side_rate = slab(0)
    side_code = jnp.where(inside, slab(1), -1.0)
    side_lake = slab(2)
    side_head = slab(3)
    rate_ref[...] = signed(side_rate, side_lake > 0.5)
    code_ref[...] = side_code.astype(jnp.int32)
    stores = [
        pltpu.make_async_copy(source, into, sems.at[n + 3])
        for n, (source, into) in enumerate(((rate_ref, rate_hbm), (code_ref, code_hbm)))
    ]
    for copy in stores:
        copy.start()
    for ref, rows in ((top_ref, slice(0, 2)), (bottom_ref, slice(638, 640))):
        ref[2:4, 640:768] = side_rate[rows]
        ref[4:6, 640:768] = side_code[rows]
        ref[6:8, 640:768] = side_lake[rows]

    fetches[0].wait()
    arrived = pay_ref[pl.ds(25, RUNS, stride=RUN_ROWS), :]
    by_lane = arrived.T
    tag_ref[...] = jnp.broadcast_to(by_lane[127:128, :].astype(jnp.int32), (8, LANES))
    copy = pltpu.make_async_copy(tag_ref, tags, sems.at[5])
    copy.start()
    row = rows_of(tall)
    block = (row * 6554) >> 16
    left = (by_lane[15:16, :].astype(jnp.int32) == 2 * block + 1).astype(F32).astype(BF16)
    right = (by_lane[47:48, :].astype(jnp.int32) == 2 * block).astype(F32).astype(BF16)
    square = (LANES, LANES)
    wide = lanes_of(square)
    strips = select_dot(left, jnp.where(wide < 32, arrived, 0.0))
    strips = strips + select_dot(right, jnp.where((wide >= 32) & (wide < 64), arrived, 0.0))
    strips = jnp.where((lane & 15) == row - AGG * block, strips, 0.0)
    source = rows_of(square)
    group = source >> 4
    target = jnp.where(group < 2, 126, 0) + (group & 1)
    fold = (((source & 15) < AGG) & (group < 4) & (target == wide)).astype(F32).astype(BF16)
    depth = dot_select(strips, fold) + side_head
    depth_ref[SLABS - 1, FIRST : FIRST + 640, :] = depth
    top_ref[0:2, 640:768] = depth[0:2]
    bottom_ref[0:2, 640:768] = depth[638:640]
    copy.wait()

    def settle(s, carry):
        run = tags[0, s]
        slab = (run & 1) * 3
        row = (run >> 1) * AGG
        start = s * RUN_ROWS
        cells_ref[slab, pl.ds(row, AGG), :] = pay_ref[pl.ds(start, AGG), :]
        cells_ref[slab + 1, pl.ds(row, AGG), :] = pay_ref[pl.ds(start + AGG, AGG), :]
        last = pay_ref[pl.ds(start + 2 * AGG, 5), :]
        cells_ref[slab + 2, pl.ds(row, 5), :] = last
        cells_ref[slab + 2, pl.ds(row + 5, 5), :] = pltpu.roll(last, 64, 1)
        return carry

    lax.fori_loop(0, RUNS, settle, 0, unroll=16)
    for copy in fetches[1:]:
        copy.wait()
    picks = picks_ref[...]
    chunk = 160
    for m in range(0, 640, chunk):
        cells = jnp.concatenate([cells_ref[c, m : m + chunk, :] for c in range(SLABS)], axis=1)
        laid = dot_select(cells, picks)
        for c in range(SLABS - 1):
            columns = slice(c * LANES, (c + 1) * LANES)
            depth = laid[:, columns] + head_ref[m : m + chunk, columns]
            depth_ref[c, FIRST + m : FIRST + m + chunk, :] = depth
            if m == 0:
                top_ref[0:2, columns] = depth[0:2]
            if m == 640 - chunk:
                bottom_ref[0:2, columns] = depth[chunk - 2 :]
        rows = pl.ds(FIRST + m, chunk)
        store = pltpu.make_async_copy(depth_ref.at[:, rows, :], depth_hbm.at[:, rows, :], sems.at[6 + m // chunk])
        store.start()
        stores.append(store)
    for store in stores:
        store.wait()


def place(edges, left, right, top, bottom, payload, head):
    picks = jnp.asarray(spread_columns(), BF16)
    strip = jax.ShapeDtypeStruct((8, 768), F32)
    slabs = (SLABS, ROWS, LANES)
    side = (640, LANES)
    return pl.pallas_call(
        place_kernel,
        out_shape=(
            jax.ShapeDtypeStruct(slabs, F32),
            jax.ShapeDtypeStruct(side, F32),
            jax.ShapeDtypeStruct(side, jnp.int32),
            strip,
            strip,
        ),
        in_specs=[SMEM] + [VMEM] * 4 + [HBM] * 3,
        out_specs=(HBM, HBM, HBM, VMEM, VMEM),
        scratch_shapes=[
            pltpu.VMEM(payload.shape, F32),
            pltpu.VMEM(head.shape, F32),
            pltpu.VMEM(picks.shape, BF16),
            pltpu.VMEM(slabs, F32),
            pltpu.VMEM(side, F32),
            pltpu.VMEM(side, jnp.int32),
            pltpu.VMEM((LANES, 640), F32),
            pltpu.VMEM((SLABS, 640, LANES), F32),
            pltpu.VMEM((8, LANES), jnp.int32),
            pltpu.SMEM((8, LANES), jnp.int32),
            pltpu.SemaphoreType.DMA((10,)),
        ],
        compiler_params=params(),
        name="place",
    )(edges, left, right, top, bottom, payload, head, picks)


def rim_kernel(
    moisture_ref, conduct_ref, rain_ref, rate_hbm, code_hbm, slot_hbm, head_hbm, cols_ref, soil_ref,
    rate_ref, code_ref, slot_ref, head_ref, sems,
):
    fetches = []
    for n, (source, into) in enumerate(
        ((rate_hbm, rate_ref), (code_hbm, code_ref), (slot_hbm, slot_ref), (head_hbm, head_ref))
    ):
        for side in range(2):
            columns = pl.ds(side * 512, LANES)
            fetches.append(pltpu.make_async_copy(source.at[:, columns], into.at[side], sems.at[2 * n + side]))
    for copy in fetches:
        copy.start()
    for copy in fetches:
        copy.wait()

    def four(side):
        code = code_ref[side].astype(F32)
        lake = (slot_ref[side] < LLOC).astype(F32)
        return rate_ref[side], code, lake, head_ref[side]

    lane = lanes_of((640, LANES))
    gathered = jnp.zeros((640, LANES), F32)
    for n, first in enumerate(four(0)):
        value = pltpu.roll(first, 2 * n, 1) if n else first
        gathered = jnp.where((lane >> 1) == n, value, gathered)
    for n, last in enumerate(four(1)):
        value = pltpu.roll(last, 2 * n + 10, 1)
        gathered = jnp.where((lane >> 1) == n + 4, value, gathered)
    cols_ref[...] = gathered.T[0:16, :]

    rain = rain_ref[...]
    saturation = moisture_ref[...] / POROSITY
    squared = saturation * saturation
    drainage = conduct_ref[...] * (squared * squared)
    capacity = 10.0 * conduct_ref[0:1, :] * (1.5 - saturation[0:1])
    incoming = rain * capacity / (rain + capacity)
    for k, thickness in enumerate(LAYER_DEPTHS):
        leaving = drainage[k : k + 1]
        soil_ref[k : k + 1, :] = moisture_ref[k : k + 1, :] + TIME_STEP * (incoming - leaving) / thickness
        incoming = leaving


def rim(moisture, conduct, rainfall, rate, flow_code, lake_slot, head):
    pair = (2, 640, LANES)
    return pl.pallas_call(
        rim_kernel,
        out_shape=(jax.ShapeDtypeStruct((16, 640), F32), jax.ShapeDtypeStruct(moisture.shape, F32)),
        in_specs=[VMEM] * 3 + [HBM] * 4,
        out_specs=(VMEM,) * 2,
        scratch_shapes=[
            pltpu.VMEM(pair, F32),
            pltpu.VMEM(pair, jnp.int32),
            pltpu.VMEM(pair, jnp.int32),
            pltpu.VMEM(pair, F32),
            pltpu.SemaphoreType.DMA((8,)),
        ],
        compiler_params=params(),
        cost_estimate=pl.CostEstimate(flops=0, bytes_accessed=0, transcendentals=0),
        name="rim",
    )(moisture, conduct, rainfall.reshape(1, rainfall.shape[0]), rate, flow_code, lake_slot, head)


def static_kernel(
    rate_hbm, code_hbm, slot_hbm, rates_hbm, codes_hbm, ranges_ref, top_ref, bottom_ref,
    rate_ref, code_ref, slot_ref, rates_ref, codes_ref, bits_ref, sems,
):
    fetches = [
        pltpu.make_async_copy(source, into, sems.at[n])
        for n, (source, into) in enumerate(((rate_hbm, rate_ref), (code_hbm, code_ref), (slot_hbm, slot_ref)))
    ]
    for copy in fetches:
        copy.start()
    for copy in fetches:
        copy.wait()
    for ref, base, part in ((top_ref, 0, slice(0, 2)), (bottom_ref, 632, slice(6, 8))):
        rows = slice(base, base + 8)
        ref[...] = jnp.zeros((8, 768), F32)
        ref[2:4, 0:640] = rate_ref[rows, :][part]
        ref[4:6, 0:640] = code_ref[rows, :][part].astype(F32)
        ref[6:8, 0:640] = (slot_ref[rows, :][part] < LLOC).astype(F32)

    def center(g, carry):
        rows = pl.ds(pl.multiple_of(g * 8, 8), 8)
        into = pl.ds(pl.multiple_of(g * 8 + FIRST, 8), 8)
        low = jnp.zeros((8, LANES), jnp.int32)
        high = jnp.zeros((8, LANES), jnp.int32)
        for c in range(SLABS - 1):
            columns = slice(c * LANES, (c + 1) * LANES)
            slot = slot_ref[rows, columns]
            rates_ref[c, into, :] = signed(rate_ref[rows, columns], slot < LLOC)
            codes_ref[c, into, :] = code_ref[rows, columns]
            bit = jnp.left_shift(1, slot & 31)
            low = low | jnp.where(slot < 32, bit, 0)
            high = high | jnp.where((slot >= 32) & (slot < LLOC), bit, 0)
        for shift in (4, 2, 1):
            low = low | pltpu.roll(low, shift, 0)
            high = high | pltpu.roll(high, shift, 0)
        bits_ref[0, pl.ds(g, 1), :] = low[0:1]
        bits_ref[1, pl.ds(g, 1), :] = high[0:1]
        return carry

    lax.fori_loop(0, 80, center, 0, unroll=8)
    stores = [
        pltpu.make_async_copy(source, into, sems.at[3 + n])
        for n, (source, into) in enumerate(((rates_ref, rates_hbm), (codes_ref, codes_hbm)))
    ]
    for copy in stores:
        copy.start()
    low, high = bits_ref[0], bits_ref[1]
    for shift in (64, 32, 16, 8, 4, 2, 1):
        low = low | pltpu.roll(low, shift, 1)
        high = high | pltpu.roll(high, shift, 1)
    shape = (80, LANES)
    lane = lanes_of(shape)
    found = (jnp.right_shift(jnp.where(lane < 32, low, high), lane & 31) & 1) == 1
    group = rows_of(shape)
    begin = jnp.min(jnp.where(found, group, 80), axis=0, keepdims=True)
    end = jnp.max(jnp.where(found, group + 1, 0), axis=0, keepdims=True)
    longest = jnp.max(jnp.where(lane[0:1] < LLOC, end - begin, 0), axis=1, keepdims=True)
    ranges_ref[...] = jnp.zeros((8, LANES), jnp.int32)
    ranges_ref[0:1, :] = begin
    ranges_ref[1:2, :] = end
    ranges_ref[2:3, :] = jnp.broadcast_to(longest, (1, LANES))
    for copy in stores:
        copy.wait()


def statics(rate, flow_code, lake_slot):
    slabs = (SLABS - 1, ROWS, LANES)
    strip = jax.ShapeDtypeStruct((8, 768), F32)
    return pl.pallas_call(
        static_kernel,
        out_shape=(
            jax.ShapeDtypeStruct(slabs, F32),
            jax.ShapeDtypeStruct(slabs, jnp.int32),
            jax.ShapeDtypeStruct((8, LANES), jnp.int32),
            strip,
            strip,
        ),
        in_specs=[HBM, HBM, HBM],
        out_specs=(HBM, HBM, VMEM, VMEM, VMEM),
        scratch_shapes=[
            pltpu.VMEM(rate.shape, F32),
            pltpu.VMEM(rate.shape, jnp.int32),
            pltpu.VMEM(rate.shape, jnp.int32),
            pltpu.VMEM(slabs, F32),
            pltpu.VMEM(slabs, jnp.int32),
            pltpu.VMEM((2, 80, LANES), jnp.int32),
            pltpu.SemaphoreType.DMA((5,)),
        ],
        compiler_params=params(),
        cost_estimate=pl.CostEstimate(flops=0, bytes_accessed=0, transcendentals=0),
        name="static",
    )(rate, flow_code, lake_slot)


def leave(depth, rate):
    conveyance = rate * jnp.exp(jnp.log(depth) * (2.0 / 3.0))
    return depth * conveyance / (1.0 + conveyance)


def route_kernel(
    edge_ref, ranges, up_ref, down_ref, table_ref, depth_hbm, rates_hbm, codes_hbm, rate_hbm, code_hbm, slot_hbm,
    surface_hbm, spread_ref,
    depth_ref, rates_ref, codes_ref, slot_ref, surface_ref, leave_ref, next_ref, lake_ref, sums_ref, sems,
):
    quarters = [(0, 176), (176, 160), (336, 160), (496, 176)]

    def rows_in(source, into, n, q):
        rows = pl.ds(*quarters[q])
        return pltpu.make_async_copy(source.at[:, rows, :], into.at[:, rows, :], sems.at[4 * n + q])

    depths = [rows_in(depth_hbm, depth_ref, 0, q) for q in range(4)]
    middle, side, rows = pl.ds(0, SLABS - 1), SLABS - 1, pl.ds(FIRST, 640)
    rates = [rows_in(rates_hbm, rates_ref.at[middle], 1, q) for q in range(4)]
    side_rate = pltpu.make_async_copy(rate_hbm, rates_ref.at[side, rows, :], sems.at[15])
    codes = pltpu.make_async_copy(codes_hbm, codes_ref.at[middle], sems.at[8])
    side_code = pltpu.make_async_copy(code_hbm, codes_ref.at[side, rows, :], sems.at[16])
    slots = pltpu.make_async_copy(slot_hbm, slot_ref, sems.at[9])
    side_rate.start()
    for q in range(4):
        depths[q].start()
        rates[q].start()
    codes.start()
    side_code.start()
    slots.start()
    lane = lanes_of((8, LANES))

    def at(g):
        return pl.ds(pl.multiple_of(g * 8, 8), 8)

    def start(c, rows):
        depth = depth_ref[c, rows, :]
        leaving = leave(depth, jnp.abs(rates_ref[c, rows, :]))
        leave_ref[c, rows, :] = leaving
        depth_ref[c, rows, :] = depth - leaving

    eight = (8, LANES)
    rims = ((1, up_ref, 6, edge_ref[0] == 1), (82, down_ref, 0, edge_ref[1] == 1))

    def first(g, carry):
        rows = at(g)
        for c in range(SLABS):
            start(c, rows)
        return carry

    side_rate.wait()
    for q, (begin, end) in enumerate(((2, 22), (22, 42), (42, 62), (62, 82))):
        depths[q].wait()
        rates[q].wait()
        lax.fori_loop(begin, end, first, 0, unroll=2)
    codes.wait()
    side_code.wait()
    for g, ref, offset, outside in rims:
        rows = slice(g * 8, g * 8 + 8)
        two = slice(g * 8 + offset, g * 8 + offset + 2)
        for c in range(SLABS):
            four = ref[:, c * LANES : (c + 1) * LANES]
            depth_ref[c, rows, :] = jnp.zeros(eight, F32)
            rates_ref[c, rows, :] = jnp.ones(eight, F32)
            codes_ref[c, rows, :] = jnp.full(eight, -1, jnp.int32)
            depth_ref[c, two, :] = four[0:2]
            rates_ref[c, two, :] = jnp.where(four[6:8] > 0.5, -four[2:4], four[2:4])
            codes_ref[c, two, :] = jnp.where(outside, -1, four[4:6].astype(jnp.int32))
        first(g, 0)

    def gained(ref, g, slabs):
        east, middle, west = [], [], []
        base = g * 8
        for c in range(SLABS):
            here, above, below = (ref[c, pl.ds(base + d, 8), :] for d in (0, -1, 1))
            code, code_above, code_below = (codes_ref[c, pl.ds(base + d, 8), :] for d in (0, -1, 1))

            def pick(which, number, value):
                return jnp.where(which == number, value, 0.0)

            east.append(pick(code, 0, here) + pick(code_above, 1, above) + pick(code_below, 7, below))
            middle.append(pick(code_above, 2, above) + pick(code_below, 6, below))
            west.append(pick(code, 4, here) + pick(code_above, 3, above) + pick(code_below, 5, below))
        east = [pltpu.roll(value, 1, 1) for value in east]
        west = [pltpu.roll(value, LANES - 1, 1) for value in west]
        return [
            middle[c]
            + jnp.where(lane == 0, east[c - 1], east[c])
            + jnp.where(lane == LANES - 1, west[(c + 1) % SLABS], west[c])
            for c in range(slabs)
        ]

    def second(g, carry):
        rows = at(g)
        for c, gain in enumerate(gained(leave_ref, g, SLABS)):
            rate = rates_ref[c, rows, :]
            lake = rate < 0.0
            depth = depth_ref[c, rows, :] + gain
            kept = jnp.where(lake, 0.0, depth)
            leaving = leave(kept, jnp.abs(rate))
            next_ref[c, rows, :] = leaving
            depth_ref[c, rows, :] = kept - leaving
            if c < SLABS - 1:
                lake_ref[c, rows, :] = depth - kept
        return carry

    lax.fori_loop(1, 81, second, 0, unroll=16)
    for g in (81, 82):
        second(g, 0)

    def third(g, carry):
        rows = at(g)
        out = at(g - 2)
        for c, gain in enumerate(gained(next_ref, g, SLABS - 1)):
            depth = depth_ref[c, rows, :] + gain
            kept = jnp.where(rates_ref[c, rows, :] < 0.0, 0.0, depth)
            lake_ref[c, rows, :] += depth - kept
            surface_ref[out, c * LANES : (c + 1) * LANES] = kept
        return carry

    stores = []
    for q in range(5):
        lax.fori_loop(2 + 16 * q, 18 + 16 * q, third, 0, unroll=16)
        rows = pl.ds(128 * q, 128)
        store = pltpu.make_async_copy(surface_ref.at[rows, :], surface_hbm.at[rows, :], sems.at[10 + q])
        store.start()
        stores.append(store)
    slots.wait()
    sums_ref[...] = jnp.zeros(sums_ref.shape, F32)

    def layer(e, carry):
        def lake(slot, inner):
            g = ranges[0, slot] + e
            wanted = jnp.where(g < ranges[1, slot], slot, -1)
            g = jnp.minimum(g, 79)
            rows = at(g)
            from_rows = at(g + 2)
            into = pl.ds(pl.multiple_of(slot * 8, 8), 8)
            terms = []
            for c in range(SLABS - 1):
                mine = slot_ref[rows, c * LANES : (c + 1) * LANES] == wanted
                terms.append(jnp.where(mine, lake_ref[c, from_rows, :], 0.0))
            sums_ref[into, :] += (terms[0] + terms[1]) + (terms[2] + terms[3]) + terms[4]
            return inner

        return lax.fori_loop(0, LLOC, lake, carry, unroll=8)

    lax.fori_loop(0, ranges[2, 0], layer, 0)
    tall = (LLOC, 8 * LLOC)
    gather = ((lanes_of(tall) >> 3) == rows_of(tall)).astype(F32).astype(BF16)
    totals = jnp.sum(select_dot(gather, sums_ref[...]), axis=1, keepdims=True)
    table = table_ref[...]
    owner = (table >> 6 == rows_of((LANES, LLOC))).astype(F32).astype(BF16)
    small = (LLOC, LLOC)
    turned = jnp.where(rows_of(small) == lanes_of(small), (table & 63).astype(F32), 0.0)
    number = jnp.sum(turned, axis=1, keepdims=True).astype(jnp.int32) == lanes_of((LLOC, LANES))
    spread_ref[...] = select_dot(owner, jnp.where(number, totals, 0.0))
    for store in stores:
        store.wait()


def route(edges, ranges, up, down, depth, rates, codes, rate, code, lake_slot, lake_table):
    slabs = (SLABS, ROWS, LANES)
    slab = pltpu.VMEM(slabs, F32)
    return pl.pallas_call(
        route_kernel,
        out_shape=(jax.ShapeDtypeStruct(lake_slot.shape, F32), jax.ShapeDtypeStruct((LANES, LANES), F32)),
        in_specs=[SMEM] * 2 + [VMEM] * 3 + [HBM] * 6,
        out_specs=(HBM, VMEM),
        scratch_shapes=[
            slab,
            slab,
            pltpu.VMEM(slabs, jnp.int32),
            pltpu.VMEM(lake_slot.shape, jnp.int32),
            pltpu.VMEM(lake_slot.shape, F32),
            slab,
            slab,
            slab,
            pltpu.VMEM((8 * LLOC, LANES), F32),
            pltpu.SemaphoreType.DMA((17,)),
        ],
        compiler_params=params(),
        name="route",
    )(edges, ranges, up, down, lake_table.reshape(1, LLOC), depth, rates, codes, rate, code, lake_slot)


def pool_kernel(spread_ref, phase_ref, area_ref, crest_ref, level_ref, outflow_ref):
    inflow = jnp.sum(spread_ref[...], axis=0, keepdims=True)[:, :LLOC]
    area = area_ref[...]
    phase = phase_ref[...] + inflow / area
    excess = jnp.maximum(phase - crest_ref[...], 0.0)
    outflow = excess * jnp.sqrt(excess)
    level_ref[...] = phase - outflow / area
    outflow_ref[...] = outflow


def level_pool(spread, lake_phase, lake_area, lake_crest):
    row = jax.ShapeDtypeStruct((1, LLOC), F32)
    level, outflow = pl.pallas_call(
        pool_kernel,
        out_shape=(row, row),
        in_specs=[VMEM] * 4,
        out_specs=(VMEM,) * 2,
        compiler_params=params(),
        name="pool",
    )(spread, *(value.reshape(1, LLOC) for value in (lake_phase, lake_area, lake_crest)))
    return level.reshape(LLOC), outflow.reshape(LLOC)


def body(
    moisture, conduct, rainfall, weights, land_tile, head, rate, flow_code, lake_slot, lake_table,
    lake_phase, lake_area, lake_crest,
):
    both = ("row", "col")
    at_row, at_col = lax.axis_index("row"), lax.axis_index("col")
    edges = jnp.stack(
        [at_row == 0, at_row == lax.axis_size("row") - 1, at_col == 0, at_col == lax.axis_size("col") - 1]
    ).astype(jnp.int32)
    payload = land_payload(land_tile, moisture, conduct, rainfall, weights)
    payload, rate, flow_code, lake_slot, head, moisture = lax.optimization_barrier(
        (payload, rate, flow_code, lake_slot, head, moisture)
    )
    arrived = lax.all_to_all(
        payload.reshape(RUNS, 1, RUN_ROWS * LANES), both, split_axis=0, concat_axis=0, tiled=True
    ).reshape(RUNS * RUN_ROWS, LANES)
    cols, new_moisture = rim(moisture, conduct, rainfall, rate, flow_code, lake_slot, head)
    left = lax.ppermute(cols[8:16], "col", ring("col", 1))
    right = lax.ppermute(cols[0:8], "col", ring("col", -1))
    rates, codes, ranges, top, bottom = statics(rate, flow_code, lake_slot)
    depth, side_rate, side_code, top, bottom = place(edges, left, right, top, bottom, arrived, head)
    up = lax.ppermute(bottom, "row", ring("row", 1))
    down = lax.ppermute(top, "row", ring("row", -1))
    surface, spread = route(edges, ranges, up, down, depth, rates, codes, side_rate, side_code, lake_slot, lake_table)
    spread = lax.all_to_all(
        spread.reshape(RUNS, 1, LANES), both, split_axis=0, concat_axis=0, tiled=True
    ).reshape(RUNS, LANES)
    level, outflow = level_pool(spread, lake_phase, lake_area, lake_crest)
    return (new_moisture, surface, level, outflow)


def solution(mesh):
    blocks = P(("row", "col"))
    layers = P(None, ("row", "col"))
    cells = P("row", "col")
    in_specs = (layers, layers, blocks, layers, blocks) + (cells,) * 4 + (blocks,) * 4
    out_specs = (layers, cells, blocks, blocks)
    return jax.shard_map(body, mesh=mesh, in_specs=in_specs, out_specs=out_specs, check_vma=False)
```

time: 130 us -> 90.9 us (0.70)
  local copies, waits for them, and re-layouts: 30 us -> 2.6 us
  blocking collectives: 0 us -> 17.2 us
  starting transfers between devices: 33.7 us -> 18.7 us
  Pallas kernels: 44.8 us -> 37.5 us
  waiting for transfers between devices: 17.8 us -> 13 us
  other arithmetic: 2.08 us -> 0.59 us
    unnamed x58 -> x10, local copies, waits for them, and re-layouts: 24 us -> 1.85 us
    all_to_all x0 -> x1, blocking collectives: none -> 17.2 us  [body(): lax.all_to_all(spread.reshape(RUNS, 1, LANES), both, split_axis=0, concat...]
    pallas_call x1, Pallas kernels: 24.7 us -> 10.8 us  [route(): pl.pallas_call(route_kernel, out_shape=(jax.ShapeDtypeStruct(lake_slot.sh...]
    all_to_all x1 -> x0, starting transfers between devices: 13.1 us -> none  [body(): lax.all_to_all(spread.reshape(RUNS, 1, LANES), both, split_axis=0, concat...]
    all_to_all x1, waiting for transfers between devices: 0.88 us -> 10.5 us  [body(): lax.all_to_all(payload.reshape(RUNS, 1, RUN_ROWS * LANES), both, split_ax...]
    all_to_all x1 -> x0, waiting for transfers between devices: 8.73 us -> none  [body(): lax.all_to_all(spread.reshape(RUNS, 1, LANES), both, split_axis=0, concat...]
    ppermute x4 -> x2, starting transfers between devices: 8.45 us -> 3.53 us  [the longest x1 2.46 us: body(): left = lax.ppermute(cols[8:16], 'col', ring('col', 1))]
    pallas_call x2, Pallas kernels: 7.65 us -> 12.3 us  [the longest x1 8.37 us: place(): pl.pallas_call(place_kernel, out_shape=(jax.ShapeDtypeStruct(slabs, F32),...]
  transfers between devices with their start and end apart: 8 -> 5, of which waited for: 5 -> 3; matrix products, arithmetic and copies ran while one was open for 6% -> 1% of each run, Pallas kernels for 3% -> 11%
where the time goes in v1:
time: 90.9 us; the launch traced here: 90.3 us
  Pallas kernels  37.5 us (41%)
  starting transfers between devices  18.7 us (21%)
  blocking collectives  17.2 us (19%)
  waiting for transfers between devices  13 us (14%)
  local copies, waits for them, and re-layouts  2.6 us (3%)
    all_to_all x1, blocking collectives, body(): lax.all_to_all(spread.reshape(RUNS, 1, LANES), both, split_axis=0, concat...  17.2 us
    all_to_all x1, starting transfers between devices, body(): lax.all_to_all(payload.reshape(RUNS, 1, RUN_ROWS * LANES), both, split_ax...  11.5 us
    pallas_call x1, Pallas kernels, route(): pl.pallas_call(route_kernel, out_shape=(jax.ShapeDtypeStruct(lake_slot.sh...  10.8 us
    all_to_all x1, waiting for transfers between devices, body(): lax.all_to_all(payload.reshape(RUNS, 1, RUN_ROWS * LANES), both, split_ax...  10.5 us
    pallas_call x1, Pallas kernels, place(): pl.pallas_call(place_kernel, out_shape=(jax.ShapeDtypeStruct(slabs, F32),...  8.37 us
    pallas_call x1, Pallas kernels, land_payload(): pl.pallas_call(send_kernel, out_shape=jax.ShapeDtypeStruct((RUNS * RUN_RO...  7.2 us
    pallas_call x1, Pallas kernels, statics(): pl.pallas_call(static_kernel, out_shape=(jax.ShapeDtypeStruct(slabs, F32)...  5.73 us
    pallas_call x1, Pallas kernels, rim(): pl.pallas_call(rim_kernel, out_shape=(jax.ShapeDtypeStruct((16, 640), F32...  3.97 us
  transfers between devices with their start and end apart: 5, of which 3 were waited for; matrix products, arithmetic and copies ran while one was open for 1% of the time, Pallas kernels for 11%

profile of v1, /device:TPU:1, one launch (start us, length us, event | category | flops | bytes accessed | tf_op | source)
XLA Modules:
  0.0 90.3 jit_solution(3965962020933171988)
XLA Ops:
  0.6 7.2 %land.1 = f32[3328,128]{1,0:T(8,128)} custom-call(s32[4096]{0:T(1024)} %tile_hbm.1, f32[4,4096]{1,0:T(4,128)} %moisture_ref, f32[4,4096]{1,0:T(4,128)} %conduct_ref.1, f32[1,4096]{1,0:T(1,128)} %bitcast.20, f32[100,4096]{1,0:T(8,128)} %weights_hbm.1), custom_call_target="tpu_custom_call" | custom-call | tf_op jit(solution)/shard_map/land/pallas_call | solution.py:167
  7.8 11.5 %all-to-all-start = ((f32[128,1,3328]{2,1,0:T(1,128)}), f32[128,1,3328]{2,1,0:T(1,128)S(1)}, u32[]{:S(2)}, u32[]{:S(2)}) async-start(f32[128,1,3328]{2,1,0:T(1,128)} %bitcast.18), calls=%async_computation | async-start | bytes 3407872 | tf_op jit(solution)/shard_map/all_to_all | solution.py:716
  19.3 4.0 %rim.1 = (f32[16,640]{1,0:T(8,128)}, f32[4,4096]{1,0:T(4,128)}) custom-call(f32[4,4096]{1,0:T(4,128)} %moisture_ref, f32[4,4096]{1,0:T(4,128)} %conduct_ref.1, f32[1,4096]{1,0:T(1,128)} %bitcast.21, f32[640,640]{1,0:T(8,128)} %rate_hbm.1, s32[640,640]{1,0:T(8,128)} %code_hbm.1, s32[640,640]{1,0:T(8,128)} %slot_hbm.2, f32[640,640]{1,0:T(8,128)} %head_hbm.1), custom_call_target="tpu_custom_call" | custom-call | tf_op jit(solution)/shard_map/rim/pallas_call | solution.py:382
  23.3 0.8 fusion
  24.1 1.1 %collective-permute-start.1 = (f32[8,640]{1,0:T(8,128)S(1)}, f32[8,640]{1,0:T(8,128)S(1)}, u32[]{:S(2)}, u32[]{:S(2)}) collective-permute-start(f32[8,640]{1,0:T(8,128)S(1)} %get-tuple-element.48), channel_id=1, source_target_pairs={{0,15},{1,0},{2,1},{3,2},{4,3},{5,4},{6,5},{7,6},{8,7},{9,8},{10,9... | collective-permute-start | bytes 61448 | tf_op jit(solution)/shard_map/ppermute | solution.py:721
  25.1 2.5 %collective-permute-start = (f32[8,640]{1,0:T(8,128)S(1)}, f32[8,640]{1,0:T(8,128)S(1)}, u32[]{:S(2)}, u32[]{:S(2)}) collective-permute-start(f32[8,640]{1,0:T(8,128)S(1)} %get-tuple-element.49), channel_id=1, source_target_pairs={{0,1},{1,2},{2,3},{3,4},{4,5},{5,6},{6,7},{7,8},{8,9},{9,10},{10,1... | collective-permute-start | bytes 61448 | tf_op jit(solution)/shard_map/ppermute | solution.py:720
  27.6 0.6 add_convert_fusion.edge_ref
  28.2 5.7 %static.1 = (f32[5,672,128]{2,1,0:T(8,128)}, s32[5,672,128]{2,1,0:T(8,128)}, s32[8,128]{1,0:T(8,128)}, f32[8,768]{1,0:T(8,128)}, f32[8,768]{1,0:T(8,128)}) custom-call(f32[640,640]{1,0:T(8,128)} %rate_hbm.1, s32[640,640]{1,0:T(8,128)} %code_hbm.1, s32[640,640]{1,0:T(8,128)} %slot_hbm.2), custom_call_target="tpu_custom_call" | custom-call | tf_op jit(solution)/shard_map/static/pallas_call | solution.py:468
  33.9 1.1 %collective-permute-done.1.right_ref = f32[8,640]{1,0:T(8,128)S(1)} collective-permute-done((f32[8,640]{1,0:T(8,128)S(1)}, f32[8,640]{1,0:T(8,128)S(1)}, u32[]{:S(2)}, u32[]{:S(2)}) %collective-permute-start.1) | collective-permute-done | bytes 20512 | tf_op jit(solution)/shard_map/ppermute | solution.py:721
  35.0 0.0 copy-start.3
  35.0 0.0 collective-permute-done.left_ref
  35.0 0.0 copy-start.4
  35.0 10.5 %all-to-all-done = f32[128,1,3328]{2,1,0:T(1,128)S(1)} async-done(((f32[128,1,3328]{2,1,0:T(1,128)}), f32[128,1,3328]{2,1,0:T(1,128)S(1)}, u32[]{:S(2)}, u32[]{:S(2)}) %all-to-all-start) | async-done | bytes 1703968 | tf_op jit(solution)/shard_map/all_to_all | solution.py:716
  45.5 0.0 copy-start
  45.5 0.0 copy-done.3
  45.5 0.0 copy-done.4
  45.5 1.2 %copy-done = f32[128,1,3328]{2,1,0:T(1,128)} copy-done((f32[128,1,3328]{2,1,0:T(1,128)}, f32[128,1,3328]{2,1,0:T(1,128)S(1)}, u32[]{:S(2)}) %copy-start) | copy-done | bytes 1703960
  46.8 8.4 %place.1 = (f32[6,672,128]{2,1,0:T(8,128)}, f32[640,128]{1,0:T(8,128)}, s32[640,128]{1,0:T(8,128)}, f32[8,768]{1,0:T(8,128)}, f32[8,768]{1,0:T(8,128)}) custom-call(s32[4]{0:T(128)} %add_convert_fusion.edge_ref, f32[8,640]{1,0:T(8,128)} %copy-done.4, f32[8,640]{1,0:T(8,128)} %copy-done.3, f32[8,768]{1,0:T(8,128)} %get-tuple-element.34.top_in, ...), custom_call_target="tpu_custom_call" | custom-call | tf_op jit(solution)/shard_map/place/pallas_call | solution.py:308
  55.1 0.1 collective-permute-start.2
  55.2 3.6 %collective-permute-start.3 = (f32[8,768]{1,0:T(8,128)}, f32[8,768]{1,0:T(8,128)S(1)}, u32[]{:S(2)}, u32[]{:S(2)}) collective-permute-start(f32[8,768]{1,0:T(8,128)} %get-tuple-element.38), channel_id=1, source_target_pairs={{0,112},{16,0},{32,16},{48,32},{64,48},{80,64},{96,80},{112,96},{1... | collective-permute-start | bytes 73736 | tf_op jit(solution)/shard_map/ppermute | solution.py:725
  58.8 1.4 %collective-permute-done.2.up_ref = f32[8,768]{1,0:T(8,128)S(1)} collective-permute-done((f32[8,768]{1,0:T(8,128)}, f32[8,768]{1,0:T(8,128)S(1)}, u32[]{:S(2)}, u32[]{:S(2)}) %collective-permute-start.2) | collective-permute-done | bytes 24608 | tf_op jit(solution)/shard_map/ppermute | solution.py:724
  60.2 0.0 copy-start.1
  60.2 0.0 collective-permute-done.3.down_ref
  60.2 0.0 copy-start.2
  60.2 0.6 copy-done.1
  60.8 0.0 copy-done.2
  60.8 10.8 %route.1 = (f32[640,640]{1,0:T(8,128)}, f32[128,128]{1,0:T(8,128)}) custom-call(s32[4]{0:T(128)} %add_convert_fusion.edge_ref, s32[8,128]{1,0:T(8,128)} %get-tuple-element.32.ranges, f32[8,768]{1,0:T(8,128)} %copy-done.1, f32[8,768]{1,0:T(8,128)} %copy-done.2, s32[1,64]{1,0:T(1,128)} %bitcast.26, f32[6,672,128]{2,1,0:T(8,128)} %get-tuple-element.39.depth_hbm, ...), custom_call_target="tpu_custom_call" | custom-call | tf_op jit(solution)/shard_map/route/pallas_call | solution.py:658
  71.7 17.2 %all_to_all.10 = f32[128,1,128]{2,1,0:T(1,128)} all-to-all(f32[128,1,128]{2,1,0:T(1,128)} %bitcast.22), channel_id=1, replica_groups=mesh['row'=8,'col'=16] {'row','col'}, dimensions={0} | all-to-all | bytes 131072 | tf_op jit(solution)/shard_map/all_to_all | solution.py:727
  88.9 1.4 %pool.1 = (f32[1,64]{1,0:T(1,128)}, f32[1,64]{1,0:T(1,128)}) custom-call(f32[128,128]{1,0:T(8,128)} %bitcast.19, f32[1,64]{1,0:T(1,128)} %bitcast.23, f32[1,64]{1,0:T(1,128)} %bitcast.24, f32[1,64]{1,0:T(1,128)} %bitcast.25), custom_call_target="tpu_custom_call" | custom-call | tf_op jit(solution)/shard_map/pool/pallas_call | solution.py:692
Async XLA Ops:
  7.8 37.7 %all-to-all-start = ((f32[128,1,3328]{2,1,0:T(1,128)}), f32[128,1,3328]{2,1,0:T(1,128)S(1)}, u32[]{:S(2)}, u32[]{:S(2)}) async-start(f32[128,1,3328]{2,1,0:T(1,128)} %bitcast.18), calls=%async_computation | async-start | bytes 3407872 | tf_op jit(solution)/shard_map/all_to_all | solution.py:716
  24.1 11.0 %collective-permute-start.1 = (f32[8,640]{1,0:T(8,128)S(1)}, f32[8,640]{1,0:T(8,128)S(1)}, u32[]{:S(2)}, u32[]{:S(2)}) collective-permute-start(f32[8,640]{1,0:T(8,128)S(1)} %get-tuple-element.48), channel_id=1, source_target_pairs={{0,15},{1,0},{2,1},{3,2},{4,3},{5,4},{6,5},{7,6},{8,7},{9,8},{10,9... | collective-permute-start | bytes 61448 | tf_op jit(solution)/shard_map/ppermute | solution.py:721
  25.1 9.9 %collective-permute-start = (f32[8,640]{1,0:T(8,128)S(1)}, f32[8,640]{1,0:T(8,128)S(1)}, u32[]{:S(2)}, u32[]{:S(2)}) collective-permute-start(f32[8,640]{1,0:T(8,128)S(1)} %get-tuple-element.49), channel_id=1, source_target_pairs={{0,1},{1,2},{2,3},{3,4},{4,5},{5,6},{6,7},{7,8},{8,9},{9,10},{10,1... | collective-permute-start | bytes 61448 | tf_op jit(solution)/shard_map/ppermute | solution.py:720
  35.0 10.5 %copy-start.3 = (f32[8,640]{1,0:T(8,128)}, f32[8,640]{1,0:T(8,128)S(1)}, u32[]{:S(2)}) copy-start(f32[8,640]{1,0:T(8,128)S(1)} %collective-permute-done.1.right_ref) | copy-start | bytes 61444
  35.0 10.5 %copy-start.4 = (f32[8,640]{1,0:T(8,128)}, f32[8,640]{1,0:T(8,128)S(1)}, u32[]{:S(2)}) copy-start(f32[8,640]{1,0:T(8,128)S(1)} %collective-permute-done.left_ref) | copy-start | bytes 61444
  45.5 1.2 %copy-start = (f32[128,1,3328]{2,1,0:T(1,128)}, f32[128,1,3328]{2,1,0:T(1,128)S(1)}, u32[]{:S(2)}) copy-start(f32[128,1,3328]{2,1,0:T(1,128)S(1)} %all-to-all-done) | copy-start | bytes 5111812
  55.1 5.1 %collective-permute-start.2 = (f32[8,768]{1,0:T(8,128)}, f32[8,768]{1,0:T(8,128)S(1)}, u32[]{:S(2)}, u32[]{:S(2)}) collective-permute-start(f32[8,768]{1,0:T(8,128)} %get-tuple-element.37), channel_id=1, source_target_pairs={{0,16},{16,32},{32,48},{48,64},{64,80},{80,96},{96,112},{112,0},{1... | collective-permute-start | bytes 73736 | tf_op jit(solution)/shard_map/ppermute | solution.py:724
  55.2 5.0 %collective-permute-start.3 = (f32[8,768]{1,0:T(8,128)}, f32[8,768]{1,0:T(8,128)S(1)}, u32[]{:S(2)}, u32[]{:S(2)}) collective-permute-start(f32[8,768]{1,0:T(8,128)} %get-tuple-element.38), channel_id=1, source_target_pairs={{0,112},{16,0},{32,16},{48,32},{64,48},{80,64},{96,80},{112,96},{1... | collective-permute-start | bytes 73736 | tf_op jit(solution)/shard_map/ppermute | solution.py:725
  60.2 0.6 copy-start.1
  60.2 0.6 copy-start.2

commit v2 on v1

--- a/solution.py
+++ b/solution.py
@@ -1,6 +1,5 @@
 import jax
 import jax.numpy as jnp
-import numpy as np
 from jax import lax
 from jax.experimental import pallas as pl
 from jax.experimental.pallas import tpu as pltpu
@@ -25,8 +24,8 @@
 SMEM = pl.BlockSpec(memory_space=pltpu.SMEM)
 
 
-def params(mebibytes=60):
-    return pltpu.CompilerParams(vmem_limit_bytes=mebibytes * 1024 * 1024)
+def params(limit=60 * 1024 * 1024):
+    return pltpu.CompilerParams(vmem_limit_bytes=limit)
 
 
 def lanes_of(shape):
@@ -58,8 +57,8 @@
     return [(i, (i + step) % count) for i in range(count)]
 
 
-def dot_select(value, picks):
-    return sum(jnp.dot(part, picks, preferred_element_type=F32) for part in split3(value))
+def dot_select(value, picks, parts=3):
+    return sum(jnp.dot(part, picks, preferred_element_type=F32) for part in split3(value)[:parts])
 
 
 def quarter_transpose(arrays, quarter):
@@ -115,7 +114,6 @@
         rain = rain_ref[0:1, pl.ds(start, LANES)]
         capacity = 10.0 * conduct * (1.5 - moisture / POROSITY)
         runoff = rain - rain * capacity / (rain + capacity)
-        fetch(i).wait()
         parts = [slab_ref[i, pl.ds(b, AGG, stride=AGG), :] for b in range(AGG)]
         total = sum(parts[1:], parts[0])
         mean = jnp.sum(total, axis=0, keepdims=True) * 0.01
@@ -129,24 +127,32 @@
         )
         for r in range(4):
             tile = tile_ref[(4 * i + r) * 32]
-            tiles = jnp.where(lane == 32 * r + i, tile, tiles)
+            tiles = jnp.where(lane == (((0, 63, 64, 127)[r] + 2 * i) & 127), tile, tiles)
             for offset, length, outs in groups:
                 out_ref[pl.ds(tile * RUN_ROWS + offset, length), :] = outs[r]
-        place = lane & 63
+        place = ((lane & 63) == 2 * i) | ((lane & 63) == ((2 * i - 1) & 63))
         new_edges = []
         for b in range(2):
-            left = pltpu.roll(parts[b], i, 1)
-            right = pltpu.roll(parts[8 + b], i + 97, 1)
-            edge = jnp.where(place == i, left, edges[b])
-            new_edges.append(jnp.where(place == i + 32, right, edge))
+            both = jnp.where((lane & 1) == 0, parts[b], parts[8 + b])
+            new_edges.append(jnp.where(place, pltpu.roll(both, 2 * i, 1), edges[b]))
         return tuple(new_edges), tiles
 
     zeros = jnp.zeros((AGG, LANES), F32)
-    edges, tiles = lax.fori_loop(0, count, step, ((zeros, zeros), jnp.zeros((1, LANES), jnp.int32)))
+    state = ((zeros, zeros), jnp.zeros((1, LANES), jnp.int32))
+    group = 8
+
+    def eight(n, carry):
+        for j in range(group):
+            fetch(n * group + j).wait()
+        return lax.fori_loop(0, group, lambda j, inner: step(n * group + j, inner), carry, unroll=group)
+
+    edges, tiles = lax.fori_loop(0, count // group, eight, state)
     edge_ref[...] = jnp.zeros((LANES, LANES), F32)
     edge_ref[0:AGG, :] = edges[0]
     edge_ref[16 : 16 + AGG, :] = edges[1]
-    edge_ref[15:16, :] = (4 * (lane & 31) + (lane >> 5)).astype(F32)
+    first = 2 * lane - jnp.where(lane < 64, 0, 126)
+    second = jnp.where(lane < 63, 2 * lane + 5, jnp.where(lane == 127, 3, 2 * lane - 125))
+    edge_ref[15:16, :] = jnp.where((lane & 1) == 0, first, second).astype(F32)
     by_run = edge_ref[...].T
     square = (LANES, LANES)
     here = (rows_of(square) == tiles).astype(F32).astype(BF16)
@@ -184,67 +190,28 @@
 
 
 def spread_columns():
-    picks = np.zeros((SLABS * LANES, 640), np.float32)
-    for half in range(2):
-        for j in range(3):
-            for k in range(4 if j < 2 else 2):
-                for i in range(32):
-                    picks[(half * 3 + j) * LANES + 32 * k + i, (half * 32 + i) * AGG + 4 * j + k] = 1.0
-    return picks
+    column = lanes_of((1, 640))
+    block = (column * 6554) >> 16
+    cell = column - AGG * block
+    half = block >> 5
+    quarter = jnp.where(cell < 8, cell & 3, cell - 8)
+    source = (half * 3 + (cell >> 2)) * LANES + 32 * quarter + (block & 31)
+    return (rows_of((SLABS * LANES, 640)) == source).astype(F32).astype(BF16)
 
 
 def place_kernel(
-    edge_ref, left_ref, right_ref, top_in, bottom_in, pay_hbm, head_hbm, picks_hbm,
-    depth_hbm, rate_hbm, code_hbm, top_ref, bottom_ref,
-    pay_ref, head_ref, picks_ref, depth_ref, rate_ref, code_ref, turn_ref, cells_ref, tag_ref, tags, sems,
+    top_in, bottom_in, picks_ref, pay_ref, depth_hbm, top_ref, bottom_ref,
+    depth_ref, cells_ref, tag_ref, tags, sems,
 ):
-    fetches = [
-        pltpu.make_async_copy(source, into, sems.at[n])
-        for n, (source, into) in enumerate(((pay_hbm, pay_ref), (picks_hbm, picks_ref), (head_hbm, head_ref)))
-    ]
-    for copy in fetches:
-        copy.start()
-    top_ref[...] = top_in[...]
-    bottom_ref[...] = bottom_in[...]
-    turn_ref[...] = jnp.zeros(turn_ref.shape, F32)
-    turn_ref[0:8, :] = right_ref[...]
-    turn_ref[8:16, :] = left_ref[...]
-    turned = turn_ref[...].T
-    tall = (640, LANES)
-    lane = lanes_of(tall)
-    rightmost = lane < 2
-    leftmost = lane >= 126
-
-    def slab(n):
-        right = pltpu.roll(turned, LANES - 2 * n, 1) if n else turned
-        left = pltpu.roll(turned, 118 - 2 * n, 1)
-        return jnp.where(rightmost, right, jnp.where(leftmost, left, 0.0))
-
-    first_col, last_col = edge_ref[2] == 1, edge_ref[3] == 1
-    inside = (rightmost & jnp.logical_not(last_col)) | (leftmost & jnp.logical_not(first_col))
-    side_rate = slab(0)
-    side_code = jnp.where(inside, slab(1), -1.0)
-    side_lake = slab(2)
-    side_head = slab(3)
-    rate_ref[...] = signed(side_rate, side_lake > 0.5)
-    code_ref[...] = side_code.astype(jnp.int32)
-    stores = [
-        pltpu.make_async_copy(source, into, sems.at[n + 3])
-        for n, (source, into) in enumerate(((rate_ref, rate_hbm), (code_ref, code_hbm)))
-    ]
-    for copy in stores:
-        copy.start()
-    for ref, rows in ((top_ref, slice(0, 2)), (bottom_ref, slice(638, 640))):
-        ref[2:4, 640:768] = side_rate[rows]
-        ref[4:6, 640:768] = side_code[rows]
-        ref[6:8, 640:768] = side_lake[rows]
-
-    fetches[0].wait()
     arrived = pay_ref[pl.ds(25, RUNS, stride=RUN_ROWS), :]
     by_lane = arrived.T
     tag_ref[...] = jnp.broadcast_to(by_lane[127:128, :].astype(jnp.int32), (8, LANES))
-    copy = pltpu.make_async_copy(tag_ref, tags, sems.at[5])
+    copy = pltpu.make_async_copy(tag_ref, tags, sems.at[4])
     copy.start()
+    top_ref[...] = top_in[...]
+    bottom_ref[...] = bottom_in[...]
+    tall = (640, LANES)
+    lane = lanes_of(tall)
     row = rows_of(tall)
     block = (row * 6554) >> 16
     left = (by_lane[15:16, :].astype(jnp.int32) == 2 * block + 1).astype(F32).astype(BF16)
@@ -258,10 +225,11 @@
     group = source >> 4
     target = jnp.where(group < 2, 126, 0) + (group & 1)
     fold = (((source & 15) < AGG) & (group < 4) & (target == wide)).astype(F32).astype(BF16)
-    depth = dot_select(strips, fold) + side_head
+    depth = dot_select(strips, fold)
     depth_ref[SLABS - 1, FIRST : FIRST + 640, :] = depth
-    top_ref[0:2, 640:768] = depth[0:2]
-    bottom_ref[0:2, 640:768] = depth[638:640]
+    top_ref[0:2, 640:768] += depth[0:2]
+    bottom_ref[0:2, 640:768] += depth[638:640]
+    picks = picks_ref[...]
     copy.wait()
 
     def settle(s, carry):
@@ -277,61 +245,45 @@
         return carry
 
     lax.fori_loop(0, RUNS, settle, 0, unroll=16)
-    for copy in fetches[1:]:
-        copy.wait()
-    picks = picks_ref[...]
     chunk = 160
+    stores = []
     for m in range(0, 640, chunk):
         cells = jnp.concatenate([cells_ref[c, m : m + chunk, :] for c in range(SLABS)], axis=1)
-        laid = dot_select(cells, picks)
+        laid = dot_select(cells, picks, 2)
         for c in range(SLABS - 1):
             columns = slice(c * LANES, (c + 1) * LANES)
-            depth = laid[:, columns] + head_ref[m : m + chunk, columns]
+            depth = laid[:, columns]
             depth_ref[c, FIRST + m : FIRST + m + chunk, :] = depth
             if m == 0:
-                top_ref[0:2, columns] = depth[0:2]
+                top_ref[0:2, columns] += depth[0:2]
             if m == 640 - chunk:
-                bottom_ref[0:2, columns] = depth[chunk - 2 :]
+                bottom_ref[0:2, columns] += depth[chunk - 2 :]
         rows = pl.ds(FIRST + m, chunk)
-        store = pltpu.make_async_copy(depth_ref.at[:, rows, :], depth_hbm.at[:, rows, :], sems.at[6 + m // chunk])
+        store = pltpu.make_async_copy(depth_ref.at[:, rows, :], depth_hbm.at[:, rows, :], sems.at[m // chunk])
         store.start()
         stores.append(store)
     for store in stores:
         store.wait()
 
 
-def place(edges, left, right, top, bottom, payload, head):
-    picks = jnp.asarray(spread_columns(), BF16)
+def place(top, bottom, picks, payload):
     strip = jax.ShapeDtypeStruct((8, 768), F32)
     slabs = (SLABS, ROWS, LANES)
-    side = (640, LANES)
     return pl.pallas_call(
         place_kernel,
-        out_shape=(
-            jax.ShapeDtypeStruct(slabs, F32),
-            jax.ShapeDtypeStruct(side, F32),
-            jax.ShapeDtypeStruct(side, jnp.int32),
-            strip,
-            strip,
-        ),
-        in_specs=[SMEM] + [VMEM] * 4 + [HBM] * 3,
-        out_specs=(HBM, HBM, HBM, VMEM, VMEM),
+        out_shape=(jax.ShapeDtypeStruct(slabs, F32), strip, strip),
+        in_specs=[VMEM] * 4,
+        out_specs=(HBM, VMEM, VMEM),
         scratch_shapes=[
-            pltpu.VMEM(payload.shape, F32),
-            pltpu.VMEM(head.shape, F32),
-            pltpu.VMEM(picks.shape, BF16),
             pltpu.VMEM(slabs, F32),
-            pltpu.VMEM(side, F32),
-            pltpu.VMEM(side, jnp.int32),
-            pltpu.VMEM((LANES, 640), F32),
             pltpu.VMEM((SLABS, 640, LANES), F32),
             pltpu.VMEM((8, LANES), jnp.int32),
             pltpu.SMEM((8, LANES), jnp.int32),
-            pltpu.SemaphoreType.DMA((10,)),
+            pltpu.SemaphoreType.DMA((5,)),
         ],
-        compiler_params=params(),
+        compiler_params=params(52_500_000),
         name="place",
-    )(edges, left, right, top, bottom, payload, head, picks)
+    )(top, bottom, picks, payload)
 
 
 def rim_kernel(
@@ -398,20 +350,30 @@
 
 
 def static_kernel(
-    rate_hbm, code_hbm, slot_hbm, rates_hbm, codes_hbm, ranges_ref, top_ref, bottom_ref,
-    rate_ref, code_ref, slot_ref, rates_ref, codes_ref, bits_ref, sems,
+    rate_hbm, code_hbm, slot_hbm, head_hbm, rates_hbm, codes_hbm, ranges_ref, top_ref, bottom_ref, picks_ref,
+    rate_ref, code_ref, slot_ref, head_ref, rates_ref, codes_ref, bits_ref, sems,
 ):
     fetches = [
         pltpu.make_async_copy(source, into, sems.at[n])
-        for n, (source, into) in enumerate(((rate_hbm, rate_ref), (code_hbm, code_ref), (slot_hbm, slot_ref)))
+        for n, (source, into) in enumerate(
+            (
+                (rate_hbm, rate_ref),
+                (code_hbm, code_ref),
+                (slot_hbm, slot_ref),
+                (head_hbm.at[0:8, :], head_ref.at[0:8, :]),
+                (head_hbm.at[632:640, :], head_ref.at[8:16, :]),
+            )
+        )
     ]
     for copy in fetches:
         copy.start()
+    picks_ref[...] = spread_columns()
     for copy in fetches:
         copy.wait()
-    for ref, base, part in ((top_ref, 0, slice(0, 2)), (bottom_ref, 632, slice(6, 8))):
+    for ref, base, part, head in ((top_ref, 0, slice(0, 2), slice(0, 2)), (bottom_ref, 632, slice(6, 8), slice(14, 16))):
         rows = slice(base, base + 8)
         ref[...] = jnp.zeros((8, 768), F32)
+        ref[0:2, 0:640] = head_ref[head, :]
         ref[2:4, 0:640] = rate_ref[rows, :][part]
         ref[4:6, 0:640] = code_ref[rows, :][part].astype(F32)
         ref[6:8, 0:640] = (slot_ref[rows, :][part] < LLOC).astype(F32)
@@ -438,7 +400,7 @@
 
     lax.fori_loop(0, 80, center, 0, unroll=8)
     stores = [
-        pltpu.make_async_copy(source, into, sems.at[3 + n])
+        pltpu.make_async_copy(source, into, sems.at[5 + n])
         for n, (source, into) in enumerate(((rates_ref, rates_hbm), (codes_ref, codes_hbm)))
     ]
     for copy in stores:
@@ -462,7 +424,7 @@
         copy.wait()
 
 
-def statics(rate, flow_code, lake_slot):
+def statics(rate, flow_code, lake_slot, head):
     slabs = (SLABS - 1, ROWS, LANES)
     strip = jax.ShapeDtypeStruct((8, 768), F32)
     return pl.pallas_call(
@@ -473,22 +435,73 @@
             jax.ShapeDtypeStruct((8, LANES), jnp.int32),
             strip,
             strip,
+            jax.ShapeDtypeStruct((SLABS * LANES, 640), BF16),
         ),
-        in_specs=[HBM, HBM, HBM],
-        out_specs=(HBM, HBM, VMEM, VMEM, VMEM),
+        in_specs=[HBM] * 4,
+        out_specs=(HBM, HBM, VMEM, VMEM, VMEM, VMEM),
         scratch_shapes=[
             pltpu.VMEM(rate.shape, F32),
             pltpu.VMEM(rate.shape, jnp.int32),
             pltpu.VMEM(rate.shape, jnp.int32),
+            pltpu.VMEM((16, 640), F32),
             pltpu.VMEM(slabs, F32),
             pltpu.VMEM(slabs, jnp.int32),
             pltpu.VMEM((2, 80, LANES), jnp.int32),
-            pltpu.SemaphoreType.DMA((5,)),
+            pltpu.SemaphoreType.DMA((7,)),
         ],
-        compiler_params=params(),
+        compiler_params=params(55000000),
         cost_estimate=pl.CostEstimate(flops=0, bytes_accessed=0, transcendentals=0),
         name="static",
-    )(rate, flow_code, lake_slot)
+    )(rate, flow_code, lake_slot, head)
+
+
+def sides_kernel(
+    edge_ref, left_ref, right_ref, top_in, bottom_in, rate_ref, code_ref, head_ref, top_ref, bottom_ref, turn_ref
+):
+    top_ref[...] = top_in[...]
+    bottom_ref[...] = bottom_in[...]
+    turn_ref[...] = jnp.zeros(turn_ref.shape, F32)
+    turn_ref[0:8, :] = right_ref[...]
+    turn_ref[8:16, :] = left_ref[...]
+    turned = turn_ref[...].T
+    lane = lanes_of((640, LANES))
+    rightmost = lane < 2
+    leftmost = lane >= 126
+
+    def slab(n):
+        right = pltpu.roll(turned, LANES - 2 * n, 1) if n else turned
+        left = pltpu.roll(turned, 118 - 2 * n, 1)
+        return jnp.where(rightmost, right, jnp.where(leftmost, left, 0.0))
+
+    first_col, last_col = edge_ref[2] == 1, edge_ref[3] == 1
+    inside = (rightmost & jnp.logical_not(last_col)) | (leftmost & jnp.logical_not(first_col))
+    rate = slab(0)
+    code = jnp.where(inside, slab(1), -1.0)
+    lake = slab(2)
+    rate_ref[...] = signed(rate, lake > 0.5)
+    code_ref[...] = code.astype(jnp.int32)
+    head = slab(3)
+    head_ref[...] = head
+    for ref, rows in ((top_ref, slice(0, 2)), (bottom_ref, slice(638, 640))):
+        ref[0:2, 640:768] = head[rows]
+        ref[2:4, 640:768] = rate[rows]
+        ref[4:6, 640:768] = code[rows]
+        ref[6:8, 640:768] = lake[rows]
+
+
+def sides(edges, left, right, top, bottom):
+    strip = jax.ShapeDtypeStruct(top.shape, F32)
+    side = jax.ShapeDtypeStruct((640, LANES), F32)
+    return pl.pallas_call(
+        sides_kernel,
+        out_shape=(side, jax.ShapeDtypeStruct(side.shape, jnp.int32), side, strip, strip),
+        in_specs=[SMEM] + [VMEM] * 4,
+        out_specs=(VMEM,) * 5,
+        scratch_shapes=[pltpu.VMEM((LANES, 640), F32)],
+        compiler_params=params(55_000_000),
+        cost_estimate=pl.CostEstimate(flops=0, bytes_accessed=0, transcendentals=0),
+        name="sides",
+    )(edges, left, right, top, bottom)
 
 
 def leave(depth, rate):
@@ -497,9 +510,9 @@
 
 
 def route_kernel(
-    edge_ref, ranges, up_ref, down_ref, table_ref, depth_hbm, rates_hbm, codes_hbm, rate_hbm, code_hbm, slot_hbm,
+    edge_ref, ranges, up_ref, down_ref, table_ref, depth_hbm, head_hbm, rates_hbm, codes_hbm, rate_hbm, code_hbm, side_hbm, slot_hbm,
     surface_hbm, spread_ref,
-    depth_ref, rates_ref, codes_ref, slot_ref, surface_ref, leave_ref, next_ref, lake_ref, sums_ref, sems,
+    depth_ref, head_ref, rates_ref, codes_ref, slot_ref, surface_ref, leave_ref, next_ref, lake_ref, sums_ref, sems,
 ):
     quarters = [(0, 176), (176, 160), (336, 160), (496, 176)]
 
@@ -507,6 +520,11 @@
         rows = pl.ds(*quarters[q])
         return pltpu.make_async_copy(source.at[:, rows, :], into.at[:, rows, :], sems.at[4 * n + q])
 
+    def heads_in(q):
+        rows = pl.ds(160 * q, 160)
+        return pltpu.make_async_copy(head_hbm.at[rows, :], head_ref.at[rows, 0:640], sems.at[17 + q])
+
+    heads = [heads_in(q) for q in range(4)]
     depths = [rows_in(depth_hbm, depth_ref, 0, q) for q in range(4)]
     middle, side, rows = pl.ds(0, SLABS - 1), SLABS - 1, pl.ds(FIRST, 640)
     rates = [rows_in(rates_hbm, rates_ref.at[middle], 1, q) for q in range(4)]
@@ -514,9 +532,12 @@
     codes = pltpu.make_async_copy(codes_hbm, codes_ref.at[middle], sems.at[8])
     side_code = pltpu.make_async_copy(code_hbm, codes_ref.at[side, rows, :], sems.at[16])
     slots = pltpu.make_async_copy(slot_hbm, slot_ref, sems.at[9])
+    side_head = pltpu.make_async_copy(side_hbm, head_ref.at[:, 640:768], sems.at[21])
     side_rate.start()
+    side_head.start()
     for q in range(4):
         depths[q].start()
+        heads[q].start()
         rates[q].start()
     codes.start()
     side_code.start()
@@ -526,8 +547,8 @@
     def at(g):
         return pl.ds(pl.multiple_of(g * 8, 8), 8)
 
-    def start(c, rows):
-        depth = depth_ref[c, rows, :]
+    def start(c, rows, head):
+        depth = depth_ref[c, rows, :] + head
         leaving = leave(depth, jnp.abs(rates_ref[c, rows, :]))
         leave_ref[c, rows, :] = leaving
         depth_ref[c, rows, :] = depth - leaving
@@ -538,12 +559,14 @@
     def first(g, carry):
         rows = at(g)
         for c in range(SLABS):
-            start(c, rows)
+            start(c, rows, head_ref[at(g - 2), c * LANES : (c + 1) * LANES])
         return carry
 
     side_rate.wait()
+    side_head.wait()
     for q, (begin, end) in enumerate(((2, 22), (22, 42), (42, 62), (62, 82))):
         depths[q].wait()
+        heads[q].wait()
         rates[q].wait()
         lax.fori_loop(begin, end, first, 0, unroll=2)
     codes.wait()
@@ -559,7 +582,7 @@
             depth_ref[c, two, :] = four[0:2]
             rates_ref[c, two, :] = jnp.where(four[6:8] > 0.5, -four[2:4], four[2:4])
             codes_ref[c, two, :] = jnp.where(outside, -1, four[4:6].astype(jnp.int32))
-        first(g, 0)
+            start(c, rows, 0.0)
 
     def gained(ref, g, slabs):
         east, middle, west = [], [], []
@@ -652,16 +675,17 @@
         store.wait()
 
 
-def route(edges, ranges, up, down, depth, rates, codes, rate, code, lake_slot, lake_table):
+def route(edges, ranges, up, down, depth, head, rates, codes, rate, code, side, lake_slot, lake_table):
     slabs = (SLABS, ROWS, LANES)
     slab = pltpu.VMEM(slabs, F32)
     return pl.pallas_call(
         route_kernel,
         out_shape=(jax.ShapeDtypeStruct(lake_slot.shape, F32), jax.ShapeDtypeStruct((LANES, LANES), F32)),
-        in_specs=[SMEM] * 2 + [VMEM] * 3 + [HBM] * 6,
+        in_specs=[SMEM] * 2 + [VMEM] * 3 + [HBM] * 8,
         out_specs=(HBM, VMEM),
         scratch_shapes=[
             slab,
+            pltpu.VMEM((640, 768), F32),
             slab,
             pltpu.VMEM(slabs, jnp.int32),
             pltpu.VMEM(lake_slot.shape, jnp.int32),
@@ -670,11 +694,11 @@
             slab,
             slab,
             pltpu.VMEM((8 * LLOC, LANES), F32),
-            pltpu.SemaphoreType.DMA((17,)),
+            pltpu.SemaphoreType.DMA((22,)),
         ],
-        compiler_params=params(),
+        compiler_params=params(55000000),
         name="route",
-    )(edges, ranges, up, down, lake_table.reshape(1, LLOC), depth, rates, codes, rate, code, lake_slot)
+    )(edges, ranges, up, down, lake_table.reshape(1, LLOC), depth, head, rates, codes, rate, code, side, lake_slot)
 
 
 def pool_kernel(spread_ref, phase_ref, area_ref, crest_ref, level_ref, outflow_ref):
@@ -719,11 +743,14 @@
     cols, new_moisture = rim(moisture, conduct, rainfall, rate, flow_code, lake_slot, head)
     left = lax.ppermute(cols[8:16], "col", ring("col", 1))
     right = lax.ppermute(cols[0:8], "col", ring("col", -1))
-    rates, codes, ranges, top, bottom = statics(rate, flow_code, lake_slot)
-    depth, side_rate, side_code, top, bottom = place(edges, left, right, top, bottom, arrived, head)
+    rates, codes, ranges, top, bottom, picks = statics(rate, flow_code, lake_slot, head)
+    side_rate, side_code, side_head, top, bottom = sides(edges, left, right, top, bottom)
+    depth, top, bottom = place(top, bottom, picks, arrived)
     up = lax.ppermute(bottom, "row", ring("row", 1))
     down = lax.ppermute(top, "row", ring("row", -1))
-    surface, spread = route(edges, ranges, up, down, depth, rates, codes, side_rate, side_code, lake_slot, lake_table)
+    surface, spread = route(
+        edges, ranges, up, down, depth, head, rates, codes, side_rate, side_code, side_head, lake_slot, lake_table
+    )
     spread = lax.all_to_all(
         spread.reshape(RUNS, 1, LANES), both, split_axis=0, concat_axis=0, tiled=True
     ).reshape(RUNS, LANES)

time: 90.9 us -> 82 us (0.902)
  Pallas kernels: 37.5 us -> 31.6 us
  waiting for transfers between devices: 13 us -> 11.8 us
  local copies, waits for them, and re-layouts: 2.6 us -> 1.48 us
    pallas_call x1, Pallas kernels: 8.37 us -> 4.88 us  [place(): pl.pallas_call(place_kernel, out_shape=(jax.ShapeDtypeStruct(slabs, F32),...]
    pallas_call x1, Pallas kernels: 7.2 us -> 4.27 us  [land_payload(): pl.pallas_call(send_kernel, out_shape=jax.ShapeDtypeStruct((RUNS * RUN_RO...]
    all_to_all x1, waiting for transfers between devices: 10.5 us -> 8.46 us  [body(): lax.all_to_all(payload.reshape(RUNS, 1, RUN_ROWS * LANES), both, split_ax...]
    pallas_call x0 -> x1, Pallas kernels: none -> 1.3 us  [sides(): pl.pallas_call(sides_kernel, out_shape=(side, jax.ShapeDtypeStruct(side.s...]
    unnamed x10 -> x6, local copies, waits for them, and re-layouts: 1.85 us -> 0.73 us
    ppermute x1, waiting for transfers between devices: 1.11 us -> 2.12 us  [body(): right = lax.ppermute(cols[0:8], 'col', ring('col', -1))]
  transfers between devices with their start and end apart: 5 -> 5, of which waited for: 3 -> 3; matrix products, arithmetic and copies ran while one was open for 1% -> 1% of each run, Pallas kernels for 11% -> 13%
where the time goes in v2:
time: 82 us; the launch traced here: 81.6 us
  Pallas kernels  31.6 us (39%)
  starting transfers between devices  18.7 us (23%)
  blocking collectives  17.2 us (21%)
  waiting for transfers between devices  11.8 us (14%)
  local copies, waits for them, and re-layouts  1.48 us (2%)
    all_to_all x1, blocking collectives, body(): lax.all_to_all(spread.reshape(RUNS, 1, LANES), both, split_axis=0, concat...  17.2 us
    all_to_all x1, starting transfers between devices, body(): lax.all_to_all(payload.reshape(RUNS, 1, RUN_ROWS * LANES), both, split_ax...  11.5 us
    pallas_call x1, Pallas kernels, route(): pl.pallas_call(route_kernel, out_shape=(jax.ShapeDtypeStruct(lake_slot.sh...  10.5 us
    all_to_all x1, waiting for transfers between devices, body(): lax.all_to_all(payload.reshape(RUNS, 1, RUN_ROWS * LANES), both, split_ax...  8.46 us
    pallas_call x1, Pallas kernels, statics(): pl.pallas_call(static_kernel, out_shape=(jax.ShapeDtypeStruct(slabs, F32)...  5.12 us
    pallas_call x1, Pallas kernels, place(): pl.pallas_call(place_kernel, out_shape=(jax.ShapeDtypeStruct(slabs, F32),...  4.88 us
    pallas_call x1, Pallas kernels, land_payload(): pl.pallas_call(send_kernel, out_shape=jax.ShapeDtypeStruct((RUNS * RUN_RO...  4.27 us
    pallas_call x1, Pallas kernels, rim(): pl.pallas_call(rim_kernel, out_shape=(jax.ShapeDtypeStruct((16, 640), F32...  4.07 us
  transfers between devices with their start and end apart: 5, of which 3 were waited for; matrix products, arithmetic and copies ran while one was open for 1% of the time, Pallas kernels for 13%

profile of v2, /device:TPU:1, one launch (start us, length us, event | category | flops | bytes accessed | tf_op | source)
XLA Modules:
  0.0 81.6 jit_solution(17313493193042486332)
XLA Ops:
  0.6 4.3 %land.1 = f32[3328,128]{1,0:T(8,128)} custom-call(s32[4096]{0:T(1024)} %tile_hbm.1, f32[4,4096]{1,0:T(4,128)} %moisture_ref, f32[4,4096]{1,0:T(4,128)} %conduct_ref.1, f32[1,4096]{1,0:T(1,128)} %bitcast.22, f32[100,4096]{1,0:T(8,128)} %weights_hbm.1), custom_call_target="tpu_custom_call" | custom-call | tf_op jit(solution)/shard_map/land/pallas_call | solution.py:173
  4.9 11.5 %all-to-all-start = ((f32[128,1,3328]{2,1,0:T(1,128)}), f32[128,1,3328]{2,1,0:T(1,128)S(1)}, u32[]{:S(2)}, u32[]{:S(2)}) async-start(f32[128,1,3328]{2,1,0:T(1,128)} %bitcast.20), calls=%async_computation | async-start | bytes 3407872 | tf_op jit(solution)/shard_map/all_to_all | solution.py:740
  16.4 4.1 %rim.1 = (f32[16,640]{1,0:T(8,128)}, f32[4,4096]{1,0:T(4,128)}) custom-call(f32[4,4096]{1,0:T(4,128)} %moisture_ref, f32[4,4096]{1,0:T(4,128)} %conduct_ref.1, f32[1,4096]{1,0:T(1,128)} %bitcast.23, f32[640,640]{1,0:T(8,128)} %rate_hbm.1, s32[640,640]{1,0:T(8,128)} %code_hbm.1, s32[640,640]{1,0:T(8,128)} %slot_hbm.2, f32[640,640]{1,0:T(8,128)} %head_hbm.2), custom_call_target="tpu_custom_call" | custom-call | tf_op jit(solution)/shard_map/rim/pallas_call | solution.py:334
  20.5 0.8 fusion
  21.3 1.1 %collective-permute-start.1 = (f32[8,640]{1,0:T(8,128)S(1)}, f32[8,640]{1,0:T(8,128)S(1)}, u32[]{:S(2)}, u32[]{:S(2)}) collective-permute-start(f32[8,640]{1,0:T(8,128)S(1)} %get-tuple-element.56), channel_id=1, source_target_pairs={{0,15},{1,0},{2,1},{3,2},{4,3},{5,4},{6,5},{7,6},{8,7},{9,8},{10,9... | collective-permute-start | bytes 61448 | tf_op jit(solution)/shard_map/ppermute | solution.py:745
  22.3 2.5 %collective-permute-start = (f32[8,640]{1,0:T(8,128)S(1)}, f32[8,640]{1,0:T(8,128)S(1)}, u32[]{:S(2)}, u32[]{:S(2)}) collective-permute-start(f32[8,640]{1,0:T(8,128)S(1)} %get-tuple-element.57), channel_id=1, source_target_pairs={{0,1},{1,2},{2,3},{3,4},{4,5},{5,6},{6,7},{7,8},{8,9},{9,10},{10,1... | collective-permute-start | bytes 61448 | tf_op jit(solution)/shard_map/ppermute | solution.py:744
  24.8 0.1 add_convert_fusion.edge_ref
  24.9 5.1 %static.1 = (f32[5,672,128]{2,1,0:T(8,128)}, s32[5,672,128]{2,1,0:T(8,128)}, s32[8,128]{1,0:T(8,128)S(1)}, f32[8,768]{1,0:T(8,128)S(1)}, f32[8,768]{1,0:T(8,128)S(1)}, /*index=5*/bf16[768,640]{1,0:T(8,128)(2,1)S(1)}) custom-call(f32[640,640]{1,0:T(8,128)} %rate_hbm.1, s32[640,640]{1,0:T(8,128)} %code_hbm.1, s32[640,640]{1,0:T(8,128)} %slot_hbm.2, ...), custom_call_target="tpu_custom_call" | custom-call | tf_op jit(solution)/shard_map/static/pallas_call | solution.py:430
  30.0 0.0 copy-start.2
  30.0 2.1 %collective-permute-done.1.right_ref = f32[8,640]{1,0:T(8,128)S(1)} collective-permute-done((f32[8,640]{1,0:T(8,128)S(1)}, f32[8,640]{1,0:T(8,128)S(1)}, u32[]{:S(2)}, u32[]{:S(2)}) %collective-permute-start.1) | collective-permute-done | bytes 20512 | tf_op jit(solution)/shard_map/ppermute | solution.py:745
  32.1 0.0 collective-permute-done.left_ref
  32.1 1.3 %sides.1 = (f32[640,128]{1,0:T(8,128)S(1)}, s32[640,128]{1,0:T(8,128)S(1)}, f32[640,128]{1,0:T(8,128)S(1)}, f32[8,768]{1,0:T(8,128)S(1)}, f32[8,768]{1,0:T(8,128)S(1)}) custom-call(s32[4]{0:T(128)S(1)} %add_convert_fusion.edge_ref, f32[8,640]{1,0:T(8,128)S(1)} %collective-permute-done.left_ref, f32[8,640]{1,0:T(8,128)S(1)} %collective-permute-done.1.right_ref, ...), custom_call_target="tpu_custom_call" | custom-call | tf_op jit(solution)/shard_map/sides/pallas_call | solution.py:495
  33.4 0.0 copy-start
  33.4 0.7 copy-done
  34.2 8.5 %all-to-all-done = f32[128,1,3328]{2,1,0:T(1,128)S(1)} async-done(((f32[128,1,3328]{2,1,0:T(1,128)}), f32[128,1,3328]{2,1,0:T(1,128)S(1)}, u32[]{:S(2)}, u32[]{:S(2)}) %all-to-all-start) | async-done | bytes 1703968 | tf_op jit(solution)/shard_map/all_to_all | solution.py:740
  42.6 0.0 copy-start.1
  42.6 4.9 %place.1 = (f32[6,672,128]{2,1,0:T(8,128)}, f32[8,768]{1,0:T(8,128)S(1)}, f32[8,768]{1,0:T(8,128)S(1)}) custom-call(f32[8,768]{1,0:T(8,128)S(1)} %get-tuple-element.40.top_in, f32[8,768]{1,0:T(8,128)S(1)} %get-tuple-element.41.bottom_in, bf16[768,640]{1,0:T(8,128)(2,1)S(1)} %get-tuple-element.42.picks_ref, f32[3328,128]{1,0:T(8,128)S(1)} %bitcast.17), custom_call_target="tpu_custom_call" | custom-call | tf_op jit(solution)/shard_map/place/pallas_call | solution.py:272
  47.5 0.1 collective-permute-start.2
  47.6 3.6 %collective-permute-start.3 = (f32[8,768]{1,0:T(8,128)S(1)}, f32[8,768]{1,0:T(8,128)S(1)}, u32[]{:S(2)}, u32[]{:S(2)}) collective-permute-start(f32[8,768]{1,0:T(8,128)S(1)} %get-tuple-element.45), channel_id=1, source_target_pairs={{0,112},{16,0},{32,16},{48,32},{64,48},{80,64},{96,80},{112,96},{1... | collective-permute-start | bytes 73736 | tf_op jit(solution)/shard_map/ppermute | solution.py:750
  51.1 1.2 %collective-permute-done.2.up_ref = f32[8,768]{1,0:T(8,128)S(1)} collective-permute-done((f32[8,768]{1,0:T(8,128)S(1)}, f32[8,768]{1,0:T(8,128)S(1)}, u32[]{:S(2)}, u32[]{:S(2)}) %collective-permute-start.2) | collective-permute-done | bytes 24608 | tf_op jit(solution)/shard_map/ppermute | solution.py:749
  52.4 0.0 collective-permute-done.3.down_ref
  52.4 0.0 copy-done.2
  52.4 0.0 copy-done.1
  52.4 10.5 %route.1 = (f32[640,640]{1,0:T(8,128)}, f32[128,128]{1,0:T(8,128)S(1)}) custom-call(s32[4]{0:T(128)S(1)} %add_convert_fusion.edge_ref, s32[8,128]{1,0:T(8,128)S(1)} %get-tuple-element.36.ranges, f32[8,768]{1,0:T(8,128)S(1)} %collective-permute-done.2.up_ref, f32[8,768]{1,0:T(8,128)S(1)} %collective-permute-done.3.down_ref, s32[1,64]{1,0:T(1,128)S(1)} %bitcast.19, ...), custom_call_target="tpu_custom_call" | custom-call | tf_op jit(solution)/shard_map/route/pallas_call | solution.py:681
  62.9 17.2 %all_to_all.10 = f32[128,1,128]{2,1,0:T(1,128)} all-to-all(f32[128,1,128]{2,1,0:T(1,128)S(1)} %bitcast.18), channel_id=1, replica_groups=mesh['row'=8,'col'=16] {'row','col'}, dimensions={0} | all-to-all | bytes 131072 | tf_op jit(solution)/shard_map/all_to_all | solution.py:754
  80.1 1.4 %pool.1 = (f32[1,64]{1,0:T(1,128)}, f32[1,64]{1,0:T(1,128)}) custom-call(f32[128,128]{1,0:T(8,128)} %bitcast.21, f32[1,64]{1,0:T(1,128)} %bitcast.24, f32[1,64]{1,0:T(1,128)} %bitcast.25, f32[1,64]{1,0:T(1,128)} %bitcast.26), custom_call_target="tpu_custom_call" | custom-call | tf_op jit(solution)/shard_map/pool/pallas_call | solution.py:716
Async XLA Ops:
  4.9 37.7 %all-to-all-start = ((f32[128,1,3328]{2,1,0:T(1,128)}), f32[128,1,3328]{2,1,0:T(1,128)S(1)}, u32[]{:S(2)}, u32[]{:S(2)}) async-start(f32[128,1,3328]{2,1,0:T(1,128)} %bitcast.20), calls=%async_computation | async-start | bytes 3407872 | tf_op jit(solution)/shard_map/all_to_all | solution.py:740
  21.3 10.9 %collective-permute-start.1 = (f32[8,640]{1,0:T(8,128)S(1)}, f32[8,640]{1,0:T(8,128)S(1)}, u32[]{:S(2)}, u32[]{:S(2)}) collective-permute-start(f32[8,640]{1,0:T(8,128)S(1)} %get-tuple-element.56), channel_id=1, source_target_pairs={{0,15},{1,0},{2,1},{3,2},{4,3},{5,4},{6,5},{7,6},{8,7},{9,8},{10,9... | collective-permute-start | bytes 61448 | tf_op jit(solution)/shard_map/ppermute | solution.py:745
  22.3 9.8 %collective-permute-start = (f32[8,640]{1,0:T(8,128)S(1)}, f32[8,640]{1,0:T(8,128)S(1)}, u32[]{:S(2)}, u32[]{:S(2)}) collective-permute-start(f32[8,640]{1,0:T(8,128)S(1)} %get-tuple-element.57), channel_id=1, source_target_pairs={{0,1},{1,2},{2,3},{3,4},{4,5},{5,6},{6,7},{7,8},{8,9},{9,10},{10,1... | collective-permute-start | bytes 61448 | tf_op jit(solution)/shard_map/ppermute | solution.py:744
  30.0 22.4 %copy-start.2 = (s32[64]{0:T(128)S(1)}, s32[64]{0:T(128)}, u32[]{:S(2)}) copy-start(s32[64]{0:T(128)} %param.22) | copy-start | bytes 772
  33.4 0.7 copy-start
  42.6 9.8 %copy-start.1 = (f32[640,128]{1,0:T(8,128)S(1)}, f32[640,128]{1,0:T(8,128)}, u32[]{:S(2)}) copy-start(f32[640,128]{1,0:T(8,128)} %copy-done) | copy-start | bytes 983044
  47.5 4.9 %collective-permute-start.2 = (f32[8,768]{1,0:T(8,128)S(1)}, f32[8,768]{1,0:T(8,128)S(1)}, u32[]{:S(2)}, u32[]{:S(2)}) collective-permute-start(f32[8,768]{1,0:T(8,128)S(1)} %get-tuple-element.44), channel_id=1, source_target_pairs={{0,16},{16,32},{32,48},{48,64},{64,80},{80,96},{96,112},{112,0},{1... | collective-permute-start | bytes 73736 | tf_op jit(solution)/shard_map/ppermute | solution.py:749
  47.6 4.8 %collective-permute-start.3 = (f32[8,768]{1,0:T(8,128)S(1)}, f32[8,768]{1,0:T(8,128)S(1)}, u32[]{:S(2)}, u32[]{:S(2)}) collective-permute-start(f32[8,768]{1,0:T(8,128)S(1)} %get-tuple-element.45), channel_id=1, source_target_pairs={{0,112},{16,0},{32,16},{48,32},{64,48},{80,64},{96,80},{112,96},{1... | collective-permute-start | bytes 73736 | tf_op jit(solution)/shard_map/ppermute | solution.py:750

commit v3 on v2

--- a/solution.py
+++ b/solution.py
@@ -50,6 +50,11 @@
 
 def signed(rate, lake):
     return jnp.where(lake, -rate, rate)
+
+
+def leave(depth, rate):
+    conveyance = rate * jnp.exp(jnp.log(depth) * (2.0 / 3.0))
+    return depth * conveyance / (1.0 + conveyance)
 
 
 def ring(axis, step):
@@ -504,85 +509,117 @@
     )(edges, left, right, top, bottom)
 
 
-def leave(depth, rate):
-    conveyance = rate * jnp.exp(jnp.log(depth) * (2.0 / 3.0))
-    return depth * conveyance / (1.0 + conveyance)
+def open_kernel(
+    depth_hbm, head_hbm, side_hbm, rates_hbm, rate_hbm, leave_hbm, stay_hbm,
+    depth_ref, head_ref, rates_ref, leave_ref, sems,
+):
+    middle, side, center = pl.ds(0, SLABS - 1), SLABS - 1, pl.ds(FIRST, 640)
+    fetches, stores = [], []
+    for q in range(4):
+        rows = pl.ds(FIRST + 160 * q, 160)
+        from_rows = pl.ds(160 * q, 160)
+        pairs = (
+            (depth_hbm.at[:, rows, :], depth_ref.at[:, rows, :]),
+            (rates_hbm.at[:, rows, :], rates_ref.at[middle, rows, :]),
+            (head_hbm.at[from_rows, :], head_ref.at[from_rows, 0:640]),
+        )
+        fetches.append([pltpu.make_async_copy(*pair, sems.at[3 * q + n]) for n, pair in enumerate(pairs)])
+        pairs = (
+            (leave_ref.at[:, rows, :], leave_hbm.at[:, rows, :]),
+            (depth_ref.at[:, rows, :], stay_hbm.at[:, rows, :]),
+        )
+        stores.append([pltpu.make_async_copy(*pair, sems.at[12 + 2 * q + n]) for n, pair in enumerate(pairs)])
+    narrow = [
+        pltpu.make_async_copy(rate_hbm, rates_ref.at[side, center, :], sems.at[20]),
+        pltpu.make_async_copy(side_hbm, head_ref.at[:, 640:768], sems.at[21]),
+    ]
+    for copy in narrow + [copy for group in fetches for copy in group]:
+        copy.start()
+    for copy in narrow:
+        copy.wait()
+
+    def step(g, carry):
+        rows = pl.ds(pl.multiple_of(g * 8, 8), 8)
+        from_rows = pl.ds(pl.multiple_of(g * 8 - FIRST, 8), 8)
+        for c in range(SLABS):
+            depth = depth_ref[c, rows, :] + head_ref[from_rows, c * LANES : (c + 1) * LANES]
+            leaving = leave(depth, jnp.abs(rates_ref[c, rows, :]))
+            leave_ref[c, rows, :] = leaving
+            depth_ref[c, rows, :] = depth - leaving
+        return carry
+
+    for q in range(4):
+        for copy in fetches[q]:
+            copy.wait()
+        lax.fori_loop(2 + 20 * q, 22 + 20 * q, step, 0, unroll=5)
+        for copy in stores[q]:
+            copy.start()
+    for group in stores:
+        for copy in group:
+            copy.wait()
+
+
+def opening(depth, head, side, rates, rate):
+    slab = pltpu.VMEM(depth.shape, F32)
+    return pl.pallas_call(
+        open_kernel,
+        out_shape=(jax.ShapeDtypeStruct(depth.shape, F32),) * 2,
+        in_specs=[HBM] * 5,
+        out_specs=(HBM, HBM),
+        scratch_shapes=[slab, pltpu.VMEM((640, 768), F32), slab, slab, pltpu.SemaphoreType.DMA((22,))],
+        compiler_params=params(55_000_000),
+        name="open",
+    )(depth, head, side, rates, rate)
 
 
 def route_kernel(
-    edge_ref, ranges, up_ref, down_ref, table_ref, depth_hbm, head_hbm, rates_hbm, codes_hbm, rate_hbm, code_hbm, side_hbm, slot_hbm,
+    edge_ref, ranges, up_ref, down_ref, table_ref, leave_hbm, stay_hbm, rates_hbm, codes_hbm, rate_hbm, code_hbm, slot_hbm,
     surface_hbm, spread_ref,
-    depth_ref, head_ref, rates_ref, codes_ref, slot_ref, surface_ref, leave_ref, next_ref, lake_ref, sums_ref, sems,
+    leave_ref, stay_ref, rates_ref, codes_ref, slot_ref, surface_ref, next_ref, lake_ref, sums_ref, sems,
 ):
-    quarters = [(0, 176), (176, 160), (336, 160), (496, 176)]
-
-    def rows_in(source, into, n, q):
-        rows = pl.ds(*quarters[q])
-        return pltpu.make_async_copy(source.at[:, rows, :], into.at[:, rows, :], sems.at[4 * n + q])
-
-    def heads_in(q):
-        rows = pl.ds(160 * q, 160)
-        return pltpu.make_async_copy(head_hbm.at[rows, :], head_ref.at[rows, 0:640], sems.at[17 + q])
-
-    heads = [heads_in(q) for q in range(4)]
-    depths = [rows_in(depth_hbm, depth_ref, 0, q) for q in range(4)]
-    middle, side, rows = pl.ds(0, SLABS - 1), SLABS - 1, pl.ds(FIRST, 640)
-    rates = [rows_in(rates_hbm, rates_ref.at[middle], 1, q) for q in range(4)]
-    side_rate = pltpu.make_async_copy(rate_hbm, rates_ref.at[side, rows, :], sems.at[15])
-    codes = pltpu.make_async_copy(codes_hbm, codes_ref.at[middle], sems.at[8])
-    side_code = pltpu.make_async_copy(code_hbm, codes_ref.at[side, rows, :], sems.at[16])
-    slots = pltpu.make_async_copy(slot_hbm, slot_ref, sems.at[9])
-    side_head = pltpu.make_async_copy(side_hbm, head_ref.at[:, 640:768], sems.at[21])
-    side_rate.start()
-    side_head.start()
+    middle, side, center = pl.ds(0, SLABS - 1), SLABS - 1, pl.ds(FIRST, 640)
+    pairs = (
+        (leave_hbm, leave_ref),
+        (codes_hbm, codes_ref.at[middle]),
+        (stay_hbm, stay_ref),
+        (rates_hbm, rates_ref.at[middle]),
+    )
+    quarters = []
     for q in range(4):
-        depths[q].start()
-        heads[q].start()
-        rates[q].start()
-    codes.start()
-    side_code.start()
-    slots.start()
+        rows = pl.ds(FIRST + 160 * q, 160)
+        quarters.append(
+            [
+                pltpu.make_async_copy(source.at[:, rows, :], into.at[:, rows, :], sems.at[4 * q + n])
+                for n, (source, into) in enumerate(pairs)
+            ]
+        )
+    narrow = [
+        pltpu.make_async_copy(code_hbm, codes_ref.at[side, center, :], sems.at[16]),
+        pltpu.make_async_copy(rate_hbm, rates_ref.at[side, center, :], sems.at[17]),
+    ]
+    slots = pltpu.make_async_copy(slot_hbm, slot_ref, sems.at[18])
+    for copy in quarters[0] + narrow + quarters[1] + quarters[2] + quarters[3] + [slots]:
+        copy.start()
     lane = lanes_of((8, LANES))
 
     def at(g):
         return pl.ds(pl.multiple_of(g * 8, 8), 8)
 
-    def start(c, rows, head):
-        depth = depth_ref[c, rows, :] + head
-        leaving = leave(depth, jnp.abs(rates_ref[c, rows, :]))
-        leave_ref[c, rows, :] = leaving
-        depth_ref[c, rows, :] = depth - leaving
-
     eight = (8, LANES)
-    rims = ((1, up_ref, 6, edge_ref[0] == 1), (82, down_ref, 0, edge_ref[1] == 1))
-
-    def first(g, carry):
-        rows = at(g)
-        for c in range(SLABS):
-            start(c, rows, head_ref[at(g - 2), c * LANES : (c + 1) * LANES])
-        return carry
-
-    side_rate.wait()
-    side_head.wait()
-    for q, (begin, end) in enumerate(((2, 22), (22, 42), (42, 62), (62, 82))):
-        depths[q].wait()
-        heads[q].wait()
-        rates[q].wait()
-        lax.fori_loop(begin, end, first, 0, unroll=2)
-    codes.wait()
-    side_code.wait()
-    for g, ref, offset, outside in rims:
+    for g, ref, offset, outside in ((1, up_ref, 6, edge_ref[0] == 1), (82, down_ref, 0, edge_ref[1] == 1)):
         rows = slice(g * 8, g * 8 + 8)
         two = slice(g * 8 + offset, g * 8 + offset + 2)
         for c in range(SLABS):
             four = ref[:, c * LANES : (c + 1) * LANES]
-            depth_ref[c, rows, :] = jnp.zeros(eight, F32)
             rates_ref[c, rows, :] = jnp.ones(eight, F32)
             codes_ref[c, rows, :] = jnp.full(eight, -1, jnp.int32)
-            depth_ref[c, two, :] = four[0:2]
-            rates_ref[c, two, :] = jnp.where(four[6:8] > 0.5, -four[2:4], four[2:4])
+            leave_ref[c, rows, :] = jnp.zeros(eight, F32)
+            stay_ref[c, rows, :] = jnp.zeros(eight, F32)
+            leaving = leave(four[0:2], four[2:4])
+            leave_ref[c, two, :] = leaving
+            stay_ref[c, two, :] = four[0:2] - leaving
+            rates_ref[c, two, :] = signed(four[2:4], four[6:8] > 0.5)
             codes_ref[c, two, :] = jnp.where(outside, -1, four[4:6].astype(jnp.int32))
-            start(c, rows, 0.0)
 
     def gained(ref, g, slabs):
         east, middle, west = [], [], []
@@ -611,16 +648,22 @@
         for c, gain in enumerate(gained(leave_ref, g, SLABS)):
             rate = rates_ref[c, rows, :]
             lake = rate < 0.0
-            depth = depth_ref[c, rows, :] + gain
+            depth = stay_ref[c, rows, :] + gain
             kept = jnp.where(lake, 0.0, depth)
             leaving = leave(kept, jnp.abs(rate))
             next_ref[c, rows, :] = leaving
-            depth_ref[c, rows, :] = kept - leaving
+            stay_ref[c, rows, :] = kept - leaving
             if c < SLABS - 1:
                 lake_ref[c, rows, :] = depth - kept
         return carry
 
-    lax.fori_loop(1, 81, second, 0, unroll=16)
+    for q in range(4):
+        for copy in quarters[q]:
+            copy.wait()
+        if q == 0:
+            for copy in narrow:
+                copy.wait()
+        lax.fori_loop(1 + 20 * q, 21 + 20 * q, second, 0, unroll=20)
     for g in (81, 82):
         second(g, 0)
 
@@ -628,7 +671,7 @@
         rows = at(g)
         out = at(g - 2)
         for c, gain in enumerate(gained(next_ref, g, SLABS - 1)):
-            depth = depth_ref[c, rows, :] + gain
+            depth = stay_ref[c, rows, :] + gain
             kept = jnp.where(rates_ref[c, rows, :] < 0.0, 0.0, depth)
             lake_ref[c, rows, :] += depth - kept
             surface_ref[out, c * LANES : (c + 1) * LANES] = kept
@@ -638,7 +681,7 @@
     for q in range(5):
         lax.fori_loop(2 + 16 * q, 18 + 16 * q, third, 0, unroll=16)
         rows = pl.ds(128 * q, 128)
-        store = pltpu.make_async_copy(surface_ref.at[rows, :], surface_hbm.at[rows, :], sems.at[10 + q])
+        store = pltpu.make_async_copy(surface_ref.at[rows, :], surface_hbm.at[rows, :], sems.at[19 + q])
         store.start()
         stores.append(store)
     slots.wait()
@@ -675,30 +718,29 @@
         store.wait()
 
 
-def route(edges, ranges, up, down, depth, head, rates, codes, rate, code, side, lake_slot, lake_table):
+def route(edges, ranges, up, down, leaving, stay, rates, codes, rate, code, lake_slot, lake_table):
     slabs = (SLABS, ROWS, LANES)
     slab = pltpu.VMEM(slabs, F32)
     return pl.pallas_call(
         route_kernel,
         out_shape=(jax.ShapeDtypeStruct(lake_slot.shape, F32), jax.ShapeDtypeStruct((LANES, LANES), F32)),
-        in_specs=[SMEM] * 2 + [VMEM] * 3 + [HBM] * 8,
+        in_specs=[SMEM] * 2 + [VMEM] * 3 + [HBM] * 7,
         out_specs=(HBM, VMEM),
         scratch_shapes=[
             slab,
-            pltpu.VMEM((640, 768), F32),
+            slab,
             slab,
             pltpu.VMEM(slabs, jnp.int32),
             pltpu.VMEM(lake_slot.shape, jnp.int32),
             pltpu.VMEM(lake_slot.shape, F32),
             slab,
             slab,
-            slab,
             pltpu.VMEM((8 * LLOC, LANES), F32),
-            pltpu.SemaphoreType.DMA((22,)),
+            pltpu.SemaphoreType.DMA((24,)),
         ],
-        compiler_params=params(55000000),
+        compiler_params=params(55_000_000),
         name="route",
-    )(edges, ranges, up, down, lake_table.reshape(1, LLOC), depth, head, rates, codes, rate, code, side, lake_slot)
+    )(edges, ranges, up, down, lake_table.reshape(1, LLOC), leaving, stay, rates, codes, rate, code, lake_slot)
 
 
 def pool_kernel(spread_ref, phase_ref, area_ref, crest_ref, level_ref, outflow_ref):
@@ -718,7 +760,7 @@
         out_shape=(row, row),
         in_specs=[VMEM] * 4,
         out_specs=(VMEM,) * 2,
-        compiler_params=params(),
+        compiler_params=params(50_000_000),
         name="pool",
     )(spread, *(value.reshape(1, LLOC) for value in (lake_phase, lake_area, lake_crest)))
     return level.reshape(LLOC), outflow.reshape(LLOC)
@@ -748,8 +790,9 @@
     depth, top, bottom = place(top, bottom, picks, arrived)
     up = lax.ppermute(bottom, "row", ring("row", 1))
     down = lax.ppermute(top, "row", ring("row", -1))
+    leaving, stay = opening(depth, head, side_head, rates, side_rate)
     surface, spread = route(
-        edges, ranges, up, down, depth, head, rates, codes, side_rate, side_code, side_head, lake_slot, lake_table
+        edges, ranges, up, down, leaving, stay, rates, codes, side_rate, side_code, lake_slot, lake_table
     )
     spread = lax.all_to_all(
         spread.reshape(RUNS, 1, LANES), both, split_axis=0, concat_axis=0, tiled=True

time: 82 us -> 79 us (0.963)
  blocking collectives: 17.2 us -> 14 us
  Pallas kernels: 31.6 us -> 32.9 us
  waiting for transfers between devices: 11.8 us -> 10.7 us
    pallas_call x0 -> x1, Pallas kernels: none -> 4.09 us  [opening(): pl.pallas_call(open_kernel, out_shape=(jax.ShapeDtypeStruct(depth.shape,...]
    all_to_all x1, blocking collectives: 17.2 us -> 14 us  [body(): lax.all_to_all(spread.reshape(RUNS, 1, LANES), both, split_axis=0, concat...]
    pallas_call x1, Pallas kernels: 10.5 us -> 8.68 us  [route(): pl.pallas_call(route_kernel, out_shape=(jax.ShapeDtypeStruct(lake_slot.sh...]
    ppermute x1, waiting for transfers between devices: 1.21 us -> 0.01 us  [body(): up = lax.ppermute(bottom, 'row', ring('row', 1))]
    pallas_call x1, Pallas kernels: 1.41 us -> 0.55 us  [level_pool(): pl.pallas_call(pool_kernel, out_shape=(row, row), in_specs=[VMEM] * 4, ou...]
  transfers between devices with their start and end apart: 5 -> 5, of which waited for: 3 -> 2; matrix products, arithmetic and copies ran while one was open for 1% -> 1% of each run, Pallas kernels for 13% -> 18%
where the time goes in v3:
time: 79 us; the launch traced here: 78.6 us
  Pallas kernels  32.9 us (42%)
  starting transfers between devices  18.7 us (24%)
  blocking collectives  14 us (18%)
  waiting for transfers between devices  10.7 us (14%)
  local copies, waits for them, and re-layouts  1.5 us (2%)
    all_to_all x1, blocking collectives, body(): lax.all_to_all(spread.reshape(RUNS, 1, LANES), both, split_axis=0, concat...  14 us
    all_to_all x1, starting transfers between devices, body(): lax.all_to_all(payload.reshape(RUNS, 1, RUN_ROWS * LANES), both, split_ax...  11.5 us
    pallas_call x1, Pallas kernels, route(): pl.pallas_call(route_kernel, out_shape=(jax.ShapeDtypeStruct(lake_slot.sh...  8.68 us
    all_to_all x1, waiting for transfers between devices, body(): lax.all_to_all(payload.reshape(RUNS, 1, RUN_ROWS * LANES), both, split_ax...  8.46 us
    pallas_call x1, Pallas kernels, statics(): pl.pallas_call(static_kernel, out_shape=(jax.ShapeDtypeStruct(slabs, F32)...  5.13 us
    pallas_call x1, Pallas kernels, place(): pl.pallas_call(place_kernel, out_shape=(jax.ShapeDtypeStruct(slabs, F32),...  4.87 us
    pallas_call x1, Pallas kernels, land_payload(): pl.pallas_call(send_kernel, out_shape=jax.ShapeDtypeStruct((RUNS * RUN_RO...  4.29 us
    pallas_call x1, Pallas kernels, opening(): pl.pallas_call(open_kernel, out_shape=(jax.ShapeDtypeStruct(depth.shape,...  4.09 us
  transfers between devices with their start and end apart: 5, of which 2 were waited for; matrix products, arithmetic and copies ran while one was open for 1% of the time, Pallas kernels for 18%

profile of v3, /device:TPU:1, one launch (start us, length us, event | category | flops | bytes accessed | tf_op | source)
XLA Modules:
  0.0 78.6 jit_solution(1963682923694780761)
XLA Ops:
  0.6 4.3 %land.1 = f32[3328,128]{1,0:T(8,128)} custom-call(s32[4096]{0:T(1024)} %tile_hbm.1, f32[4,4096]{1,0:T(4,128)} %moisture_ref, f32[4,4096]{1,0:T(4,128)} %conduct_ref.1, f32[1,4096]{1,0:T(1,128)} %bitcast.25, f32[100,4096]{1,0:T(8,128)} %weights_hbm.1), custom_call_target="tpu_custom_call" | custom-call | tf_op jit(solution)/shard_map/land/pallas_call | solution.py:178
  4.9 11.5 %all-to-all-start = ((f32[128,1,3328]{2,1,0:T(1,128)}), f32[128,1,3328]{2,1,0:T(1,128)S(1)}, u32[]{:S(2)}, u32[]{:S(2)}) async-start(f32[128,1,3328]{2,1,0:T(1,128)} %bitcast.24), calls=%async_computation | async-start | bytes 3407872 | tf_op jit(solution)/shard_map/all_to_all | solution.py:782
  16.4 4.0 %rim.1 = (f32[16,640]{1,0:T(8,128)}, f32[4,4096]{1,0:T(4,128)}) custom-call(f32[4,4096]{1,0:T(4,128)} %moisture_ref, f32[4,4096]{1,0:T(4,128)} %conduct_ref.1, f32[1,4096]{1,0:T(1,128)} %bitcast.26, f32[640,640]{1,0:T(8,128)} %rate_hbm.1, s32[640,640]{1,0:T(8,128)} %code_hbm.1, s32[640,640]{1,0:T(8,128)} %slot_hbm.2, f32[640,640]{1,0:T(8,128)} %head_hbm.2), custom_call_target="tpu_custom_call" | custom-call | tf_op jit(solution)/shard_map/rim/pallas_call | solution.py:339
  20.4 0.8 fusion
  21.2 1.1 %collective-permute-start.1 = (f32[8,640]{1,0:T(8,128)S(1)}, f32[8,640]{1,0:T(8,128)S(1)}, u32[]{:S(2)}, u32[]{:S(2)}) collective-permute-start(f32[8,640]{1,0:T(8,128)S(1)} %get-tuple-element.60), channel_id=1, source_target_pairs={{0,15},{1,0},{2,1},{3,2},{4,3},{5,4},{6,5},{7,6},{8,7},{9,8},{10,9... | collective-permute-start | bytes 61448 | tf_op jit(solution)/shard_map/ppermute | solution.py:787
  22.2 2.5 %collective-permute-start = (f32[8,640]{1,0:T(8,128)S(1)}, f32[8,640]{1,0:T(8,128)S(1)}, u32[]{:S(2)}, u32[]{:S(2)}) collective-permute-start(f32[8,640]{1,0:T(8,128)S(1)} %get-tuple-element.61), channel_id=1, source_target_pairs={{0,1},{1,2},{2,3},{3,4},{4,5},{5,6},{6,7},{7,8},{8,9},{9,10},{10,1... | collective-permute-start | bytes 61448 | tf_op jit(solution)/shard_map/ppermute | solution.py:786
  24.7 0.1 add_convert_fusion.edge_ref
  24.8 5.1 %static.1 = (f32[5,672,128]{2,1,0:T(8,128)}, s32[5,672,128]{2,1,0:T(8,128)}, s32[8,128]{1,0:T(8,128)S(1)}, f32[8,768]{1,0:T(8,128)S(1)}, f32[8,768]{1,0:T(8,128)S(1)}, /*index=5*/bf16[768,640]{1,0:T(8,128)(2,1)S(1)}) custom-call(f32[640,640]{1,0:T(8,128)} %rate_hbm.1, s32[640,640]{1,0:T(8,128)} %code_hbm.1, s32[640,640]{1,0:T(8,128)} %slot_hbm.2, ...), custom_call_target="tpu_custom_call" | custom-call | tf_op jit(solution)/shard_map/static/pallas_call | solution.py:435
  29.9 2.2 %collective-permute-done.1.right_ref = f32[8,640]{1,0:T(8,128)S(1)} collective-permute-done((f32[8,640]{1,0:T(8,128)S(1)}, f32[8,640]{1,0:T(8,128)S(1)}, u32[]{:S(2)}, u32[]{:S(2)}) %collective-permute-start.1) | collective-permute-done | bytes 20512 | tf_op jit(solution)/shard_map/ppermute | solution.py:787
  32.1 0.0 collective-permute-done.left_ref
  32.1 1.3 %sides.1 = (f32[640,128]{1,0:T(8,128)S(1)}, s32[640,128]{1,0:T(8,128)S(1)}, f32[640,128]{1,0:T(8,128)S(1)}, f32[8,768]{1,0:T(8,128)S(1)}, f32[8,768]{1,0:T(8,128)S(1)}) custom-call(s32[4]{0:T(128)S(1)} %add_convert_fusion.edge_ref, f32[8,640]{1,0:T(8,128)S(1)} %collective-permute-done.left_ref, f32[8,640]{1,0:T(8,128)S(1)} %collective-permute-done.1.right_ref, ...), custom_call_target="tpu_custom_call" | custom-call | tf_op jit(solution)/shard_map/sides/pallas_call | solution.py:500
  33.4 0.0 copy-start
  33.5 0.7 copy-done
  34.2 8.5 %all-to-all-done = f32[128,1,3328]{2,1,0:T(1,128)S(1)} async-done(((f32[128,1,3328]{2,1,0:T(1,128)}), f32[128,1,3328]{2,1,0:T(1,128)S(1)}, u32[]{:S(2)}, u32[]{:S(2)}) %all-to-all-start) | async-done | bytes 1703968 | tf_op jit(solution)/shard_map/all_to_all | solution.py:782
  42.6 0.0 copy-start.1
  42.6 4.9 %place.1 = (f32[6,672,128]{2,1,0:T(8,128)}, f32[8,768]{1,0:T(8,128)S(1)}, f32[8,768]{1,0:T(8,128)S(1)}) custom-call(f32[8,768]{1,0:T(8,128)S(1)} %get-tuple-element.42.top_in, f32[8,768]{1,0:T(8,128)S(1)} %get-tuple-element.43.bottom_in, bf16[768,640]{1,0:T(8,128)(2,1)S(1)} %get-tuple-element.44.picks_ref, f32[3328,128]{1,0:T(8,128)S(1)} %bitcast.17), custom_call_target="tpu_custom_call" | custom-call | tf_op jit(solution)/shard_map/place/pallas_call | solution.py:277
  47.5 0.1 collective-permute-start.2
  47.6 3.6 %collective-permute-start.3 = (f32[8,768]{1,0:T(8,128)S(1)}, f32[8,768]{1,0:T(8,128)S(1)}, u32[]{:S(2)}, u32[]{:S(2)}) collective-permute-start(f32[8,768]{1,0:T(8,128)S(1)} %get-tuple-element.47), channel_id=1, source_target_pairs={{0,112},{16,0},{32,16},{48,32},{64,48},{80,64},{96,80},{112,96},{1... | collective-permute-start | bytes 73736 | tf_op jit(solution)/shard_map/ppermute | solution.py:792
  51.2 0.0 copy-done.1
  51.2 4.1 %open.1 = (f32[6,672,128]{2,1,0:T(8,128)}, f32[6,672,128]{2,1,0:T(8,128)}) custom-call(f32[6,672,128]{2,1,0:T(8,128)} %get-tuple-element.48.depth_hbm, f32[640,640]{1,0:T(8,128)} %head_hbm.2, f32[640,128]{1,0:T(8,128)S(1)} %copy-done.1, f32[5,672,128]{2,1,0:T(8,128)} %get-tuple-element.50.rates_hbm, f32[640,128]{1,0:T(8,128)S(1)} %get-tuple-element.51.rate_hbm), custom_call_target="tpu_custom_call" | custom-call | tf_op jit(solution)/shard_map/open/pallas_call | solution.py:564
  55.3 0.0 collective-permute-done.2.up_ref
  55.3 0.0 collective-permute-done.3.down_ref
  55.3 0.0 copy-done.2
  55.3 0.0 copy-start.3
  55.3 0.0 copy-start.4
  55.3 0.0 copy-start.5
  55.3 8.7 %route.1 = (f32[640,640]{1,0:T(8,128)}, f32[128,128]{1,0:T(8,128)S(1)}) custom-call(s32[4]{0:T(128)S(1)} %add_convert_fusion.edge_ref, s32[8,128]{1,0:T(8,128)S(1)} %get-tuple-element.38.ranges, f32[8,768]{1,0:T(8,128)S(1)} %collective-permute-done.2.up_ref, f32[8,768]{1,0:T(8,128)S(1)} %collective-permute-done.3.down_ref, s32[1,64]{1,0:T(1,128)S(1)} %bitcast.20, ...), custom_call_target="tpu_custom_call" | custom-call | tf_op jit(solution)/shard_map/route/pallas_call | solution.py:724
  64.0 14.0 %all_to_all.10 = f32[128,1,128]{2,1,0:T(1,128)S(1)} all-to-all(f32[128,1,128]{2,1,0:T(1,128)S(1)} %bitcast.19), channel_id=1, replica_groups=mesh['row'=8,'col'=16] {'row','col'}, dimensions={0} | all-to-all | bytes 131072 | tf_op jit(solution)/shard_map/all_to_all | solution.py:797
  78.0 0.0 copy-done.3
  78.0 0.0 copy-done.4
  78.0 0.0 copy-done.5
  78.0 0.6 pool.1
  (1 shorter events, 0.0 us)
Async XLA Ops:
  4.9 37.7 %all-to-all-start = ((f32[128,1,3328]{2,1,0:T(1,128)}), f32[128,1,3328]{2,1,0:T(1,128)S(1)}, u32[]{:S(2)}, u32[]{:S(2)}) async-start(f32[128,1,3328]{2,1,0:T(1,128)} %bitcast.24), calls=%async_computation | async-start | bytes 3407872 | tf_op jit(solution)/shard_map/all_to_all | solution.py:782
  21.2 11.0 %collective-permute-start.1 = (f32[8,640]{1,0:T(8,128)S(1)}, f32[8,640]{1,0:T(8,128)S(1)}, u32[]{:S(2)}, u32[]{:S(2)}) collective-permute-start(f32[8,640]{1,0:T(8,128)S(1)} %get-tuple-element.60), channel_id=1, source_target_pairs={{0,15},{1,0},{2,1},{3,2},{4,3},{5,4},{6,5},{7,6},{8,7},{9,8},{10,9... | collective-permute-start | bytes 61448 | tf_op jit(solution)/shard_map/ppermute | solution.py:787
  22.2 9.9 %collective-permute-start = (f32[8,640]{1,0:T(8,128)S(1)}, f32[8,640]{1,0:T(8,128)S(1)}, u32[]{:S(2)}, u32[]{:S(2)}) collective-permute-start(f32[8,640]{1,0:T(8,128)S(1)} %get-tuple-element.61), channel_id=1, source_target_pairs={{0,1},{1,2},{2,3},{3,4},{4,5},{5,6},{6,7},{7,8},{8,9},{9,10},{10,1... | collective-permute-start | bytes 61448 | tf_op jit(solution)/shard_map/ppermute | solution.py:786
  33.4 0.7 copy-start
  42.6 8.5 %copy-start.1 = (f32[640,128]{1,0:T(8,128)S(1)}, f32[640,128]{1,0:T(8,128)}, u32[]{:S(2)}) copy-start(f32[640,128]{1,0:T(8,128)} %copy-done) | copy-start | bytes 983044
  47.5 7.8 %collective-permute-start.2 = (f32[8,768]{1,0:T(8,128)S(1)}, f32[8,768]{1,0:T(8,128)S(1)}, u32[]{:S(2)}, u32[]{:S(2)}) collective-permute-start(f32[8,768]{1,0:T(8,128)S(1)} %get-tuple-element.46), channel_id=1, source_target_pairs={{0,16},{16,32},{32,48},{48,64},{64,80},{80,96},{96,112},{112,0},{1... | collective-permute-start | bytes 73736 | tf_op jit(solution)/shard_map/ppermute | solution.py:791
  47.6 7.7 %collective-permute-start.3 = (f32[8,768]{1,0:T(8,128)S(1)}, f32[8,768]{1,0:T(8,128)S(1)}, u32[]{:S(2)}, u32[]{:S(2)}) collective-permute-start(f32[8,768]{1,0:T(8,128)S(1)} %get-tuple-element.47), channel_id=1, source_target_pairs={{0,112},{16,0},{32,16},{48,32},{64,48},{80,64},{96,80},{112,96},{1... | collective-permute-start | bytes 73736 | tf_op jit(solution)/shard_map/ppermute | solution.py:792
  51.2 4.1 %copy-start.2 = (s32[64]{0:T(128)S(1)}, s32[64]{0:T(128)}, u32[]{:S(2)}) copy-start(s32[64]{0:T(128)} %param.22) | copy-start | bytes 772
  55.3 22.7 %copy-start.3 = (f32[64]{0:T(128)S(1)}, f32[64]{0:T(128)}, u32[]{:S(2)}) copy-start(f32[64]{0:T(128)} %param.23) | copy-start | bytes 772
  55.3 22.7 %copy-start.4 = (f32[64]{0:T(128)S(1)}, f32[64]{0:T(128)}, u32[]{:S(2)}) copy-start(f32[64]{0:T(128)} %param.24) | copy-start | bytes 772
  55.3 22.7 %copy-start.5 = (f32[64]{0:T(128)S(1)}, f32[64]{0:T(128)}, u32[]{:S(2)}) copy-start(f32[64]{0:T(128)} %param.25) | copy-start | bytes 772

commit v4 on v3

--- a/solution.py
+++ b/solution.py
@@ -249,7 +249,7 @@
         cells_ref[slab + 2, pl.ds(row + 5, 5), :] = pltpu.roll(last, 64, 1)
         return carry
 
-    lax.fori_loop(0, RUNS, settle, 0, unroll=16)
+    lax.fori_loop(0, RUNS, settle, 0, unroll=32)
     chunk = 160
     stores = []
     for m in range(0, 640, chunk):
@@ -702,7 +702,7 @@
             sums_ref[into, :] += (terms[0] + terms[1]) + (terms[2] + terms[3]) + terms[4]
             return inner
 
-        return lax.fori_loop(0, LLOC, lake, carry, unroll=8)
+        return lax.fori_loop(0, LLOC, lake, carry, unroll=LLOC)
 
     lax.fori_loop(0, ranges[2, 0], layer, 0)
     tall = (LLOC, 8 * LLOC)

time: 79 us -> 78.2 us (0.990)
  Pallas kernels: 32.9 us -> 32.1 us
  transfers between devices with their start and end apart: 5 -> 5, of which waited for: 2 -> 2; matrix products, arithmetic and copies ran while one was open for 1% -> 1% of each run, Pallas kernels for 18% -> 19%
where the time goes in v4:
time: 78.2 us; the launch traced here: 77.8 us
  Pallas kernels  32.1 us (41%)
  starting transfers between devices  18.7 us (24%)
  blocking collectives  14 us (18%)
  waiting for transfers between devices  10.7 us (14%)
  local copies, waits for them, and re-layouts  1.5 us (2%)
    all_to_all x1, blocking collectives, body(): lax.all_to_all(spread.reshape(RUNS, 1, LANES), both, split_axis=0, concat...  14 us
    all_to_all x1, starting transfers between devices, body(): lax.all_to_all(payload.reshape(RUNS, 1, RUN_ROWS * LANES), both, split_ax...  11.5 us
    all_to_all x1, waiting for transfers between devices, body(): lax.all_to_all(payload.reshape(RUNS, 1, RUN_ROWS * LANES), both, split_ax...  8.46 us
    pallas_call x1, Pallas kernels, route(): pl.pallas_call(route_kernel, out_shape=(jax.ShapeDtypeStruct(lake_slot.sh...  8.21 us
    pallas_call x1, Pallas kernels, statics(): pl.pallas_call(static_kernel, out_shape=(jax.ShapeDtypeStruct(slabs, F32)...  5.13 us
    pallas_call x1, Pallas kernels, place(): pl.pallas_call(place_kernel, out_shape=(jax.ShapeDtypeStruct(slabs, F32),...  4.61 us
    pallas_call x1, Pallas kernels, land_payload(): pl.pallas_call(send_kernel, out_shape=jax.ShapeDtypeStruct((RUNS * RUN_RO...  4.29 us
    pallas_call x1, Pallas kernels, opening(): pl.pallas_call(open_kernel, out_shape=(jax.ShapeDtypeStruct(depth.shape,...  4.09 us
  transfers between devices with their start and end apart: 5, of which 2 were waited for; matrix products, arithmetic and copies ran while one was open for 1% of the time, Pallas kernels for 19%

profile of v4, /device:TPU:1, one launch (start us, length us, event | category | flops | bytes accessed | tf_op | source)
XLA Modules:
  0.0 77.8 jit_solution(10528144269658296387)
XLA Ops:
  0.6 4.3 %land.1 = f32[3328,128]{1,0:T(8,128)} custom-call(s32[4096]{0:T(1024)} %tile_hbm.1, f32[4,4096]{1,0:T(4,128)} %moisture_ref, f32[4,4096]{1,0:T(4,128)} %conduct_ref.1, f32[1,4096]{1,0:T(1,128)} %bitcast.25, f32[100,4096]{1,0:T(8,128)} %weights_hbm.1), custom_call_target="tpu_custom_call" | custom-call | tf_op jit(solution)/shard_map/land/pallas_call | solution.py:178
  4.9 11.5 %all-to-all-start = ((f32[128,1,3328]{2,1,0:T(1,128)}), f32[128,1,3328]{2,1,0:T(1,128)S(1)}, u32[]{:S(2)}, u32[]{:S(2)}) async-start(f32[128,1,3328]{2,1,0:T(1,128)} %bitcast.24), calls=%async_computation | async-start | bytes 3407872 | tf_op jit(solution)/shard_map/all_to_all | solution.py:782
  16.4 4.0 %rim.1 = (f32[16,640]{1,0:T(8,128)}, f32[4,4096]{1,0:T(4,128)}) custom-call(f32[4,4096]{1,0:T(4,128)} %moisture_ref, f32[4,4096]{1,0:T(4,128)} %conduct_ref.1, f32[1,4096]{1,0:T(1,128)} %bitcast.26, f32[640,640]{1,0:T(8,128)} %rate_hbm.1, s32[640,640]{1,0:T(8,128)} %code_hbm.1, s32[640,640]{1,0:T(8,128)} %slot_hbm.2, f32[640,640]{1,0:T(8,128)} %head_hbm.2), custom_call_target="tpu_custom_call" | custom-call | tf_op jit(solution)/shard_map/rim/pallas_call | solution.py:339
  20.4 0.8 fusion
  21.2 1.1 %collective-permute-start.1 = (f32[8,640]{1,0:T(8,128)S(1)}, f32[8,640]{1,0:T(8,128)S(1)}, u32[]{:S(2)}, u32[]{:S(2)}) collective-permute-start(f32[8,640]{1,0:T(8,128)S(1)} %get-tuple-element.60), channel_id=1, source_target_pairs={{0,15},{1,0},{2,1},{3,2},{4,3},{5,4},{6,5},{7,6},{8,7},{9,8},{10,9... | collective-permute-start | bytes 61448 | tf_op jit(solution)/shard_map/ppermute | solution.py:787
  22.2 2.5 %collective-permute-start = (f32[8,640]{1,0:T(8,128)S(1)}, f32[8,640]{1,0:T(8,128)S(1)}, u32[]{:S(2)}, u32[]{:S(2)}) collective-permute-start(f32[8,640]{1,0:T(8,128)S(1)} %get-tuple-element.61), channel_id=1, source_target_pairs={{0,1},{1,2},{2,3},{3,4},{4,5},{5,6},{6,7},{7,8},{8,9},{9,10},{10,1... | collective-permute-start | bytes 61448 | tf_op jit(solution)/shard_map/ppermute | solution.py:786
  24.7 0.1 add_convert_fusion.edge_ref
  24.8 5.1 %static.1 = (f32[5,672,128]{2,1,0:T(8,128)}, s32[5,672,128]{2,1,0:T(8,128)}, s32[8,128]{1,0:T(8,128)S(1)}, f32[8,768]{1,0:T(8,128)S(1)}, f32[8,768]{1,0:T(8,128)S(1)}, /*index=5*/bf16[768,640]{1,0:T(8,128)(2,1)S(1)}) custom-call(f32[640,640]{1,0:T(8,128)} %rate_hbm.1, s32[640,640]{1,0:T(8,128)} %code_hbm.1, s32[640,640]{1,0:T(8,128)} %slot_hbm.2, ...), custom_call_target="tpu_custom_call" | custom-call | tf_op jit(solution)/shard_map/static/pallas_call | solution.py:435
  29.9 2.2 %collective-permute-done.1.right_ref = f32[8,640]{1,0:T(8,128)S(1)} collective-permute-done((f32[8,640]{1,0:T(8,128)S(1)}, f32[8,640]{1,0:T(8,128)S(1)}, u32[]{:S(2)}, u32[]{:S(2)}) %collective-permute-start.1) | collective-permute-done | bytes 20512 | tf_op jit(solution)/shard_map/ppermute | solution.py:787
  32.1 0.0 collective-permute-done.left_ref
  32.1 1.3 %sides.1 = (f32[640,128]{1,0:T(8,128)S(1)}, s32[640,128]{1,0:T(8,128)S(1)}, f32[640,128]{1,0:T(8,128)S(1)}, f32[8,768]{1,0:T(8,128)S(1)}, f32[8,768]{1,0:T(8,128)S(1)}) custom-call(s32[4]{0:T(128)S(1)} %add_convert_fusion.edge_ref, f32[8,640]{1,0:T(8,128)S(1)} %collective-permute-done.left_ref, f32[8,640]{1,0:T(8,128)S(1)} %collective-permute-done.1.right_ref, ...), custom_call_target="tpu_custom_call" | custom-call | tf_op jit(solution)/shard_map/sides/pallas_call | solution.py:500
  33.4 0.0 copy-start
  33.5 0.7 copy-done
  34.2 8.5 %all-to-all-done = f32[128,1,3328]{2,1,0:T(1,128)S(1)} async-done(((f32[128,1,3328]{2,1,0:T(1,128)}), f32[128,1,3328]{2,1,0:T(1,128)S(1)}, u32[]{:S(2)}, u32[]{:S(2)}) %all-to-all-start) | async-done | bytes 1703968 | tf_op jit(solution)/shard_map/all_to_all | solution.py:782
  42.6 0.0 copy-start.1
  42.6 4.6 %place.1 = (f32[6,672,128]{2,1,0:T(8,128)}, f32[8,768]{1,0:T(8,128)S(1)}, f32[8,768]{1,0:T(8,128)S(1)}) custom-call(f32[8,768]{1,0:T(8,128)S(1)} %get-tuple-element.42.top_in, f32[8,768]{1,0:T(8,128)S(1)} %get-tuple-element.43.bottom_in, bf16[768,640]{1,0:T(8,128)(2,1)S(1)} %get-tuple-element.44.picks_ref, f32[3328,128]{1,0:T(8,128)S(1)} %bitcast.17), custom_call_target="tpu_custom_call" | custom-call | tf_op jit(solution)/shard_map/place/pallas_call | solution.py:277
  47.3 0.1 collective-permute-start.2
  47.3 3.6 %collective-permute-start.3 = (f32[8,768]{1,0:T(8,128)S(1)}, f32[8,768]{1,0:T(8,128)S(1)}, u32[]{:S(2)}, u32[]{:S(2)}) collective-permute-start(f32[8,768]{1,0:T(8,128)S(1)} %get-tuple-element.47), channel_id=1, source_target_pairs={{0,112},{16,0},{32,16},{48,32},{64,48},{80,64},{96,80},{112,96},{1... | collective-permute-start | bytes 73736 | tf_op jit(solution)/shard_map/ppermute | solution.py:792
  50.9 0.0 copy-done.1
  50.9 4.1 %open.1 = (f32[6,672,128]{2,1,0:T(8,128)}, f32[6,672,128]{2,1,0:T(8,128)}) custom-call(f32[6,672,128]{2,1,0:T(8,128)} %get-tuple-element.48.depth_hbm, f32[640,640]{1,0:T(8,128)} %head_hbm.2, f32[640,128]{1,0:T(8,128)S(1)} %copy-done.1, f32[5,672,128]{2,1,0:T(8,128)} %get-tuple-element.50.rates_hbm, f32[640,128]{1,0:T(8,128)S(1)} %get-tuple-element.51.rate_hbm), custom_call_target="tpu_custom_call" | custom-call | tf_op jit(solution)/shard_map/open/pallas_call | solution.py:564
  55.0 0.0 collective-permute-done.2.up_ref
  55.0 0.0 collective-permute-done.3.down_ref
  55.0 0.0 copy-done.2
  55.0 0.0 copy-start.3
  55.0 0.0 copy-start.4
  55.1 0.0 copy-start.5
  55.1 8.2 %route.1 = (f32[640,640]{1,0:T(8,128)}, f32[128,128]{1,0:T(8,128)S(1)}) custom-call(s32[4]{0:T(128)S(1)} %add_convert_fusion.edge_ref, s32[8,128]{1,0:T(8,128)S(1)} %get-tuple-element.38.ranges, f32[8,768]{1,0:T(8,128)S(1)} %collective-permute-done.2.up_ref, f32[8,768]{1,0:T(8,128)S(1)} %collective-permute-done.3.down_ref, s32[1,64]{1,0:T(1,128)S(1)} %bitcast.20, ...), custom_call_target="tpu_custom_call" | custom-call | tf_op jit(solution)/shard_map/route/pallas_call | solution.py:724
  63.3 14.0 %all_to_all.10 = f32[128,1,128]{2,1,0:T(1,128)S(1)} all-to-all(f32[128,1,128]{2,1,0:T(1,128)S(1)} %bitcast.19), channel_id=1, replica_groups=mesh['row'=8,'col'=16] {'row','col'}, dimensions={0} | all-to-all | bytes 131072 | tf_op jit(solution)/shard_map/all_to_all | solution.py:797
  77.3 0.0 copy-done.3
  77.3 0.0 copy-done.4
  77.3 0.0 copy-done.5
  77.3 0.6 pool.1
  (1 shorter events, 0.0 us)
Async XLA Ops:
  4.9 37.7 %all-to-all-start = ((f32[128,1,3328]{2,1,0:T(1,128)}), f32[128,1,3328]{2,1,0:T(1,128)S(1)}, u32[]{:S(2)}, u32[]{:S(2)}) async-start(f32[128,1,3328]{2,1,0:T(1,128)} %bitcast.24), calls=%async_computation | async-start | bytes 3407872 | tf_op jit(solution)/shard_map/all_to_all | solution.py:782
  21.2 11.0 %collective-permute-start.1 = (f32[8,640]{1,0:T(8,128)S(1)}, f32[8,640]{1,0:T(8,128)S(1)}, u32[]{:S(2)}, u32[]{:S(2)}) collective-permute-start(f32[8,640]{1,0:T(8,128)S(1)} %get-tuple-element.60), channel_id=1, source_target_pairs={{0,15},{1,0},{2,1},{3,2},{4,3},{5,4},{6,5},{7,6},{8,7},{9,8},{10,9... | collective-permute-start | bytes 61448 | tf_op jit(solution)/shard_map/ppermute | solution.py:787
  22.2 9.9 %collective-permute-start = (f32[8,640]{1,0:T(8,128)S(1)}, f32[8,640]{1,0:T(8,128)S(1)}, u32[]{:S(2)}, u32[]{:S(2)}) collective-permute-start(f32[8,640]{1,0:T(8,128)S(1)} %get-tuple-element.61), channel_id=1, source_target_pairs={{0,1},{1,2},{2,3},{3,4},{4,5},{5,6},{6,7},{7,8},{8,9},{9,10},{10,1... | collective-permute-start | bytes 61448 | tf_op jit(solution)/shard_map/ppermute | solution.py:786
  33.4 0.7 copy-start
  42.6 8.3 %copy-start.1 = (f32[640,128]{1,0:T(8,128)S(1)}, f32[640,128]{1,0:T(8,128)}, u32[]{:S(2)}) copy-start(f32[640,128]{1,0:T(8,128)} %copy-done) | copy-start | bytes 983044
  47.3 7.8 %collective-permute-start.2 = (f32[8,768]{1,0:T(8,128)S(1)}, f32[8,768]{1,0:T(8,128)S(1)}, u32[]{:S(2)}, u32[]{:S(2)}) collective-permute-start(f32[8,768]{1,0:T(8,128)S(1)} %get-tuple-element.46), channel_id=1, source_target_pairs={{0,16},{16,32},{32,48},{48,64},{64,80},{80,96},{96,112},{112,0},{1... | collective-permute-start | bytes 73736 | tf_op jit(solution)/shard_map/ppermute | solution.py:791
  47.3 7.7 %collective-permute-start.3 = (f32[8,768]{1,0:T(8,128)S(1)}, f32[8,768]{1,0:T(8,128)S(1)}, u32[]{:S(2)}, u32[]{:S(2)}) collective-permute-start(f32[8,768]{1,0:T(8,128)S(1)} %get-tuple-element.47), channel_id=1, source_target_pairs={{0,112},{16,0},{32,16},{48,32},{64,48},{80,64},{96,80},{112,96},{1... | collective-permute-start | bytes 73736 | tf_op jit(solution)/shard_map/ppermute | solution.py:792
  50.9 4.1 %copy-start.2 = (s32[64]{0:T(128)S(1)}, s32[64]{0:T(128)}, u32[]{:S(2)}) copy-start(s32[64]{0:T(128)} %param.22) | copy-start | bytes 772
  55.0 22.2 %copy-start.3 = (f32[64]{0:T(128)S(1)}, f32[64]{0:T(128)}, u32[]{:S(2)}) copy-start(f32[64]{0:T(128)} %param.23) | copy-start | bytes 772
  55.0 22.2 %copy-start.4 = (f32[64]{0:T(128)S(1)}, f32[64]{0:T(128)}, u32[]{:S(2)}) copy-start(f32[64]{0:T(128)} %param.24) | copy-start | bytes 772
  55.1 22.2 %copy-start.5 = (f32[64]{0:T(128)S(1)}, f32[64]{0:T(128)}, u32[]{:S(2)}) copy-start(f32[64]{0:T(128)} %param.25) | copy-start | bytes 772

commit v5 on v4

--- a/solution.py
+++ b/solution.py
@@ -53,8 +53,17 @@
 
 
 def leave(depth, rate):
-    conveyance = rate * jnp.exp(jnp.log(depth) * (2.0 / 3.0))
+    conveyance = rate * jnp.exp2(jnp.log2(depth) * (2.0 / 3.0))
     return depth * conveyance / (1.0 + conveyance)
+
+
+def swap(axis, first):
+    count = lax.axis_size(axis)
+    pairs = []
+    for i in range(first, first + count, 2):
+        a, b = i % count, (i + 1) % count
+        pairs += [(a, b), (b, a)]
+    return pairs
 
 
 def ring(axis, step):
@@ -551,7 +560,7 @@
     for q in range(4):
         for copy in fetches[q]:
             copy.wait()
-        lax.fori_loop(2 + 20 * q, 22 + 20 * q, step, 0, unroll=5)
+        lax.fori_loop(2 + 20 * q, 22 + 20 * q, step, 0, unroll=10)
         for copy in stores[q]:
             copy.start()
     for group in stores:
@@ -788,8 +797,11 @@
     rates, codes, ranges, top, bottom, picks = statics(rate, flow_code, lake_slot, head)
     side_rate, side_code, side_head, top, bottom = sides(edges, left, right, top, bottom)
     depth, top, bottom = place(top, bottom, picks, arrived)
-    up = lax.ppermute(bottom, "row", ring("row", 1))
-    down = lax.ppermute(top, "row", ring("row", -1))
+    even = at_row % 2 == 0
+    near = lax.ppermute(jnp.where(even, bottom, top), "row", swap("row", 0))
+    far = lax.ppermute(jnp.where(even, top, bottom), "row", swap("row", 1))
+    up = jnp.where(even, far, near)
+    down = jnp.where(even, near, far)
     leaving, stay = opening(depth, head, side_head, rates, side_rate)
     surface, spread = route(
         edges, ranges, up, down, leaving, stay, rates, codes, side_rate, side_code, lake_slot, lake_table

time: 78.2 us -> 77.6 us (level)
  starting transfers between devices: 18.7 us -> 15.8 us
  blocking collectives: 14 us -> 16.1 us
    ppermute x2, starting transfers between devices: 3.64 us -> 0.75 us  [the longest x1 0.67 us: body(): far = lax.ppermute(jnp.where(even, top, bottom), 'row', swap('row', 1))]
    all_to_all x1, blocking collectives: 14 us -> 16.1 us  [body(): lax.all_to_all(spread.reshape(RUNS, 1, LANES), both, split_axis=0, concat...]
  transfers between devices with their start and end apart: 5 -> 5, of which waited for: 2 -> 3; matrix products, arithmetic and copies ran while one was open for 1% -> 1% of each run, Pallas kernels for 19% -> 19%
where the time goes in v5:
time: 77.6 us; the launch traced here: 77.2 us
  Pallas kernels  32 us (41%)
  blocking collectives  16.1 us (21%)
  starting transfers between devices  15.8 us (20%)
  waiting for transfers between devices  10.9 us (14%)
  local copies, waits for them, and re-layouts  1.5 us (2%)
  between operations  0.78 us (1%)
    all_to_all x1, blocking collectives, body(): lax.all_to_all(spread.reshape(RUNS, 1, LANES), both, split_axis=0, concat...  16.1 us
    all_to_all x1, starting transfers between devices, body(): lax.all_to_all(payload.reshape(RUNS, 1, RUN_ROWS * LANES), both, split_ax...  11.5 us
    all_to_all x1, waiting for transfers between devices, body(): lax.all_to_all(payload.reshape(RUNS, 1, RUN_ROWS * LANES), both, split_ax...  8.46 us
    pallas_call x1, Pallas kernels, route(): pl.pallas_call(route_kernel, out_shape=(jax.ShapeDtypeStruct(lake_slot.sh...  8.07 us
    pallas_call x1, Pallas kernels, statics(): pl.pallas_call(static_kernel, out_shape=(jax.ShapeDtypeStruct(slabs, F32)...  5.14 us
    pallas_call x1, Pallas kernels, place(): pl.pallas_call(place_kernel, out_shape=(jax.ShapeDtypeStruct(slabs, F32),...  4.63 us
    pallas_call x1, Pallas kernels, land_payload(): pl.pallas_call(send_kernel, out_shape=jax.ShapeDtypeStruct((RUNS * RUN_RO...  4.3 us
    pallas_call x1, Pallas kernels, opening(): pl.pallas_call(open_kernel, out_shape=(jax.ShapeDtypeStruct(depth.shape,...  4.09 us
  transfers between devices with their start and end apart: 5, of which 3 were waited for; matrix products, arithmetic and copies ran while one was open for 1% of the time, Pallas kernels for 19%

profile of v5, /device:TPU:1, one launch (start us, length us, event | category | flops | bytes accessed | tf_op | source)
XLA Modules:
  0.0 77.2 jit_solution(11427200232306713280)
XLA Ops:
  0.6 4.3 %land.1 = f32[3328,128]{1,0:T(8,128)} custom-call(s32[4096]{0:T(1024)} %tile_hbm.1, f32[4,4096]{1,0:T(4,128)} %moisture_ref, f32[4,4096]{1,0:T(4,128)} %conduct_ref.1, f32[1,4096]{1,0:T(1,128)} %bitcast.25, f32[100,4096]{1,0:T(8,128)} %weights_hbm.1), custom_call_target="tpu_custom_call" | custom-call | tf_op jit(solution)/shard_map/land/pallas_call | solution.py:187
  4.9 11.5 %all-to-all-start = ((f32[128,1,3328]{2,1,0:T(1,128)}), f32[128,1,3328]{2,1,0:T(1,128)S(1)}, u32[]{:S(2)}, u32[]{:S(2)}) async-start(f32[128,1,3328]{2,1,0:T(1,128)} %bitcast.24), calls=%async_computation | async-start | bytes 3407872 | tf_op jit(solution)/shard_map/all_to_all | solution.py:791
  16.4 4.0 %rim.1 = (f32[16,640]{1,0:T(8,128)}, f32[4,4096]{1,0:T(4,128)}) custom-call(f32[4,4096]{1,0:T(4,128)} %moisture_ref, f32[4,4096]{1,0:T(4,128)} %conduct_ref.1, f32[1,4096]{1,0:T(1,128)} %bitcast.26, f32[640,640]{1,0:T(8,128)} %rate_hbm.1, s32[640,640]{1,0:T(8,128)} %code_hbm.1, s32[640,640]{1,0:T(8,128)} %slot_hbm.2, f32[640,640]{1,0:T(8,128)} %head_hbm.2), custom_call_target="tpu_custom_call" | custom-call | tf_op jit(solution)/shard_map/rim/pallas_call | solution.py:348
  20.4 0.8 fusion
  21.2 1.1 %collective-permute-start.1 = (f32[8,640]{1,0:T(8,128)S(1)}, f32[8,640]{1,0:T(8,128)S(1)}, u32[]{:S(2)}, u32[]{:S(2)}) collective-permute-start(f32[8,640]{1,0:T(8,128)S(1)} %get-tuple-element.64), channel_id=1, source_target_pairs={{0,15},{1,0},{2,1},{3,2},{4,3},{5,4},{6,5},{7,6},{8,7},{9,8},{10,9... | collective-permute-start | bytes 61448 | tf_op jit(solution)/shard_map/ppermute | solution.py:796
  22.2 2.5 %collective-permute-start = (f32[8,640]{1,0:T(8,128)S(1)}, f32[8,640]{1,0:T(8,128)S(1)}, u32[]{:S(2)}, u32[]{:S(2)}) collective-permute-start(f32[8,640]{1,0:T(8,128)S(1)} %get-tuple-element.65), channel_id=1, source_target_pairs={{0,1},{1,2},{2,3},{3,4},{4,5},{5,6},{6,7},{7,8},{8,9},{9,10},{10,1... | collective-permute-start | bytes 61448 | tf_op jit(solution)/shard_map/ppermute | solution.py:795
  24.7 0.1 add_convert_fusion.edge_ref
  24.8 5.1 %static.1 = (f32[5,672,128]{2,1,0:T(8,128)}, s32[5,672,128]{2,1,0:T(8,128)}, s32[8,128]{1,0:T(8,128)S(1)}, f32[8,768]{1,0:T(8,128)S(1)}, f32[8,768]{1,0:T(8,128)S(1)}, /*index=5*/bf16[768,640]{1,0:T(8,128)(2,1)S(1)}) custom-call(f32[640,640]{1,0:T(8,128)} %rate_hbm.1, s32[640,640]{1,0:T(8,128)} %code_hbm.1, s32[640,640]{1,0:T(8,128)} %slot_hbm.2, ...), custom_call_target="tpu_custom_call" | custom-call | tf_op jit(solution)/shard_map/static/pallas_call | solution.py:444
  29.9 2.2 %collective-permute-done.1.right_ref = f32[8,640]{1,0:T(8,128)S(1)} collective-permute-done((f32[8,640]{1,0:T(8,128)S(1)}, f32[8,640]{1,0:T(8,128)S(1)}, u32[]{:S(2)}, u32[]{:S(2)}) %collective-permute-start.1) | collective-permute-done | bytes 20512 | tf_op jit(solution)/shard_map/ppermute | solution.py:796
  32.1 0.0 collective-permute-done.left_ref
  32.1 1.3 %sides.1 = (f32[640,128]{1,0:T(8,128)S(1)}, s32[640,128]{1,0:T(8,128)S(1)}, f32[640,128]{1,0:T(8,128)S(1)}, f32[8,768]{1,0:T(8,128)S(1)}, f32[8,768]{1,0:T(8,128)S(1)}) custom-call(s32[4]{0:T(128)S(1)} %add_convert_fusion.edge_ref, f32[8,640]{1,0:T(8,128)S(1)} %collective-permute-done.left_ref, f32[8,640]{1,0:T(8,128)S(1)} %collective-permute-done.1.right_ref, ...), custom_call_target="tpu_custom_call" | custom-call | tf_op jit(solution)/shard_map/sides/pallas_call | solution.py:509
  33.5 0.0 copy-start
  33.5 0.7 copy-done
  34.2 8.5 %all-to-all-done = f32[128,1,3328]{2,1,0:T(1,128)S(1)} async-done(((f32[128,1,3328]{2,1,0:T(1,128)}), f32[128,1,3328]{2,1,0:T(1,128)S(1)}, u32[]{:S(2)}, u32[]{:S(2)}) %all-to-all-start) | async-done | bytes 1703968 | tf_op jit(solution)/shard_map/all_to_all | solution.py:791
  42.6 0.0 copy-start.1
  42.6 4.6 %place.1 = (f32[6,672,128]{2,1,0:T(8,128)}, f32[8,768]{1,0:T(8,128)S(1)}, f32[8,768]{1,0:T(8,128)S(1)}) custom-call(f32[8,768]{1,0:T(8,128)S(1)} %get-tuple-element.42.top_in, f32[8,768]{1,0:T(8,128)S(1)} %get-tuple-element.43.bottom_in, bf16[768,640]{1,0:T(8,128)(2,1)S(1)} %get-tuple-element.44.picks_ref, f32[3328,128]{1,0:T(8,128)S(1)} %bitcast.17), custom_call_target="tpu_custom_call" | custom-call | tf_op jit(solution)/shard_map/place/pallas_call | solution.py:286
  47.3 0.1 collective-permute-start.3
  47.4 0.7 collective-permute-start.2
  48.1 0.0 copy-done.1
  48.1 4.1 %open.1 = (f32[6,672,128]{2,1,0:T(8,128)}, f32[6,672,128]{2,1,0:T(8,128)}) custom-call(f32[6,672,128]{2,1,0:T(8,128)} %get-tuple-element.48.depth_hbm, f32[640,640]{1,0:T(8,128)} %head_hbm.2, f32[640,128]{1,0:T(8,128)S(1)} %copy-done.1, f32[5,672,128]{2,1,0:T(8,128)} %get-tuple-element.50.rates_hbm, f32[640,128]{1,0:T(8,128)S(1)} %get-tuple-element.51.rate_hbm), custom_call_target="tpu_custom_call" | custom-call | tf_op jit(solution)/shard_map/open/pallas_call | solution.py:573
  52.2 0.0 collective-permute-done.3
  52.2 0.3 collective-permute-done.2
  52.4 0.0 copy-done.2
  52.5 0.0 copy-start.3
  52.5 0.0 copy-start.4
  52.5 0.0 copy-start.5
  52.5 8.1 %route.1 = (f32[640,640]{1,0:T(8,128)}, f32[128,128]{1,0:T(8,128)S(1)}) custom-call(s32[4]{0:T(128)S(1)} %add_convert_fusion.edge_ref, s32[8,128]{1,0:T(8,128)S(1)} %get-tuple-element.38.ranges, f32[8,768]{1,0:T(8,128)S(1)} %get-tuple-element.61.up_ref, f32[8,768]{1,0:T(8,128)S(1)} %get-tuple-element.60.down_ref, s32[1,64]{1,0:T(1,128)S(1)} %bitcast.20, ...), custom_call_target="tpu_custom_call" | custom-call | tf_op jit(solution)/shard_map/route/pallas_call | solution.py:733
  60.6 16.1 %all_to_all.10 = f32[128,1,128]{2,1,0:T(1,128)S(1)} all-to-all(f32[128,1,128]{2,1,0:T(1,128)S(1)} %bitcast.19), channel_id=1, replica_groups=mesh['row'=8,'col'=16] {'row','col'}, dimensions={0} | all-to-all | bytes 131072 | tf_op jit(solution)/shard_map/all_to_all | solution.py:809
  76.7 0.0 copy-done.3
  76.7 0.0 copy-done.4
  76.7 0.0 copy-done.5
  76.7 0.6 pool.1
  (3 shorter events, 0.0 us)
Async XLA Ops:
  4.9 37.7 %all-to-all-start = ((f32[128,1,3328]{2,1,0:T(1,128)}), f32[128,1,3328]{2,1,0:T(1,128)S(1)}, u32[]{:S(2)}, u32[]{:S(2)}) async-start(f32[128,1,3328]{2,1,0:T(1,128)} %bitcast.24), calls=%async_computation | async-start | bytes 3407872 | tf_op jit(solution)/shard_map/all_to_all | solution.py:791
  21.2 11.0 %collective-permute-start.1 = (f32[8,640]{1,0:T(8,128)S(1)}, f32[8,640]{1,0:T(8,128)S(1)}, u32[]{:S(2)}, u32[]{:S(2)}) collective-permute-start(f32[8,640]{1,0:T(8,128)S(1)} %get-tuple-element.64), channel_id=1, source_target_pairs={{0,15},{1,0},{2,1},{3,2},{4,3},{5,4},{6,5},{7,6},{8,7},{9,8},{10,9... | collective-permute-start | bytes 61448 | tf_op jit(solution)/shard_map/ppermute | solution.py:796
  22.2 9.9 %collective-permute-start = (f32[8,640]{1,0:T(8,128)S(1)}, f32[8,640]{1,0:T(8,128)S(1)}, u32[]{:S(2)}, u32[]{:S(2)}) collective-permute-start(f32[8,640]{1,0:T(8,128)S(1)} %get-tuple-element.65), channel_id=1, source_target_pairs={{0,1},{1,2},{2,3},{3,4},{4,5},{5,6},{6,7},{7,8},{8,9},{9,10},{10,1... | collective-permute-start | bytes 61448 | tf_op jit(solution)/shard_map/ppermute | solution.py:795
  33.5 0.7 copy-start
  42.6 5.4 %copy-start.1 = (f32[640,128]{1,0:T(8,128)S(1)}, f32[640,128]{1,0:T(8,128)}, u32[]{:S(2)}) copy-start(f32[640,128]{1,0:T(8,128)} %copy-done) | copy-start | bytes 983044
  47.3 4.9 %collective-permute-start.3 = (f32[8,768]{1,0:T(8,128)S(1)}, f32[8,768]{1,0:T(8,128)S(1)}, u32[]{:S(2)}, u32[]{:S(2)}) collective-permute-start(f32[8,768]{1,0:T(8,128)S(1)} %get-tuple-element.62), channel_id=1, source_target_pairs={{0,16},{16,0},{32,48},{48,32},{64,80},{80,64},{96,112},{112,96},{1... | collective-permute-start | bytes 73736 | tf_op jit(solution)/shard_map/ppermute | solution.py:801
  47.4 5.0 %collective-permute-start.2 = (f32[8,768]{1,0:T(8,128)S(1)}, f32[8,768]{1,0:T(8,128)S(1)}, u32[]{:S(2)}, u32[]{:S(2)}) collective-permute-start(f32[8,768]{1,0:T(8,128)S(1)} %get-tuple-element.63), channel_id=1, source_target_pairs={{16,32},{32,16},{48,64},{64,48},{80,96},{96,80},{112,0},{0,112},{1... | collective-permute-start | bytes 73736 | tf_op jit(solution)/shard_map/ppermute | solution.py:802
  48.1 4.4 %copy-start.2 = (s32[64]{0:T(128)S(1)}, s32[64]{0:T(128)}, u32[]{:S(2)}) copy-start(s32[64]{0:T(128)} %param.22) | copy-start | bytes 772
  52.5 24.2 %copy-start.3 = (f32[64]{0:T(128)S(1)}, f32[64]{0:T(128)}, u32[]{:S(2)}) copy-start(f32[64]{0:T(128)} %param.23) | copy-start | bytes 772
  52.5 24.2 %copy-start.4 = (f32[64]{0:T(128)S(1)}, f32[64]{0:T(128)}, u32[]{:S(2)}) copy-start(f32[64]{0:T(128)} %param.24) | copy-start | bytes 772
  52.5 24.2 %copy-start.5 = (f32[64]{0:T(128)S(1)}, f32[64]{0:T(128)}, u32[]{:S(2)}) copy-start(f32[64]{0:T(128)} %param.25) | copy-start | bytes 772
